TPU v7x, 32 devices: a whole 2x2x4 slice. The times are simulated.
32 devices in a mesh: tm: 4 (over y, x), lat: 8 (over z, core).
Axes of the slice: x: 2, y: 2, z: 4, core: 2. Of those that a mesh axis runs over, the one named last changes fastest.
Arguments:
- frames: bfloat16 [64, 2048, 4096], P('tm', 'lat'), may hold values from -6 to 6
- owner_map: int32 [512], replicated, may hold values from 0 to 511, as said below
Outputs:
- spectrum: float32 [2, 512, 8, 1024], P(None, 'lat', None, 'tm')
Inputs may be any that keep to these rules, and one draw needn't show every extreme that they name: owner_map is a permutation of 0 to 511; entries 2 i and 2 i + 1 hold an order m and the order 512 - 1 - m.
All inputs are finite; a program needn't handle non-finite values.
Results may differ from a plain program's by a relative error of at most 0.0064.
Values may be sent and summed in bfloat16 or wider, within the bound.
No kernel may reach another device: no remote copies, remote signals or barrier semaphores. Data moves between devices by JAX's collectives and lax.ppermute only.
A program may use at most 128 MiB of HBM per device.

v0:
```python
from functools import partial
import math

import jax
import jax.numpy as jnp
from jax import lax
from jax.sharding import PartitionSpec as P

L = 1024
F = 8


def longitude_table(owner_map, nlon_count):
    points = jnp.arange(nlon_count, dtype=jnp.int32)
    phases = points[:, None] * owner_map[None, :] % nlon_count
    angles = phases.astype(jnp.float32) * (2.0 * math.pi / nlon_count)
    factor = math.sqrt(2.0 / nlon_count)
    cos_part = (jnp.cos(angles) * factor).astype(jnp.bfloat16)
    sin_part = (-jnp.sin(angles) * factor).astype(jnp.bfloat16)
    return jnp.concatenate([cos_part, sin_part], axis=1)


def order_setup(orders, nlat_count, order_count):
    order_val = orders.astype(jnp.float32)[:, None]
    steps_k = jnp.arange(1, order_count + 1, dtype=jnp.float32)[None, :]
    growth = jnp.sum(
        jnp.where(steps_k <= order_val, jnp.log1p(0.5 / steps_k), 0.0), axis=1, keepdims=True
    )
    colatitude = (jnp.arange(nlat_count, dtype=jnp.float32) + 0.5) * (math.pi / nlat_count)
    cosine = jnp.cos(colatitude)
    sine_row = jnp.sin(colatitude)
    lognorm = 0.5 * math.log(0.5) + 0.5 * growth + order_val * jnp.log(sine_row)[None, :]
    weight = sine_row * (math.pi / nlat_count) * math.sqrt(nlat_count)
    safe_log = jnp.maximum(lognorm, -60.0)
    start_value = jnp.where(lognorm >= -60.0, jnp.exp(safe_log), 0.0)
    diagonal_start = start_value * weight[None, :]
    return (order_val, cosine, diagonal_start)


def legendre_step(order_val, cosine, diagonal_start, state, degree):
    previous_p, older_p = state
    level = degree.astype(jnp.float32)
    level_sq = level * level
    order_sq = order_val * order_val
    lower = level - 1.0
    rising_coef = jnp.sqrt(
        jnp.maximum(4.0 * level_sq - 1.0, 0.0) / jnp.maximum(level_sq - order_sq, 1.0)
    )
    falling_coef = jnp.sqrt(
        jnp.maximum(lower * lower - order_sq, 0.0) / jnp.maximum(4.0 * lower * lower - 1.0, 1.0)
    )
    rising = rising_coef * (cosine[None, :] * previous_p - falling_coef * older_p)
    current = jnp.where(
        level == order_val, diagonal_start, jnp.where(level > order_val, rising, 0.0)
    )
    return ((current, previous_p), current.astype(jnp.bfloat16))


def time_table(total_frames, band_count, first_frame, frame_count):
    frames_at = first_frame + jnp.arange(frame_count, dtype=jnp.int32)
    frequency = total_frames // 8 + jnp.arange(band_count, dtype=jnp.int32)
    phases = frequency[:, None] * frames_at[None, :] % total_frames
    angles = phases.astype(jnp.float32) * (2.0 * math.pi / total_frames)
    factor = 1.0 / math.sqrt(total_frames)
    cos_part = jnp.cos(angles) * factor
    sin_part = jnp.sin(angles) * factor
    top_row = jnp.stack([cos_part, sin_part], axis=1)
    low_row = jnp.stack([-sin_part, cos_part], axis=1)
    return jnp.stack([top_row, low_row], axis=0).astype(jnp.bfloat16)


def shards(frames, owner_map):
    frame_count, lat_rows, nlon_count = frames.shape
    order_count = owner_map.shape[0]
    lat_count = lax.axis_size("lat")
    time_count = lax.axis_size("tm")
    per_lat = order_count // lat_count
    owned_count = per_lat // time_count
    lon_weights = longitude_table(owner_map, nlon_count)
    coefficients = jnp.einsum(
        "nc,trn->ctr", lon_weights, frames, preferred_element_type=jnp.float32
    )
    coefficients = coefficients.astype(jnp.bfloat16).reshape(2, order_count, frame_count, lat_rows)
    total_frames = frame_count * time_count
    weights = time_table(total_frames, F, lax.axis_index("tm") * frame_count, frame_count)
    partial_terms = jnp.einsum(
        "efct,cktr->ekfr", weights, coefficients, preferred_element_type=jnp.float32
    )
    partial_terms = partial_terms.reshape(2, lat_count, per_lat, F, lat_rows)
    summed = lax.psum_scatter(partial_terms, "tm", scatter_dimension=2, tiled=True).astype(
        jnp.bfloat16
    )
    band = lax.all_to_all(summed, "lat", split_axis=1, concat_axis=4, tiled=True)
    nlat_count = band.shape[4]
    band = band.reshape(2, owned_count, F, nlat_count)
    first_slot = lax.axis_index("lat") * per_lat + lax.axis_index("tm") * owned_count
    orders = lax.dynamic_slice_in_dim(owner_map, first_slot, owned_count)
    order_val, cosine, diagonal_start = order_setup(orders, nlat_count, order_count)
    span_len = min(128, L)
    stepper = partial(legendre_step, order_val, cosine, diagonal_start)

    def one_span(state, offset):
        state, polynomials = lax.scan(
            stepper, state, offset + jnp.arange(span_len, dtype=jnp.int32), unroll=16
        )
        product = jnp.einsum(
            "ekfr,lkr->ekfl", band, polynomials, preferred_element_type=jnp.float32
        )
        return (state, product)

    zero_rows = jnp.zeros((owned_count, nlat_count), jnp.float32)
    _, pieces = lax.scan(
        one_span, (zero_rows, zero_rows), jnp.arange(L // span_len, dtype=jnp.int32) * span_len
    )
    spectra = jnp.moveaxis(pieces, 0, 3).reshape(2, owned_count, F, L)
    return lax.all_to_all(spectra, "tm", split_axis=3, concat_axis=1, tiled=True)


def solution(mesh):
    return jax.shard_map(
        shards,
        mesh=mesh,
        in_specs=(P("tm", "lat", None), P()),
        out_specs=P(None, "lat", None, "tm"),
        check_vma=False,
    )
```

profile of v0, /device:TPU:0, one launch (start us, length us, event | category | flops | bytes accessed | tf_op | source)
XLA Modules:
  0.0 1564.1 jit_solution(12282173016245473389)
XLA Ops:
  6.5 38.4 %multiply_convert_fusion.1 = (bf16[4096,512]{0,1:T(8,128)(2,1)}, bf16[4096,512]{0,1:T(8,128)(2,1)}) fusion(s32[512]{0:T(512)} %param.7), kind=kLoop, calls=%fused_computation.136 | loop fusion | flops 39845888 | bytes 8390656 | tf_op jit(solution)/shard_map/convert_element_type | solution.py:18
  45.0 42.7 %fusion.39 = bf16[1024,16,256]{2,0,1:T(8,128)(2,1)} fusion(bf16[16,256,4096]{2,1,0:T(8,128)(2,1)} %param.6, bf16[4096,512]{0,1:T(8,128)(2,1)} %get-tuple-element.821, bf16[4096,512]{0,1:T(8,128)(2,1)} %get-tuple-element.820), kind=kOutput, calls=%fused_computation.140 | convolution fusion | flops 34380709888 | bytes 50331648 | tf_op jit(solution)/shard_map/nc,trn->ctr/dot_general | solution.py:80
  87.8 8.2 fusion.34
  96.0 1.4 copy.55
  97.4 8.0 copy.59
  105.4 89.2 %reduce-scatter.5.cloned.1.call-done = f32[16,32768]{1,0:T(8,128)} async-done(((f32[64,32768]{1,0:T(8,128)}), f32[16,32768]{1,0:T(8,128)}) %reduce-scatter.5.cloned.1.call-update) | async-done | bytes 2097168
  194.6 2.2 copy.60
  197.9 4.6 all-to-all-start
  203.5 25.5 %all-to-all-done = bf16[2,8,16,8,256]{4,3,0,2,1:T(8,128)(2,1)S(1)} async-done(((bf16[2,8,16,8,256]{4,3,0,2,1:T(8,128)(2,1)}), bf16[2,8,16,8,256]{4,3,0,2,1:T(8,128)(2,1)S(1)}, u32[]{:S(2)}, u32[]{:S(2)}) %all-to-all-start) | async-done | bytes 1048608 | tf_op jit(solution)/shard_map/all_to_all | solution.py:93
  229.9 1.3 reshape.1154
  231.3 1279.7 %while.53 = (s32[]{:T(128)}, f32[16,2048]{1,0:T(8,128)S(1)}, f32[16,2048]{1,0:T(8,128)S(1)}, f32[8,2,16,8,128]{4,3,1,2,0:T(8,128)}, s32[8]{0:T(128)S(1)}, /*inde...) while((s32[]{:T(128)}, f32[16,2048]{1,0:T(8,128)S(1)}, ...), condition=%wide.region_5.6_spmd.clone.clone, body=%wide.region_2.5_spmd.clone.clone.sunk | while | flops 161454640 | bytes 24424056 | solution.py:112
  233.0 149.9 %while.54 = (s32[]{:T(128)}, f32[16,2048]{1,0:T(8,128)S(1)}, f32[16,2048]{1,0:T(8,128)S(1)}, bf16[8,16,16,2048]{3,2,1,0:T(8,128)(2,1)}, s32[8,16]{1,0:T(8,128)S(...) while((s32[]{:T(128)}, f32[16,2048]{1,0:T(8,128)S(1)}, ...), condition=%wide.region_4.4_spmd.clone, body=%wide.region_3.3_spmd.clone.sunk | while | flops 27035824 | bytes 10504361 | solution.py:103
  344.3 1.1 bitcast_dynamic-update-slice_fusion.47
  381.8 1.1 bitcast_dynamic-update-slice_fusion.47
  382.9 8.5 fusion.60
  392.9 149.9 %while.54 = (s32[]{:T(128)}, f32[16,2048]{1,0:T(8,128)S(1)}, f32[16,2048]{1,0:T(8,128)S(1)}, bf16[8,16,16,2048]{3,2,1,0:T(8,128)(2,1)}, s32[8,16]{1,0:T(8,128)S(...) while((s32[]{:T(128)}, f32[16,2048]{1,0:T(8,128)S(1)}, ...), condition=%wide.region_4.4_spmd.clone, body=%wide.region_3.3_spmd.clone.sunk | while | flops 27035824 | bytes 10504361 | solution.py:103
  504.2 1.1 bitcast_dynamic-update-slice_fusion.47
  541.7 1.1 bitcast_dynamic-update-slice_fusion.47
  542.8 8.5 fusion.60
  552.9 149.9 %while.54 = (s32[]{:T(128)}, f32[16,2048]{1,0:T(8,128)S(1)}, f32[16,2048]{1,0:T(8,128)S(1)}, bf16[8,16,16,2048]{3,2,1,0:T(8,128)(2,1)}, s32[8,16]{1,0:T(8,128)S(...) while((s32[]{:T(128)}, f32[16,2048]{1,0:T(8,128)S(1)}, ...), condition=%wide.region_4.4_spmd.clone, body=%wide.region_3.3_spmd.clone.sunk | while | flops 27035824 | bytes 10504361 | solution.py:103
  664.2 1.1 bitcast_dynamic-update-slice_fusion.47
  701.7 1.1 bitcast_dynamic-update-slice_fusion.47
  702.8 8.5 fusion.60
  712.8 149.9 %while.54 = (s32[]{:T(128)}, f32[16,2048]{1,0:T(8,128)S(1)}, f32[16,2048]{1,0:T(8,128)S(1)}, bf16[8,16,16,2048]{3,2,1,0:T(8,128)(2,1)}, s32[8,16]{1,0:T(8,128)S(...) while((s32[]{:T(128)}, f32[16,2048]{1,0:T(8,128)S(1)}, ...), condition=%wide.region_4.4_spmd.clone, body=%wide.region_3.3_spmd.clone.sunk | while | flops 27035824 | bytes 10504361 | solution.py:103
  824.1 1.1 bitcast_dynamic-update-slice_fusion.47
  861.6 1.1 bitcast_dynamic-update-slice_fusion.47
  862.7 8.5 fusion.60
  872.7 149.9 %while.54 = (s32[]{:T(128)}, f32[16,2048]{1,0:T(8,128)S(1)}, f32[16,2048]{1,0:T(8,128)S(1)}, bf16[8,16,16,2048]{3,2,1,0:T(8,128)(2,1)}, s32[8,16]{1,0:T(8,128)S(...) while((s32[]{:T(128)}, f32[16,2048]{1,0:T(8,128)S(1)}, ...), condition=%wide.region_4.4_spmd.clone, body=%wide.region_3.3_spmd.clone.sunk | while | flops 27035824 | bytes 10504361 | solution.py:103
  984.0 1.1 bitcast_dynamic-update-slice_fusion.47
  1021.5 1.1 bitcast_dynamic-update-slice_fusion.47
  1022.6 8.5 fusion.60
  1032.7 149.9 %while.54 = (s32[]{:T(128)}, f32[16,2048]{1,0:T(8,128)S(1)}, f32[16,2048]{1,0:T(8,128)S(1)}, bf16[8,16,16,2048]{3,2,1,0:T(8,128)(2,1)}, s32[8,16]{1,0:T(8,128)S(...) while((s32[]{:T(128)}, f32[16,2048]{1,0:T(8,128)S(1)}, ...), condition=%wide.region_4.4_spmd.clone, body=%wide.region_3.3_spmd.clone.sunk | while | flops 27035824 | bytes 10504361 | solution.py:103
  1144.0 1.1 bitcast_dynamic-update-slice_fusion.47
  1181.5 1.1 bitcast_dynamic-update-slice_fusion.47
  1182.6 8.5 fusion.60
  1192.6 149.9 %while.54 = (s32[]{:T(128)}, f32[16,2048]{1,0:T(8,128)S(1)}, f32[16,2048]{1,0:T(8,128)S(1)}, bf16[8,16,16,2048]{3,2,1,0:T(8,128)(2,1)}, s32[8,16]{1,0:T(8,128)S(...) while((s32[]{:T(128)}, f32[16,2048]{1,0:T(8,128)S(1)}, ...), condition=%wide.region_4.4_spmd.clone, body=%wide.region_3.3_spmd.clone.sunk | while | flops 27035824 | bytes 10504361 | solution.py:103
  1341.4 1.1 bitcast_dynamic-update-slice_fusion.47
  1342.5 8.5 fusion.60
  1352.5 149.9 %while.54 = (s32[]{:T(128)}, f32[16,2048]{1,0:T(8,128)S(1)}, f32[16,2048]{1,0:T(8,128)S(1)}, bf16[8,16,16,2048]{3,2,1,0:T(8,128)(2,1)}, s32[8,16]{1,0:T(8,128)S(...) while((s32[]{:T(128)}, f32[16,2048]{1,0:T(8,128)S(1)}, ...), condition=%wide.region_4.4_spmd.clone, body=%wide.region_3.3_spmd.clone.sunk | while | flops 27035824 | bytes 10504361 | solution.py:103
  1501.3 1.1 bitcast_dynamic-update-slice_fusion.47
  1502.4 8.5 fusion.60
  1511.0 6.2 copy.51
  1517.2 5.8 reshape.1157
  1523.0 16.6 %all_to_all.33 = f32[4,1,65536]{2,1,0:T(1,128)S(1)} all-to-all(f32[4,1,65536]{2,1,0:T(1,128)S(1)} %reshape.1157), channel_id=1, replica_groups=mesh['tm'=4,'lat'=8] {'tm'}, dimensions={0} | all-to-all | bytes 2097152 | tf_op jit(solution)/shard_map/all_to_all | solution.py:116
  1540.2 3.8 reduce
  1544.0 6.1 reshape.1158
  1550.1 5.5 copy.52
  1555.7 1.2 copy.44
  (1660 shorter events, 531.6 us)
Async XLA Ops:
  6.5 188.1 %reduce-scatter.5.cloned.1.call-start = ((), (), s32[]{:S(2)}) async-start(), calls=%async_computation.3 | async-start | bytes 10485760
  197.9 31.2 %all-to-all-start = ((bf16[2,8,16,8,256]{4,3,0,2,1:T(8,128)(2,1)}), bf16[2,8,16,8,256]{4,3,0,2,1:T(8,128)(2,1)S(1)}, u32[]{:S(2)}, u32[]{:S(2)}) async-start(bf16[2,8,16,8,256]{4,3,0,2,1:T(8,128)(2,1)} %copy.70), calls=%async_computation | async-start | bytes 2097152 | tf_op jit(solution)/shard_map/all_to_all | solution.py:93
  233.0 149.9 %copy-start = (bf16[2,16,8,2048]{3,2,0,1:T(8,128)(2,1)S(1)}, bf16[2,16,8,2048]{3,2,0,1:T(8,128)(2,1)}, u32[]{:S(2)}) copy-start(bf16[2,16,8,2048]{3,2,0,1:T(8,128)(2,1)} %get-tuple-element.1237) | copy-start | bytes 3145732 | tf_op jit(solution)/shard_map/while
  392.9 149.9 %copy-start = (bf16[2,16,8,2048]{3,2,0,1:T(8,128)(2,1)S(1)}, bf16[2,16,8,2048]{3,2,0,1:T(8,128)(2,1)}, u32[]{:S(2)}) copy-start(bf16[2,16,8,2048]{3,2,0,1:T(8,128)(2,1)} %get-tuple-element.1237) | copy-start | bytes 3145732 | tf_op jit(solution)/shard_map/while
  552.9 149.9 %copy-start = (bf16[2,16,8,2048]{3,2,0,1:T(8,128)(2,1)S(1)}, bf16[2,16,8,2048]{3,2,0,1:T(8,128)(2,1)}, u32[]{:S(2)}) copy-start(bf16[2,16,8,2048]{3,2,0,1:T(8,128)(2,1)} %get-tuple-element.1237) | copy-start | bytes 3145732 | tf_op jit(solution)/shard_map/while
  712.8 149.9 %copy-start = (bf16[2,16,8,2048]{3,2,0,1:T(8,128)(2,1)S(1)}, bf16[2,16,8,2048]{3,2,0,1:T(8,128)(2,1)}, u32[]{:S(2)}) copy-start(bf16[2,16,8,2048]{3,2,0,1:T(8,128)(2,1)} %get-tuple-element.1237) | copy-start | bytes 3145732 | tf_op jit(solution)/shard_map/while
  872.7 149.9 %copy-start = (bf16[2,16,8,2048]{3,2,0,1:T(8,128)(2,1)S(1)}, bf16[2,16,8,2048]{3,2,0,1:T(8,128)(2,1)}, u32[]{:S(2)}) copy-start(bf16[2,16,8,2048]{3,2,0,1:T(8,128)(2,1)} %get-tuple-element.1237) | copy-start | bytes 3145732 | tf_op jit(solution)/shard_map/while
  1032.6 149.9 %copy-start = (bf16[2,16,8,2048]{3,2,0,1:T(8,128)(2,1)S(1)}, bf16[2,16,8,2048]{3,2,0,1:T(8,128)(2,1)}, u32[]{:S(2)}) copy-start(bf16[2,16,8,2048]{3,2,0,1:T(8,128)(2,1)} %get-tuple-element.1237) | copy-start | bytes 3145732 | tf_op jit(solution)/shard_map/while
  1192.6 149.9 %copy-start = (bf16[2,16,8,2048]{3,2,0,1:T(8,128)(2,1)S(1)}, bf16[2,16,8,2048]{3,2,0,1:T(8,128)(2,1)}, u32[]{:S(2)}) copy-start(bf16[2,16,8,2048]{3,2,0,1:T(8,128)(2,1)} %get-tuple-element.1237) | copy-start | bytes 3145732 | tf_op jit(solution)/shard_map/while
  1352.5 149.9 %copy-start = (bf16[2,16,8,2048]{3,2,0,1:T(8,128)(2,1)S(1)}, bf16[2,16,8,2048]{3,2,0,1:T(8,128)(2,1)}, u32[]{:S(2)}) copy-start(bf16[2,16,8,2048]{3,2,0,1:T(8,128)(2,1)} %get-tuple-element.1237) | copy-start | bytes 3145732 | tf_op jit(solution)/shard_map/while
Sparse Core Ops, SparseCore 0:
  105.5 89.0 reduce-scatter.4
where the time goes:
time: 1580 us; the launch traced here: 1560 us
  loops' own time  668 us (42%)
  other arithmetic  466 us (29%)
  local copies, waits for them, and re-layouts  161 us (10%)
  matrix products  119 us (8%)
  waiting for transfers between devices  115 us (7%)
  blocking collectives  16.6 us (1%)
    another operation x8, loops' own time, one_span(): lax.scan(stepper, state, offset + jnp.arange(span_len, dtype=jnp.int32),...  668 us
    while x960, other arithmetic  363 us
    unnamed x2, waiting for transfers between devices  89.3 us
    dot_general x8, matrix products, one_span(): jnp.einsum('ekfr,lkr->ekfl', band, polynomials, preferred_element_type=jn...  68.4 us
    dynamic_update_slice x64, local copies, waits for them, and re-layouts, one_span(): lax.scan(stepper, state, offset + jnp.arange(span_len, dtype=jnp.int32),...  68.1 us
    slice x64, local copies, waits for them, and re-layouts, one_span(): lax.scan(stepper, state, offset + jnp.arange(span_len, dtype=jnp.int32),...  45.9 us
    concatenate x64, other arithmetic, one_span(): lax.scan(stepper, state, offset + jnp.arange(span_len, dtype=jnp.int32),...  42.8 us
    dot_general x1, matrix products, shards(): jnp.einsum('nc,trn->ctr', lon_weights, frames, preferred_element_type=jnp...  42.7 us
  transfers between devices with their start and end apart: 2, of which 2 were waited for; matrix products, arithmetic and copies ran while one was open for 0% of the time, Pallas kernels for 0%

commit v1 on v0

v1 whole, which is shorter than its diff:
```python
from functools import partial
import math

import jax
import jax.numpy as jnp
import numpy as np
from jax import lax
from jax.experimental import pallas as pl
from jax.experimental.pallas import tpu as pltpu
from jax.sharding import PartitionSpec as P

L = 1024
F = 8
EF = 2 * F
ROWS = 16
WIDE = ROWS * EF
CHUNKS = 4
GROUP = 8
SPAN = 128
VMEM = 48 * 1024 * 1024


def natural_tables(nlon, order_count):
    half = nlon // 2
    points = np.arange(half, dtype=np.int64)[None, :]
    factor = np.float32(math.sqrt(2.0 / nlon))
    tables = []
    for parity in range(2):
        orders = np.arange(parity, order_count, 2, dtype=np.int64)[:, None]
        angles = (orders * points % nlon).astype(np.float32) * np.float32(2.0 * math.pi / nlon)
        parts = [np.cos(angles) * factor, -np.sin(angles) * factor]
        tables.append(np.concatenate(parts, axis=0).astype(jnp.bfloat16))
    return tables


def time_table(total_frames, band_count, first_frame, frame_count):
    frames_at = first_frame + jnp.arange(frame_count, dtype=jnp.int32)
    frequency = total_frames // 8 + jnp.arange(band_count, dtype=jnp.int32)
    phases = frequency[:, None] * frames_at[None, :] % total_frames
    angles = phases.astype(jnp.float32) * (2.0 * math.pi / total_frames)
    factor = 1.0 / math.sqrt(total_frames)
    cos_part = jnp.cos(angles) * factor
    sin_part = jnp.sin(angles) * factor
    top_row = jnp.stack([cos_part, sin_part], axis=1)
    low_row = jnp.stack([-sin_part, cos_part], axis=1)
    return jnp.stack([top_row, low_row], axis=0).astype(jnp.bfloat16)


def transform_kernel(south_ref, frames_ref, even_ref, odd_ref, time_ref, place_ref, *outs):
    frame_count, rows, nlon = frames_ref.shape
    half = nlon // 2
    image = frames_ref[...].reshape(frame_count * rows, nlon)
    near, far = image[:, :half], image[:, half:]
    bands = []
    for table_ref, folded in ((even_ref, near + far), (odd_ref, near - far)):
        count = table_ref.shape[0] // 2
        coef = lax.dot_general(
            table_ref[...], folded, (((1,), (1,)), ((), ())), preferred_element_type=jnp.float32
        ).astype(jnp.bfloat16)
        bands.append(
            jnp.dot(coef[:count], time_ref[0], preferred_element_type=jnp.float32)
            + jnp.dot(coef[count:], time_ref[1], preferred_element_type=jnp.float32)
        )
    band = jnp.concatenate(bands, axis=0).astype(jnp.bfloat16)
    placed = jnp.dot(place_ref[...], band, preferred_element_type=jnp.float32).astype(jnp.bfloat16)
    size = outs[0].shape[0]
    for i, out in enumerate(outs):
        out[...] = placed[i * size : (i + 1) * size]


def transform_chunk(chunk, south, frames, even, odd, time_mat, place):
    frame_count, row_count, nlon = frames.shape
    blocks = row_count // ROWS
    per_chunk = blocks // CHUNKS
    order_count = place.shape[0]
    size = order_count // 4

    def frame_block(b, south_ref):
        at = chunk * per_chunk + b
        return (0, jnp.where(south_ref[0] == 1, blocks - 1 - at, at), 0)

    def whole(b, south_ref):
        return (0, 0)

    out = jax.ShapeDtypeStruct((size, per_chunk * WIDE), jnp.bfloat16)
    flops = 2 * blocks // CHUNKS * WIDE * order_count * (nlon + 2 * WIDE + order_count)
    return pl.pallas_call(
        transform_kernel,
        grid_spec=pltpu.PrefetchScalarGridSpec(
            num_scalar_prefetch=1,
            grid=(per_chunk,),
            in_specs=[
                pl.BlockSpec((frame_count, ROWS, nlon), frame_block),
                pl.BlockSpec(even.shape, whole),
                pl.BlockSpec(odd.shape, whole),
                pl.BlockSpec(time_mat.shape, lambda b, s: (0, 0, 0)),
                pl.BlockSpec(place.shape, whole),
            ],
            out_specs=[pl.BlockSpec((size, WIDE), lambda b, s: (0, b))] * 4,
        ),
        out_shape=[out] * 4,
        compiler_params=pltpu.CompilerParams(vmem_limit_bytes=VMEM),
        cost_estimate=pl.CostEstimate(
            flops=flops, bytes_accessed=frames.size * 2 // CHUNKS + 4 * 2**20, transcendentals=0
        ),
        name="longitude_time",
    )(south, frames, even, odd, time_mat, place)


def degree_tables(orders, degree_count):
    level = jnp.arange(degree_count, dtype=jnp.float32)[None, :]
    level_sq = level * level
    order_sq = jnp.square(orders.astype(jnp.float32))[:, None]
    lower = level - 1.0
    rising = jnp.sqrt(
        jnp.maximum(4.0 * level_sq - 1.0, 0.0) / jnp.maximum(level_sq - order_sq, 1.0)
    )
    falling = jnp.sqrt(
        jnp.maximum(lower * lower - order_sq, 0.0) / jnp.maximum(4.0 * lower * lower - 1.0, 1.0)
    )
    return rising, rising * falling


def order_start(orders, rows, nlat_count, order_count):
    order_val = orders.astype(jnp.float32)[:, None]
    steps_k = jnp.arange(1, order_count + 1, dtype=jnp.float32)[None, :]
    growth = jnp.sum(
        jnp.where(steps_k <= order_val, jnp.log1p(0.5 / steps_k), 0.0), axis=1, keepdims=True
    )
    colatitude = (rows.astype(jnp.float32) + 0.5) * (math.pi / nlat_count)
    cosine = jnp.cos(colatitude)
    sine_row = jnp.sin(colatitude)
    lognorm = 0.5 * math.log(0.5) + 0.5 * growth + order_val * jnp.log(sine_row)[None, :]
    weight = sine_row * (math.pi / nlat_count) * math.sqrt(nlat_count)
    safe_log = jnp.maximum(lognorm, -60.0)
    start_value = jnp.where(lognorm >= -60.0, jnp.exp(safe_log), 0.0)
    return cosine, start_value * weight[None, :]


def polynomial_kernel(
    half,
    order_ref, rise_a, fall_a, rise_b, fall_b, x_ref, start_a, start_b,
    out_a, out_b, state_a, state_b,
):
    step = pl.program_id(0)
    base = step * SPAN
    chunks, _, lanes_a = out_a.shape
    lanes_b = out_b.shape[2]

    @pl.when(step == 0)
    def _():
        state_a[...] = jnp.zeros_like(state_a)
        state_b[...] = jnp.zeros_like(state_b)

    x_a = x_ref[...]
    x_b = jnp.concatenate(
        [x_a[:, (c + 1) * lanes_a - lanes_b : (c + 1) * lanes_a] for c in range(chunks)], axis=1
    )
    group_a = (0, rise_a, fall_a, x_a, start_a, state_a, out_a, lanes_a)
    group_b = (1, rise_b, fall_b, x_b, start_b, state_b, out_b, lanes_b)

    def run(*groups):
        states = [(g[5][0], g[5][1]) for g, _ in groups]
        for i in range(SPAN // 2):
            for n, ((which, rise, fall, x, start, _, out, lanes), begins) in enumerate(groups):
                made = []
                for at in (2 * i, 2 * i + 1):
                    older, last = states[n]
                    new = (rise[:, at : at + 1] * x) * last - fall[:, at : at + 1] * older
                    if begins:
                        here = jnp.where(order_ref[which, :, :1] == base + at, 1.0, 0.0)
                        new = new + here * start[...]
                    states[n] = (last, new)
                    made.append(new)
                both = jnp.concatenate(made, axis=0).astype(jnp.bfloat16)
                for c in range(chunks):
                    out[c, 2 * GROUP * i : 2 * GROUP * (i + 1), :] = both[
                        :, c * lanes : (c + 1) * lanes
                    ]
        for (g, _), state in zip(groups, states):
            g[5][0], g[5][1] = state

    @pl.when(step < half)
    def _():
        run((group_a, True))

    @pl.when(jnp.logical_and(step >= half, step < 2 * half))
    def _():
        run((group_a, False), (group_b, True))

    @pl.when(step >= 2 * half)
    def _():
        run((group_a, False), (group_b, False))


def polynomials(small, large, order_count, nlat, rows_each):
    nlat_count = nlat * rows_each
    half = order_count // 2 // SPAN
    rows = jnp.arange(nlat_count // 2, dtype=jnp.int32)
    rows = rows.reshape(nlat // 2, CHUNKS, rows_each // CHUNKS).transpose(1, 0, 2)
    lanes_a = nlat_count // 2 // CHUNKS
    lanes_b = lanes_a // 2
    cosine, start_a = order_start(small, rows.reshape(-1), nlat_count, order_count)
    _, start_b = order_start(
        large, rows[:, nlat // 4 :].reshape(-1), nlat_count, order_count
    )
    rise_a, fall_a = degree_tables(small, L)
    rise_b, fall_b = degree_tables(large, L)
    orders = jnp.broadcast_to(jnp.stack([small, large])[:, :, None], (2, GROUP, 128))
    x = jnp.broadcast_to(cosine[None, :], (GROUP, nlat_count // 2))
    table = pl.BlockSpec((GROUP, SPAN), lambda s: (0, s))

    def fixed(shape):
        return pl.BlockSpec(shape, lambda s: (0,) * len(shape))

    return pl.pallas_call(
        partial(polynomial_kernel, half),
        grid=(L // SPAN,),
        in_specs=[
            fixed(orders.shape), table, table, table, table,
            fixed(x.shape), fixed(start_a.shape), fixed(start_b.shape),
        ],
        out_specs=[
            pl.BlockSpec((CHUNKS, SPAN * GROUP, lanes_a), lambda s: (0, s, 0)),
            pl.BlockSpec(
                (CHUNKS, SPAN * GROUP, lanes_b), lambda s: (0, jnp.maximum(s - half, 0), 0)
            ),
        ],
        out_shape=[
            jax.ShapeDtypeStruct((CHUNKS, L * GROUP, lanes_a), jnp.bfloat16),
            jax.ShapeDtypeStruct(
                (CHUNKS, (L - order_count // 2) * GROUP, lanes_b), jnp.bfloat16
            ),
        ],
        scratch_shapes=[
            pltpu.VMEM((2,) + start_a.shape, jnp.float32),
            pltpu.VMEM((2,) + start_b.shape, jnp.float32),
        ],
        compiler_params=pltpu.CompilerParams(vmem_limit_bytes=VMEM),
        cost_estimate=pl.CostEstimate(
            flops=2 * 10**9, bytes_accessed=24 * 2**20, transcendentals=0
        ),
        name="legendre",
    )(orders, rise_a, fall_a, rise_b, fall_b, x, start_a, start_b)


def swap_groups(x):
    sub = lax.broadcasted_iota(jnp.int32, x.shape, 1)
    lane = lax.broadcasted_iota(jnp.int32, x.shape, 2) // EF
    for bit in (1, 2, 4):
        down = pltpu.roll(pltpu.roll(x, 8 - bit, 1), EF * bit, 2)
        up = pltpu.roll(pltpu.roll(x, bit, 1), 128 - EF * bit, 2)
        sub_on, lane_on = (sub & bit) != 0, (lane & bit) != 0
        x = jnp.where(sub_on == lane_on, x, jnp.where(sub_on, up, down))
    return x


def contract_kernel(half, last, z_ref, mask_ref, p_a, p_b, *refs):
    acc_ref = refs[0] if len(refs) == 4 else None
    out_ref, w_a, w_b = refs[-3:]
    step = pl.program_id(0)
    nlat = z_ref.shape[0]
    lanes = z_ref.shape[2]

    @pl.when(step == 0)
    def _():
        for g, w_ref, first in ((0, w_a, 0), (1, w_b, nlat // 4)):
            for part, sign in ((0, 1.0), (1, -1.0)):
                pieces = []
                for s in range(first, nlat // 2):
                    north = z_ref[s].astype(jnp.float32)[g * GROUP : (g + 1) * GROUP]
                    south = z_ref[nlat - 1 - s].astype(jnp.float32)[g * GROUP : (g + 1) * GROUP]
                    both = north + sign * south
                    pieces += [both[:, i : i + 128] for i in range(0, lanes, 128)]
                block = swap_groups(jnp.stack(pieces, axis=0))
                w_ref[:, part * 128 : (part + 1) * 128] = block.reshape(
                    len(pieces) * GROUP, 128
                ).astype(jnp.bfloat16)

    def picked(p_ref, w_ref, g):
        tile = 256
        out = []
        for i in range(0, SPAN * GROUP, tile):
            product = jnp.dot(
                p_ref[0, i : i + tile, :], w_ref[...], preferred_element_type=jnp.float32
            ).reshape(tile // 16, 16, 256)
            kept = product[:, :, :128] * mask_ref[g, 0] + product[:, :, 128:] * mask_ref[g, 1]
            out.append(jnp.sum(kept.reshape(tile // GROUP, GROUP, 128), axis=1))
        return jnp.concatenate(out, axis=0)

    def put(part, value):
        at = slice(part * 128, (part + 1) * 128)
        if acc_ref is not None:
            value = value + acc_ref[:, at]
        if last:
            out_ref[0, at, :] = value.T.astype(out_ref.dtype)
        else:
            out_ref[:, at] = value

    put(0, picked(p_a, w_a, 0))

    @pl.when(step < half)
    def _():
        put(1, jnp.zeros((SPAN, 128), jnp.float32))

    @pl.when(step >= half)
    def _():
        put(1, picked(p_b, w_b, 1))


def contract_chunk(chunk, z, masks, p_a, p_b, acc, half, ntm):
    last = chunk == CHUNKS - 1
    lanes_a, lanes_b = p_a.shape[2], p_b.shape[2]
    acc_spec = pl.BlockSpec((SPAN, 256), lambda s: (s, 0))
    spans = L // ntm // SPAN
    if last:
        out_shape = jax.ShapeDtypeStruct((ntm, 256, L // ntm), jnp.bfloat16)
        out_spec = pl.BlockSpec((1, 256, SPAN), lambda s: (s // spans, 0, s % spans))
    else:
        out_shape = jax.ShapeDtypeStruct((L, 256), jnp.float32)
        out_spec = acc_spec
    return pl.pallas_call(
        partial(contract_kernel, half, last),
        grid=(L // SPAN,),
        in_specs=[
            pl.BlockSpec(z.shape, lambda s: (0, 0, 0)),
            pl.BlockSpec(masks.shape, lambda s: (0, 0, 0, 0)),
            pl.BlockSpec((1, SPAN * GROUP, lanes_a), lambda s: (chunk, s, 0)),
            pl.BlockSpec(
                (1, SPAN * GROUP, lanes_b), lambda s: (chunk, jnp.maximum(s - half, 0), 0)
            ),
        ]
        + [acc_spec] * (acc is not None),
        out_specs=out_spec,
        out_shape=out_shape,
        scratch_shapes=[
            pltpu.VMEM((lanes_a, 256), jnp.bfloat16),
            pltpu.VMEM((lanes_b, 256), jnp.bfloat16),
        ],
        compiler_params=pltpu.CompilerParams(vmem_limit_bytes=VMEM),
        cost_estimate=pl.CostEstimate(
            flops=2 * L * GROUP * (lanes_a + lanes_b) * 256,
            bytes_accessed=L * GROUP * (lanes_a + lanes_b) * 2 + 2 * 2**20,
            transcendentals=0,
        ),
        name="latitude_sum",
    )(z, masks, p_a, p_b, *([acc] if acc is not None else []))


def swap_with(x, axis, bit):
    count = lax.axis_size(axis)
    return lax.ppermute(x, axis, [(i, i ^ (1 << bit)) for i in range(count)])


def add(a, b):
    return (a.astype(jnp.float32) + b.astype(jnp.float32)).astype(jnp.bfloat16)


def reduce_over_time(keep, send, bits):
    for i, bit in enumerate(bits):
        got = swap_with(send, "tm", bit)
        if i == len(bits) - 1:
            return add(keep, got)
        middle = keep.shape[0] // 2
        send = add(keep[middle:], got[middle:])
        keep = add(keep[:middle], got[:middle])


def bit_order(bits, count):
    offsets = []
    for position in range(count):
        offset = 0
        for i, bit in enumerate(bits):
            if position >> (len(bits) - 1 - i) & 1:
                offset |= 1 << bit
        offsets.append(offset)
    return jnp.array(offsets, jnp.int32)


def shards(frames, owner_map):
    frame_count, row_count, nlon = frames.shape
    order_count = owner_map.shape[0]
    nlat, ntm = lax.axis_size("lat"), lax.axis_size("tm")
    my_tm, my_lat = lax.axis_index("tm"), lax.axis_index("lat")
    south = my_lat >= nlat // 2
    levels = ntm.bit_length() - 1
    bits_a = list(range(levels))
    bits_b = bits_a[-1:] + bits_a[:-1]

    pairs = owner_map.reshape(nlat, ntm, -1, 2)
    owned = pairs.shape[2]
    small, large = jnp.min(pairs, axis=3), jnp.max(pairs, axis=3)

    def in_order(orders, bits):
        return orders.transpose(1, 0, 2)[bit_order(bits, ntm) ^ my_tm].reshape(-1)

    wanted = jnp.concatenate([in_order(small, bits_a), in_order(large, bits_b)])
    wanted = wanted // 2 + wanted % 2 * (order_count // 2)
    place = (wanted[:, None] == jnp.arange(order_count, dtype=jnp.int32)[None, :]).astype(
        jnp.bfloat16
    )
    even, odd = (jnp.asarray(t) for t in natural_tables(nlon, order_count))
    weights = time_table(frame_count * ntm, F, my_tm * frame_count, frame_count)
    row_in, row_out = jnp.arange(ROWS)[:, None], jnp.arange(ROWS)[None, :]
    same_row = (jnp.where(south, ROWS - 1 - row_in, row_in) == row_out).astype(jnp.bfloat16)
    time_mat = (
        weights.transpose(2, 3, 0, 1).reshape(2, frame_count, 1, 1, EF)
        * same_row[None, None, :, :, None]
    ).reshape(2, frame_count * ROWS, WIDE)
    south_flag = south.astype(jnp.int32).reshape(1)

    def padded(orders):
        return jnp.pad(orders[my_lat, my_tm], (0, GROUP - owned), mode="edge")

    my_small, my_large = padded(small), padded(large)
    p_a, p_b = polynomials(my_small, my_large, order_count, nlat, row_count)
    half = order_count // 2 // SPAN
    mine = jnp.stack([my_small, my_large])
    slot = jnp.arange(GROUP)
    own = slot[:, None] == (jnp.arange(128) // EF)[None, :]
    parity = (mine[:, None, :] + jnp.arange(2)[None, :, None]) % 2
    masks = jnp.stack(
        [
            (own[None, None] & (parity[..., None] == u)).reshape(2, 2 * GROUP, 128)
            for u in range(2)
        ],
        axis=1,
    ).astype(jnp.float32)

    acc = None
    for chunk in range(CHUNKS):
        keep_a, send_a, keep_b, send_b = transform_chunk(
            chunk, south_flag, frames, even, odd, time_mat, place
        )
        done_a = reduce_over_time(keep_a, send_a, bits_a)
        done_b = reduce_over_time(keep_b, send_b, bits_b)
        width = done_a.shape[1]
        band = jnp.concatenate(
            [done_a.reshape(nlat, owned, width), done_b.reshape(nlat, owned, width)], axis=1
        )
        band = lax.all_to_all(band, "lat", split_axis=0, concat_axis=0, tiled=True)
        if owned < GROUP:
            band = jnp.pad(
                band.reshape(nlat, 2, owned, width),
                ((0, 0), (0, 0), (0, GROUP - owned), (0, 0)),
            ).reshape(nlat, 2 * GROUP, width)
        acc = contract_chunk(chunk, band, masks, p_a, p_b, acc, half, ntm)

    spectra = lax.all_to_all(acc, "tm", split_axis=0, concat_axis=0, tiled=True)
    spectra = spectra.reshape(ntm, 2, GROUP, 2, F, L // ntm)[:, :, :owned]
    first_small = (pairs[my_lat, :, :, 0] < order_count // 2)[:, :, None, None, None]
    low, high = spectra[:, 0], spectra[:, 1]
    slots = jnp.stack(
        [jnp.where(first_small, low, high), jnp.where(first_small, high, low)], axis=2
    )
    slots = slots.transpose(3, 0, 1, 2, 4, 5).reshape(2, ntm * owned * 2, F, L // ntm)
    return slots.astype(jnp.float32)


def solution(mesh):
    return jax.shard_map(
        shards,
        mesh=mesh,
        in_specs=(P("tm", "lat", None), P()),
        out_specs=P(None, "lat", None, "tm"),
        check_vma=False,
    )
```

time: 1580 us -> 224 us (0.14)
  loops' own time: 668 us -> 0 us
  other arithmetic: 466 us -> 27.1 us
  local copies, waits for them, and re-layouts: 161 us -> 21.8 us
  matrix products: 119 us -> 0 us
  Pallas kernels: 0 us -> 103 us
  waiting for transfers between devices: 115 us -> 31.5 us
  starting transfers between devices: 4.6 us -> 38.2 us
  blocking collectives: 16.6 us -> 0 us
    another operation x9 -> x0, loops' own time: 668 us -> none  [the longest x8 668 us: one_span(): lax.scan(stepper, state, offset + jnp.arange(span_len, dtype=jnp.int32),...]
    while x960 -> x0, other arithmetic: 363 us -> none
    dot_general x10 -> x0, matrix products: 119 us -> none  [the longest x8 68.4 us: one_span(): jnp.einsum('ekfr,lkr->ekfl', band, polynomials, preferred_element_type=jn...]
    pallas_call x0 -> x9, Pallas kernels: none -> 103 us  [the longest x4 56.4 us: transform_chunk(): pl.pallas_call(transform_kernel, grid_spec=pltpu.PrefetchScalarGridSpec(n...]
    unnamed x2 -> x0, waiting for transfers between devices: 89.3 us -> none
    dynamic_update_slice x64 -> x0, local copies, waits for them, and re-layouts: 68.1 us -> none  [one_span(): lax.scan(stepper, state, offset + jnp.arange(span_len, dtype=jnp.int32),...]
    slice x64 -> x0, local copies, waits for them, and re-layouts: 45.9 us -> none  [one_span(): lax.scan(stepper, state, offset + jnp.arange(span_len, dtype=jnp.int32),...]
    concatenate x64 -> x4, other arithmetic: 42.8 us -> 2.87 us  [shards(): jnp.concatenate([done_a.reshape(nlat, owned, width), done_b.reshape(nlat,...]
  transfers between devices with their start and end apart: 2 -> 21, of which waited for: 2 -> 6; matrix products, arithmetic and copies ran while one was open for 0% -> 12% of each run, Pallas kernels for 0% -> 36%
where the time goes in v1:
time: 224 us; the launch traced here: 222 us
  Pallas kernels  103 us (46%)
  starting transfers between devices  38.2 us (17%)
  waiting for transfers between devices  31.5 us (14%)
  other arithmetic  27.1 us (12%)
  local copies, waits for them, and re-layouts  21.8 us (10%)
    pallas_call x4, Pallas kernels, transform_chunk(): pl.pallas_call(transform_kernel, grid_spec=pltpu.PrefetchScalarGridSpec(n...  56.4 us
    pallas_call x4, Pallas kernels, contract_chunk(): pl.pallas_call(partial(contract_kernel, half, last), grid=(L // SPAN,), i...  34.5 us
    all_to_all x4, waiting for transfers between devices, shards(): band = lax.all_to_all(band, 'lat', split_axis=0, concat_axis=0, tiled=True)  20.7 us
    ppermute x16, starting transfers between devices, swap_with(): return lax.ppermute(x, axis, [(i, i ^ 1 << bit) for i in range(count)])  19.7 us
    all_to_all x4, starting transfers between devices, shards(): band = lax.all_to_all(band, 'lat', split_axis=0, concat_axis=0, tiled=True)  15.1 us
    pallas_call x1, Pallas kernels, polynomials(): pl.pallas_call(partial(polynomial_kernel, half), grid=(L // SPAN,), in_sp...  12.2 us
    all_to_all x1, waiting for transfers between devices, shards(): spectra = lax.all_to_all(acc, 'tm', split_axis=0, concat_axis=0, tiled=True)  8.89 us
    mul x5, local copies, waits for them, and re-layouts, shards(): weights.transpose(2, 3, 0, 1).reshape(2, frame_count, 1, 1, EF)  8.35 us
  transfers between devices with their start and end apart: 21, of which 6 were waited for; matrix products, arithmetic and copies ran while one was open for 12% of the time, Pallas kernels for 36%

profile of v1, /device:TPU:0, one launch (start us, length us, event | category | flops | bytes accessed | tf_op | source)
XLA Modules:
  0.0 222.3 jit_solution(994906395451520670)
XLA Ops:
  2.0 1.2 fusion.35
  4.7 1.2 mul.295
  6.0 2.2 mul.296
  8.2 1.6 mul.293
  9.8 3.2 %mul.294 = bf16[2,256,256]{2,1,0:T(8,128)(2,1)S(1)} reshape(bf16[2,16,16,16,16]{4,3,2,1,0:T(8,128)(2,1)} %mul.293) | data formatting | bytes 524288 | tf_op jit(solution)/shard_map/mul | solution.py:407
  13.1 1.6 copy-done.1
  14.6 14.2 %longitude_time.7 = (bf16[128,1024]{1,0:T(8,128)(2,1)S(1)}, bf16[128,1024]{1,0:T(8,128)(2,1)}, bf16[128,1024]{1,0:T(8,128)(2,1)S(1)}, bf16[128,1024]{1,0:T(8,128)(2,1)}) custom-call(s32[1]{0:T(128)} %bitcast.south_ref, bf16[16,256,4096]{2,1,0:T(8,128)(2,1)} %frames_ref.7, bf16[512,2048]{1,0:T(8,128)(2,1)S(1)} %copy-done.1, bf16[512,2048]{1,0:T(8,128)(2,1)S(1)} %copy-done, ...), custom_call_target="tpu_custom_call" | custom-call | flops 5368709120 | bytes 12582912 | tf_op jit(solution)/shard_map/longitude_time/pallas_call | solution.py:87
  30.3 2.9 %collective-permute-start.12 = (bf16[128,1024]{1,0:T(8,128)(2,1)}, bf16[128,1024]{1,0:T(8,128)(2,1)}, u32[]{:S(2)}, u32[]{:S(2)}) collective-permute-start(bf16[128,1024]{1,0:T(8,128)(2,1)} %get-tuple-element.38), channel_id=1, source_target_pairs={{0,8},{8,0},{16,24},{24,16},{1,9},{9,1},{17,25},{25,17},{2,10},{10... | collective-permute-start | bytes 786440 | tf_op jit(solution)/shard_map/ppermute | solution.py:352
  33.3 1.5 collective-permute-start.14
  34.8 14.3 %longitude_time.6 = (bf16[128,1024]{1,0:T(8,128)(2,1)S(1)}, bf16[128,1024]{1,0:T(8,128)(2,1)}, bf16[128,1024]{1,0:T(8,128)(2,1)S(1)}, bf16[128,1024]{1,0:T(8,128)(2,1)}) custom-call(s32[1]{0:T(128)} %bitcast.south_ref, bf16[16,256,4096]{2,1,0:T(8,128)(2,1)} %frames_ref.7, bf16[512,2048]{1,0:T(8,128)(2,1)S(1)} %copy-done.1, bf16[512,2048]{1,0:T(8,128)(2,1)S(1)} %copy-done, ...), custom_call_target="tpu_custom_call" | custom-call | flops 5368709120 | bytes 12582912 | tf_op jit(solution)/shard_map/longitude_time/pallas_call | solution.py:87
  49.7 14.2 %longitude_time.4 = (bf16[128,1024]{1,0:T(8,128)(2,1)S(1)}, bf16[128,1024]{1,0:T(8,128)(2,1)}, bf16[128,1024]{1,0:T(8,128)(2,1)S(1)}, bf16[128,1024]{1,0:T(8,128)(2,1)S(1)}) custom-call(s32[1]{0:T(128)} %bitcast.south_ref, bf16[16,256,4096]{2,1,0:T(8,128)(2,1)} %frames_ref.7, bf16[512,2048]{1,0:T(8,128)(2,1)S(1)} %copy-done.1, ...), custom_call_target="tpu_custom_call" | custom-call | flops 5368709120 | bytes 12582912 | tf_op jit(solution)/shard_map/longitude_time/pallas_call | solution.py:87
  64.6 1.9 collective-permute-start
  70.9 1.6 copy-done.2
  72.5 13.6 %longitude_time.5 = (bf16[128,1024]{1,0:T(8,128)(2,1)S(1)}, bf16[128,1024]{1,0:T(8,128)(2,1)S(1)}, bf16[128,1024]{1,0:T(8,128)(2,1)S(1)}, bf16[128,1024]{1,0:T(8,128)(2,1)S(1)}) custom-call(s32[1]{0:T(128)} %bitcast.south_ref, bf16[16,256,4096]{2,1,0:T(8,128)(2,1)} %frames_ref.7, bf16[512,2048]{1,0:T(8,128)(2,1)S(1)} %copy-done.2, ...), custom_call_target="tpu_custom_call" | custom-call | flops 5368709120 | bytes 12582912 | tf_op jit(solution)/shard_map/longitude_time/pallas_call | solution.py:87
  93.1 0.9 select_reduce_fusion
  95.5 12.2 %legendre.1 = (bf16[4,8192,256]{2,1,0:T(8,128)(2,1)}, bf16[4,6144,128]{2,1,0:T(8,128)(2,1)}) custom-call(s32[2,8,128]{2,1,0:T(8,128)S(1)} %broadcast_in_dim.41.order_ref, f32[8,1024]{1,0:T(8,128)S(1)} %get-tuple-element.55.rise_a, f32[8,1024]{1,0:T(8,128)S(1)} %get-tuple-element.54.fall_a, f32[8,1024]{1,0:T(8,128)S(1)} %get-tuple-element.56.rise_b, ...), custom_call_target="tpu_custom_call" | custom-call | flops 2000000000 | bytes 25165824 | tf_op jit(solution)/shard_map/legendre/pallas_call | solution.py:216
  107.7 1.5 collective-permute-start.2
  109.3 0.9 add_convert_fusion.4
  110.8 0.9 add_convert_fusion.1
  111.9 1.6 add_convert_fusion.10
  113.5 2.0 collective-permute-start.13
  115.5 1.6 add_convert_fusion.7
  117.1 1.5 collective-permute-start.15
  118.6 1.6 add_convert_fusion.22
  120.9 1.2 collective-permute-done.6
  122.1 2.1 collective-permute-start.1
  125.4 1.0 fusion.7
  126.4 1.7 collective-permute-start.5
  128.0 1.0 fusion.8
  129.7 4.9 %all-to-all-start.3 = ((bf16[8,16,1024]{2,1,0:T(8,128)(2,1)}), bf16[8,16,1024]{2,1,0:T(8,128)(2,1)S(1)}, u32[]{:S(2)}, u32[]{:S(2)}) async-start(bf16[8,16,1024]{2,1,0:T(8,128)(2,1)} %pad_maximum_fusion.3), calls=%async_computation.3 | async-start | bytes 524288 | tf_op jit(solution)/shard_map/all_to_all | solution.py:441
  134.6 2.0 collective-permute-start.7
  136.6 1.0 fusion.5
  137.6 1.0 fusion.6
  139.4 4.9 %all-to-all-done.3.z_ref = bf16[8,16,1024]{2,1,0:T(8,128)(2,1)S(1)} async-done(((bf16[8,16,1024]{2,1,0:T(8,128)(2,1)}), bf16[8,16,1024]{2,1,0:T(8,128)(2,1)S(1)}, u32[]{:S(2)}, u32[]{:S(2)}) %all-to-all-start.3) | async-done | bytes 262176 | tf_op jit(solution)/shard_map/all_to_all | solution.py:441
  144.3 3.4 %all-to-all-start.2 = ((bf16[8,16,1024]{2,1,0:T(8,128)(2,1)}), bf16[8,16,1024]{2,1,0:T(8,128)(2,1)S(1)}, u32[]{:S(2)}, u32[]{:S(2)}) async-start(bf16[8,16,1024]{2,1,0:T(8,128)(2,1)} %pad_maximum_fusion.2), calls=%async_computation.2 | async-start | bytes 524288 | tf_op jit(solution)/shard_map/all_to_all | solution.py:441
  147.8 1.0 fusion.4
  149.5 7.9 %all-to-all-done.2.z_ref = bf16[8,16,1024]{2,1,0:T(8,128)(2,1)S(1)} async-done(((bf16[8,16,1024]{2,1,0:T(8,128)(2,1)}), bf16[8,16,1024]{2,1,0:T(8,128)(2,1)S(1)}, u32[]{:S(2)}, u32[]{:S(2)}) %all-to-all-start.2) | async-done | bytes 262176 | tf_op jit(solution)/shard_map/all_to_all | solution.py:441
  157.4 3.4 %all-to-all-start.1 = ((bf16[8,16,1024]{2,1,0:T(8,128)(2,1)}), bf16[8,16,1024]{2,1,0:T(8,128)(2,1)S(1)}, u32[]{:S(2)}, u32[]{:S(2)}) async-start(bf16[8,16,1024]{2,1,0:T(8,128)(2,1)} %pad_maximum_fusion.1), calls=%async_computation.1 | async-start | bytes 524288 | tf_op jit(solution)/shard_map/all_to_all | solution.py:441
  160.8 1.0 fusion.1
  162.6 7.9 %all-to-all-done.1.z_ref = bf16[8,16,1024]{2,1,0:T(8,128)(2,1)S(1)} async-done(((bf16[8,16,1024]{2,1,0:T(8,128)(2,1)}), bf16[8,16,1024]{2,1,0:T(8,128)(2,1)S(1)}, u32[]{:S(2)}, u32[]{:S(2)}) %all-to-all-start.1) | async-done | bytes 262176 | tf_op jit(solution)/shard_map/all_to_all | solution.py:441
  170.5 3.4 %all-to-all-start = ((bf16[8,16,1024]{2,1,0:T(8,128)(2,1)}), bf16[8,16,1024]{2,1,0:T(8,128)(2,1)S(1)}, u32[]{:S(2)}, u32[]{:S(2)}) async-start(bf16[8,16,1024]{2,1,0:T(8,128)(2,1)} %pad_maximum_fusion), calls=%async_computation | async-start | bytes 524288 | tf_op jit(solution)/shard_map/all_to_all | solution.py:441
  173.9 8.2 %latitude_sum.4.refs_0_ = f32[1024,256]{1,0:T(8,128)S(1)} custom-call(bf16[8,16,1024]{2,1,0:T(8,128)(2,1)S(1)} %all-to-all-done.3.z_ref, f32[2,2,16,128]{3,2,1,0:T(8,128)S(1)} %add_convert_fusion.24.mask_ref, bf16[4,8192,256]{2,1,0:T(8,128)(2,1)} %get-tuple-element.27.p_a, bf16[4,6144,128]{2,1,0:T(8,128)(2,1)} %get-tuple-element.28.p_b), custom_call_target="tpu_custom_call" | custom-call | flops 1610612736 | bytes 8388608 | tf_op jit(solution)/shard_map/latitude_sum/pallas_call | solution.py:322
  182.2 8.3 %latitude_sum.5.refs_0_ = f32[1024,256]{1,0:T(8,128)S(1)} custom-call(bf16[8,16,1024]{2,1,0:T(8,128)(2,1)S(1)} %all-to-all-done.2.z_ref, f32[2,2,16,128]{3,2,1,0:T(8,128)S(1)} %add_convert_fusion.24.mask_ref, bf16[4,8192,256]{2,1,0:T(8,128)(2,1)} %get-tuple-element.27.p_a, bf16[4,6144,128]{2,1,0:T(8,128)(2,1)} %get-tuple-element.28.p_b, ...), custom_call_target="tpu_custom_call" | custom-call | flops 1610612736 | bytes 8388608 | tf_op jit(solution)/shard_map/latitude_sum/pallas_call | solution.py:322
  190.5 8.3 %latitude_sum.6.refs_0_ = f32[1024,256]{1,0:T(8,128)S(1)} custom-call(bf16[8,16,1024]{2,1,0:T(8,128)(2,1)S(1)} %all-to-all-done.1.z_ref, f32[2,2,16,128]{3,2,1,0:T(8,128)S(1)} %add_convert_fusion.24.mask_ref, bf16[4,8192,256]{2,1,0:T(8,128)(2,1)} %get-tuple-element.27.p_a, bf16[4,6144,128]{2,1,0:T(8,128)(2,1)} %get-tuple-element.28.p_b, ...), custom_call_target="tpu_custom_call" | custom-call | flops 1610612736 | bytes 8388608 | tf_op jit(solution)/shard_map/latitude_sum/pallas_call | solution.py:322
  198.8 9.7 %latitude_sum.7 = bf16[4,256,256]{2,1,0:T(8,128)(2,1)} custom-call(bf16[8,16,1024]{2,1,0:T(8,128)(2,1)S(1)} %all-to-all-done.z_ref, f32[2,2,16,128]{3,2,1,0:T(8,128)S(1)} %add_convert_fusion.24.mask_ref, bf16[4,8192,256]{2,1,0:T(8,128)(2,1)} %get-tuple-element.27.p_a, bf16[4,6144,128]{2,1,0:T(8,128)(2,1)} %get-tuple-element.28.p_b, ...), custom_call_target="tpu_custom_call" | custom-call | flops 1610612736 | bytes 8388608 | tf_op jit(solution)/shard_map/latitude_sum/pallas_call | solution.py:322
  208.5 3.5 %all-to-all-start.4 = ((bf16[4,256,256]{2,1,0:T(8,128)(2,1)}), bf16[4,256,256]{2,1,0:T(8,128)(2,1)S(1)}, u32[]{:S(2)}, u32[]{:S(2)}) async-start(bf16[4,256,256]{2,1,0:T(8,128)(2,1)} %latitude_sum.7), calls=%async_computation.4 | async-start | bytes 1048576 | tf_op jit(solution)/shard_map/all_to_all | solution.py:449
  212.1 8.9 %all-to-all-done.4 = bf16[4,256,256]{2,1,0:T(8,128)(2,1)S(1)} async-done(((bf16[4,256,256]{2,1,0:T(8,128)(2,1)}), bf16[4,256,256]{2,1,0:T(8,128)(2,1)S(1)}, u32[]{:S(2)}, u32[]{:S(2)}) %all-to-all-start.4) | async-done | bytes 524320 | tf_op jit(solution)/shard_map/all_to_all | solution.py:449
  221.2 1.1 copy.23
  (137 shorter events, 25.0 us)
Async XLA Ops:
  0.0 13.0 %copy-start = (bf16[512,2048]{1,0:T(8,128)(2,1)S(1)}, bf16[512,2048]{1,0:T(8,128)(2,1)}, u32[]{:S(2)}) copy-start(bf16[512,2048]{1,0:T(8,128)(2,1)} %constant.137.clone.odd_ref) | copy-start | bytes 6291460
  3.2 1.5 copy-start.22
  13.0 1.6 copy-start.1
  28.9 0.7 copy-start.9
  29.6 0.7 copy-start.13
  30.3 77.4 %collective-permute-start.12 = (bf16[128,1024]{1,0:T(8,128)(2,1)}, bf16[128,1024]{1,0:T(8,128)(2,1)}, u32[]{:S(2)}, u32[]{:S(2)}) collective-permute-start(bf16[128,1024]{1,0:T(8,128)(2,1)} %get-tuple-element.38), channel_id=1, source_target_pairs={{0,8},{8,0},{16,24},{24,16},{1,9},{9,1},{17,25},{25,17},{2,10},{10... | collective-permute-start | bytes 786440 | tf_op jit(solution)/shard_map/ppermute | solution.py:352
  33.3 76.9 %collective-permute-start.14 = (bf16[128,1024]{1,0:T(8,128)(2,1)}, bf16[128,1024]{1,0:T(8,128)(2,1)}, u32[]{:S(2)}, u32[]{:S(2)}) collective-permute-start(bf16[128,1024]{1,0:T(8,128)(2,1)} %get-tuple-element.40), channel_id=1, source_target_pairs={{0,16},{8,24},{16,0},{24,8},{1,17},{9,25},{17,1},{25,9},{2,18},{10... | collective-permute-start | bytes 786440 | tf_op jit(solution)/shard_map/ppermute | solution.py:352
  49.1 14.9 %copy-start.3 = (bf16[128,1024]{1,0:T(8,128)(2,1)}, bf16[128,1024]{1,0:T(8,128)(2,1)S(1)}, u32[]{:S(2)}) copy-start(bf16[128,1024]{1,0:T(8,128)(2,1)S(1)} %get-tuple-element.35) | copy-start | bytes 786436
  49.1 14.9 %copy-start.5 = (bf16[128,1024]{1,0:T(8,128)(2,1)}, bf16[128,1024]{1,0:T(8,128)(2,1)S(1)}, u32[]{:S(2)}) copy-start(bf16[128,1024]{1,0:T(8,128)(2,1)S(1)} %get-tuple-element.33) | copy-start | bytes 786436
  49.1 62.7 %collective-permute-start.8 = (bf16[128,1024]{1,0:T(8,128)(2,1)}, bf16[128,1024]{1,0:T(8,128)(2,1)}, u32[]{:S(2)}, u32[]{:S(2)}) collective-permute-start(bf16[128,1024]{1,0:T(8,128)(2,1)} %get-tuple-element.34), channel_id=1, source_target_pairs={{0,8},{8,0},{16,24},{24,16},{1,9},{9,1},{17,25},{25,17},{2,10},{10... | collective-permute-start | bytes 786440 | tf_op jit(solution)/shard_map/ppermute | solution.py:352
  49.6 63.9 %collective-permute-start.10 = (bf16[128,1024]{1,0:T(8,128)(2,1)}, bf16[128,1024]{1,0:T(8,128)(2,1)}, u32[]{:S(2)}, u32[]{:S(2)}) collective-permute-start(bf16[128,1024]{1,0:T(8,128)(2,1)} %get-tuple-element.36), channel_id=1, source_target_pairs={{0,16},{8,24},{16,0},{24,8},{1,17},{9,25},{17,1},{25,9},{2,18},{10... | collective-permute-start | bytes 786440 | tf_op jit(solution)/shard_map/ppermute | solution.py:352
  63.9 0.7 copy-start.15
  64.6 52.4 %collective-permute-start = (bf16[128,1024]{1,0:T(8,128)(2,1)}, bf16[128,1024]{1,0:T(8,128)(2,1)}, u32[]{:S(2)}, u32[]{:S(2)}) collective-permute-start(bf16[128,1024]{1,0:T(8,128)(2,1)} %get-tuple-element.24), channel_id=1, source_target_pairs={{0,8},{8,0},{16,24},{24,16},{1,9},{9,1},{17,25},{25,17},{2,10},{10... | collective-permute-start | bytes 786440 | tf_op jit(solution)/shard_map/ppermute | solution.py:352
  70.9 1.6 copy-start.2
  86.2 0.7 copy-start.7
  86.9 0.7 copy-start.11
  87.6 0.7 copy-start.17
  88.3 0.7 copy-start.19
  89.0 18.7 %copy-start.16 = (bf16[128,1024]{1,0:T(8,128)(2,1)S(1)}, bf16[128,1024]{1,0:T(8,128)(2,1)}, u32[]{:S(2)}) copy-start(bf16[128,1024]{1,0:T(8,128)(2,1)} %copy-done.15) | copy-start | bytes 786436
  89.0 20.3 %copy-start.14 = (bf16[128,1024]{1,0:T(8,128)(2,1)S(1)}, bf16[128,1024]{1,0:T(8,128)(2,1)}, u32[]{:S(2)}) copy-start(bf16[128,1024]{1,0:T(8,128)(2,1)} %copy-done.13) | copy-start | bytes 786436
  89.0 21.8 %copy-start.10 = (bf16[128,1024]{1,0:T(8,128)(2,1)S(1)}, bf16[128,1024]{1,0:T(8,128)(2,1)}, u32[]{:S(2)}) copy-start(bf16[128,1024]{1,0:T(8,128)(2,1)} %copy-done.9) | copy-start | bytes 786436
  89.0 22.9 %copy-start.6 = (bf16[128,1024]{1,0:T(8,128)(2,1)S(1)}, bf16[128,1024]{1,0:T(8,128)(2,1)}, u32[]{:S(2)}) copy-start(bf16[128,1024]{1,0:T(8,128)(2,1)} %copy-done.5) | copy-start | bytes 786436
  89.0 26.5 %copy-start.4 = (bf16[128,1024]{1,0:T(8,128)(2,1)S(1)}, bf16[128,1024]{1,0:T(8,128)(2,1)}, u32[]{:S(2)}) copy-start(bf16[128,1024]{1,0:T(8,128)(2,1)} %copy-done.3) | copy-start | bytes 786436
  89.0 21.2 %copy-start.20 = (bf16[128,1024]{1,0:T(8,128)(2,1)S(1)}, bf16[128,1024]{1,0:T(8,128)(2,1)}, u32[]{:S(2)}) copy-start(bf16[128,1024]{1,0:T(8,128)(2,1)} %copy-done.19) | copy-start | bytes 786436
  89.0 22.8 %copy-start.18 = (bf16[128,1024]{1,0:T(8,128)(2,1)S(1)}, bf16[128,1024]{1,0:T(8,128)(2,1)}, u32[]{:S(2)}) copy-start(bf16[128,1024]{1,0:T(8,128)(2,1)} %copy-done.17) | copy-start | bytes 786436
  89.0 31.8 %copy-start.12 = (bf16[128,1024]{1,0:T(8,128)(2,1)S(1)}, bf16[128,1024]{1,0:T(8,128)(2,1)}, u32[]{:S(2)}) copy-start(bf16[128,1024]{1,0:T(8,128)(2,1)} %copy-done.11) | copy-start | bytes 786436
  89.0 35.1 %copy-start.8 = (bf16[128,1024]{1,0:T(8,128)(2,1)S(1)}, bf16[128,1024]{1,0:T(8,128)(2,1)}, u32[]{:S(2)}) copy-start(bf16[128,1024]{1,0:T(8,128)(2,1)} %copy-done.7) | copy-start | bytes 786436
  107.7 12.4 %collective-permute-start.2 = (bf16[128,1024]{1,0:T(8,128)(2,1)S(1)}, bf16[128,1024]{1,0:T(8,128)(2,1)S(1)}, u32[]{:S(2)}, u32[]{:S(2)}) collective-permute-start(bf16[128,1024]{1,0:T(8,128)(2,1)S(1)} %copy-done.16), channel_id=1, source_target_pairs={{0,16},{8,24},{16,0},{24,8},{1,17},{9,25},{17,1},{25,9},{2,18},{10... | collective-permute-start | bytes 786440 | tf_op jit(solution)/shard_map/ppermute | solution.py:352
  110.2 10.5 %collective-permute-start.4 = (bf16[128,1024]{1,0:T(8,128)(2,1)S(1)}, bf16[128,1024]{1,0:T(8,128)(2,1)S(1)}, u32[]{:S(2)}, u32[]{:S(2)}) collective-permute-start(bf16[128,1024]{1,0:T(8,128)(2,1)S(1)} %copy-done.20), channel_id=1, source_target_pairs={{0,8},{8,0},{16,24},{24,16},{1,9},{9,1},{17,25},{25,17},{2,10},{10... | collective-permute-start | bytes 786440 | tf_op jit(solution)/shard_map/ppermute | solution.py:352
  111.8 10.3 %collective-permute-start.6 = (bf16[128,1024]{1,0:T(8,128)(2,1)S(1)}, bf16[128,1024]{1,0:T(8,128)(2,1)S(1)}, u32[]{:S(2)}, u32[]{:S(2)}) collective-permute-start(bf16[128,1024]{1,0:T(8,128)(2,1)S(1)} %copy-done.18), channel_id=1, source_target_pairs={{0,16},{8,24},{16,0},{24,8},{1,17},{9,25},{17,1},{25,9},{2,18},{10... | collective-permute-start | bytes 786440 | tf_op jit(solution)/shard_map/ppermute | solution.py:352
  113.5 11.4 %collective-permute-start.13 = (bf16[64,1024]{1,0:T(8,128)(2,1)S(1)}, bf16[64,1024]{1,0:T(8,128)(2,1)S(1)}, u32[]{:S(2)}, u32[]{:S(2)}) collective-permute-start(bf16[64,1024]{1,0:T(8,128)(2,1)S(1)} %add_convert_fusion.4), channel_id=1, source_target_pairs={{0,16},{8,24},{16,0},{24,8},{1,17},{9,25},{17,1},{25,9},{2,18},{10... | collective-permute-start | bytes 393224 | tf_op jit(solution)/shard_map/ppermute | solution.py:352
  117.1 9.3 %collective-permute-start.15 = (bf16[64,1024]{1,0:T(8,128)(2,1)S(1)}, bf16[64,1024]{1,0:T(8,128)(2,1)S(1)}, u32[]{:S(2)}, u32[]{:S(2)}) collective-permute-start(bf16[64,1024]{1,0:T(8,128)(2,1)S(1)} %add_convert_fusion.1), channel_id=1, source_target_pairs={{0,8},{8,0},{16,24},{24,16},{1,9},{9,1},{17,25},{25,17},{2,10},{10... | collective-permute-start | bytes 393224 | tf_op jit(solution)/shard_map/ppermute | solution.py:352
  120.1 14.4 %collective-permute-start.9 = (bf16[64,1024]{1,0:T(8,128)(2,1)}, bf16[64,1024]{1,0:T(8,128)(2,1)}, u32[]{:S(2)}, u32[]{:S(2)}) collective-permute-start(bf16[64,1024]{1,0:T(8,128)(2,1)} %add_convert_fusion.10), channel_id=1, source_target_pairs={{0,16},{8,24},{16,0},{24,8},{1,17},{9,25},{17,1},{25,9},{2,18},{10... | collective-permute-start | bytes 393224 | tf_op jit(solution)/shard_map/ppermute | solution.py:352
  120.7 16.9 %collective-permute-start.11 = (bf16[64,1024]{1,0:T(8,128)(2,1)}, bf16[64,1024]{1,0:T(8,128)(2,1)}, u32[]{:S(2)}, u32[]{:S(2)}) collective-permute-start(bf16[64,1024]{1,0:T(8,128)(2,1)} %add_convert_fusion.7), channel_id=1, source_target_pairs={{0,8},{8,0},{16,24},{24,16},{1,9},{9,1},{17,25},{25,17},{2,10},{10... | collective-permute-start | bytes 393224 | tf_op jit(solution)/shard_map/ppermute | solution.py:352
  122.0 6.9 %copy-start.21 = (bf16[128,1024]{1,0:T(8,128)(2,1)}, bf16[128,1024]{1,0:T(8,128)(2,1)S(1)}, u32[]{:S(2)}) copy-start(bf16[128,1024]{1,0:T(8,128)(2,1)S(1)} %collective-permute-done.6) | copy-start | bytes 786436
  122.1 38.8 %collective-permute-start.1 = (bf16[64,1024]{1,0:T(8,128)(2,1)}, bf16[64,1024]{1,0:T(8,128)(2,1)S(1)}, u32[]{:S(2)}, u32[]{:S(2)}) collective-permute-start(bf16[64,1024]{1,0:T(8,128)(2,1)} %add_convert_fusion.22), channel_id=1, source_target_pairs={{0,16},{8,24},{16,0},{24,8},{1,17},{9,25},{17,1},{25,9},{2,18},{10... | collective-permute-start | bytes 393224 | tf_op jit(solution)/shard_map/ppermute | solution.py:352
  124.9 36.9 %collective-permute-start.3 = (bf16[64,1024]{1,0:T(8,128)(2,1)S(1)}, bf16[64,1024]{1,0:T(8,128)(2,1)S(1)}, u32[]{:S(2)}, u32[]{:S(2)}) collective-permute-start(bf16[64,1024]{1,0:T(8,128)(2,1)S(1)} %add_convert_fusion.19), channel_id=1, source_target_pairs={{0,8},{8,0},{16,24},{24,16},{1,9},{9,1},{17,25},{25,17},{2,10},{10... | collective-permute-start | bytes 393224 | tf_op jit(solution)/shard_map/ppermute | solution.py:352
  126.4 21.4 %collective-permute-start.5 = (bf16[64,1024]{1,0:T(8,128)(2,1)S(1)}, bf16[64,1024]{1,0:T(8,128)(2,1)S(1)}, u32[]{:S(2)}, u32[]{:S(2)}) collective-permute-start(bf16[64,1024]{1,0:T(8,128)(2,1)S(1)} %add_convert_fusion.16), channel_id=1, source_target_pairs={{0,16},{8,24},{16,0},{24,8},{1,17},{9,25},{17,1},{25,9},{2,18},{10... | collective-permute-start | bytes 393224 | tf_op jit(solution)/shard_map/ppermute | solution.py:352
  129.7 14.6 %all-to-all-start.3 = ((bf16[8,16,1024]{2,1,0:T(8,128)(2,1)}), bf16[8,16,1024]{2,1,0:T(8,128)(2,1)S(1)}, u32[]{:S(2)}, u32[]{:S(2)}) async-start(bf16[8,16,1024]{2,1,0:T(8,128)(2,1)} %pad_maximum_fusion.3), calls=%async_computation.3 | async-start | bytes 524288 | tf_op jit(solution)/shard_map/all_to_all | solution.py:441
  134.6 13.2 %collective-permute-start.7 = (bf16[64,1024]{1,0:T(8,128)(2,1)S(1)}, bf16[64,1024]{1,0:T(8,128)(2,1)S(1)}, u32[]{:S(2)}, u32[]{:S(2)}) collective-permute-start(bf16[64,1024]{1,0:T(8,128)(2,1)S(1)} %add_convert_fusion.13), channel_id=1, source_target_pairs={{0,8},{8,0},{16,24},{24,16},{1,9},{9,1},{17,25},{25,17},{2,10},{10... | collective-permute-start | bytes 393224 | tf_op jit(solution)/shard_map/ppermute | solution.py:352
  144.3 13.1 %all-to-all-start.2 = ((bf16[8,16,1024]{2,1,0:T(8,128)(2,1)}), bf16[8,16,1024]{2,1,0:T(8,128)(2,1)S(1)}, u32[]{:S(2)}, u32[]{:S(2)}) async-start(bf16[8,16,1024]{2,1,0:T(8,128)(2,1)} %pad_maximum_fusion.2), calls=%async_computation.2 | async-start | bytes 524288 | tf_op jit(solution)/shard_map/all_to_all | solution.py:441
  157.4 13.1 %all-to-all-start.1 = ((bf16[8,16,1024]{2,1,0:T(8,128)(2,1)}), bf16[8,16,1024]{2,1,0:T(8,128)(2,1)S(1)}, u32[]{:S(2)}, u32[]{:S(2)}) async-start(bf16[8,16,1024]{2,1,0:T(8,128)(2,1)} %pad_maximum_fusion.1), calls=%async_computation.1 | async-start | bytes 524288 | tf_op jit(solution)/shard_map/all_to_all | solution.py:441
  170.5 28.3 %all-to-all-start = ((bf16[8,16,1024]{2,1,0:T(8,128)(2,1)}), bf16[8,16,1024]{2,1,0:T(8,128)(2,1)S(1)}, u32[]{:S(2)}, u32[]{:S(2)}) async-start(bf16[8,16,1024]{2,1,0:T(8,128)(2,1)} %pad_maximum_fusion), calls=%async_computation | async-start | bytes 524288 | tf_op jit(solution)/shard_map/all_to_all | solution.py:441
  208.5 12.5 %all-to-all-start.4 = ((bf16[4,256,256]{2,1,0:T(8,128)(2,1)}), bf16[4,256,256]{2,1,0:T(8,128)(2,1)S(1)}, u32[]{:S(2)}, u32[]{:S(2)}) async-start(bf16[4,256,256]{2,1,0:T(8,128)(2,1)} %latitude_sum.7), calls=%async_computation.4 | async-start | bytes 1048576 | tf_op jit(solution)/shard_map/all_to_all | solution.py:449

commit v2 on v0

v2 whole, which is shorter than its diff:
```python
from functools import partial
import math

import jax
import jax.numpy as jnp
import numpy as np
from jax import lax
from jax.experimental import pallas as pl
from jax.experimental.pallas import tpu as pltpu
from jax.sharding import PartitionSpec as P

L = 1024
F = 8
EF = 2 * F
ROWS = 16
WIDE = ROWS * EF
QUARTERS = (2, 2)
GROUP = 8
SPAN = 128
SPAN_OUT = 256
VMEM = 24 * 1024 * 1024
VMEM_LEGENDRE = 8 * 1024 * 1024
VMEM_SUM = 24 * 1024 * 1024


def longitude_tables(nlon, order_count):
    factor = np.float32(math.sqrt(2.0 / nlon))
    tables = []
    for first, stride, length in ((0, 4, nlon // 4), (2, 4, nlon // 4), (1, 2, nlon // 2)):
        points = np.arange(length, dtype=np.int64)[:, None]
        orders = np.arange(first, order_count, stride, dtype=np.int64)[None, :]
        angles = (orders * points % nlon).astype(np.float32) * np.float32(2.0 * math.pi / nlon)
        parts = [np.cos(angles) * factor, -np.sin(angles) * factor]
        tables.append(np.concatenate(parts, axis=1).astype(jnp.bfloat16))
    return tables


def table_column(orders, order_count):
    quarter = orders // 4 + orders % 4 // 2 * (order_count // 4)
    return jnp.where(orders % 2 == 1, order_count // 2 + orders // 2, quarter)


def time_matrices(frame_count, time_count):
    total = frame_count * time_count
    frames_at = np.arange(total, dtype=np.int64)
    frequency = total // 8 + np.arange(F, dtype=np.int64)
    phases = frequency[:, None] * frames_at[None, :] % total
    angles = phases.astype(np.float32) * np.float32(2.0 * math.pi / total)
    factor = np.float32(1.0 / math.sqrt(total))
    cos_part, sin_part = np.cos(angles) * factor, np.sin(angles) * factor
    weights = np.stack(
        [np.concatenate([cos_part, -sin_part]), np.concatenate([sin_part, cos_part])]
    )
    weights = weights.reshape(2, EF, time_count, frame_count).transpose(2, 0, 1, 3)
    same = np.stack([np.eye(ROWS), np.eye(ROWS)[::-1]]).astype(np.float32)
    full = weights[:, None, :, None, :, :, None] * same[None, :, None, :, None, None, :]
    return full.reshape(time_count, 2, 2, WIDE, frame_count * ROWS).astype(jnp.bfloat16)


SHORT = pl.CostEstimate(flops=10**6, bytes_accessed=10**5, transcendentals=0)


def product(a, b):
    return jnp.dot(a, b, preferred_element_type=jnp.float32)


def transform_kernel(where_ref, frames_ref, fours_ref, twos_ref, odd_ref, time_ref, place_ref, *refs):
    frame_count, rows, nlon = frames_ref.shape
    outs, (sum_s, diff_s, odd_s) = refs[:4], refs[4:]
    half, quarter = nlon // 2, nlon // 4
    count = rows // ROWS
    tall = frame_count * ROWS
    for i in range(count):
        at = slice(i * tall, (i + 1) * tall)
        first = jnp.where(where_ref[0] == 1, count - 1 - i, i) * ROWS
        image = frames_ref[:, pl.ds(pl.multiple_of(first, ROWS), ROWS), :].reshape(tall, nlon)
        near, far = image[:, :half], image[:, half:]
        even = near + far
        odd_s[at] = near - far
        sum_s[at] = even[:, :quarter] + even[:, quarter:]
        diff_s[at] = even[:, :quarter] - even[:, quarter:]
    coefs = [
        product(folded[...], table_ref[...]).astype(jnp.bfloat16)
        for folded, table_ref in ((sum_s, fours_ref), (diff_s, twos_ref), (odd_s, odd_ref))
    ]
    for i in range(count):
        bands = []
        for coef in coefs:
            coef = coef[i * tall : (i + 1) * tall]
            middle = coef.shape[1] // 2
            bands.append(
                product(time_ref[0, 0, 0], coef[:, :middle])
                + product(time_ref[0, 0, 1], coef[:, middle:])
            )
        band = jnp.concatenate(bands, axis=1).astype(jnp.bfloat16)
        placed = lax.dot_general(
            place_ref[...], band, (((1,), (1,)), ((), ())), preferred_element_type=jnp.float32
        ).astype(jnp.bfloat16)
        size = outs[0].shape[0]
        for n, out in enumerate(outs):
            out[:, i * WIDE : (i + 1) * WIDE] = placed[n * size : (n + 1) * size]


def transform_chunk(part, where, frames, tables, time_mats, place):
    frame_count, row_count, nlon = frames.shape
    first, blocks = part
    together = 2 if first % 2 == 0 and blocks % 2 == 0 else 1
    rows = together * ROWS
    steps, first, all_steps = blocks // together, first // together, row_count // rows
    order_count = place.shape[0]
    size = order_count // 4

    def frame_block(b, where_ref):
        at = first + b
        return (0, jnp.where(where_ref[0] == 1, all_steps - 1 - at, at), 0)

    def time_block(b, where_ref):
        return (where_ref[1], where_ref[0], 0, 0, 0)

    out = pltpu.HBM((size, blocks * WIDE), jnp.bfloat16)
    tall = frame_count * rows
    flops = 2 * steps * tall * order_count * (3 * nlon // 4 + 2 * WIDE + order_count)
    in_vmem = pl.BlockSpec(memory_space=pltpu.VMEM)
    return pl.pallas_call(
        transform_kernel,
        grid_spec=pltpu.PrefetchScalarGridSpec(
            num_scalar_prefetch=1,
            grid=(steps,),
            in_specs=[
                pl.BlockSpec((frame_count, rows, nlon), frame_block),
                *([in_vmem] * len(tables)),
                pl.BlockSpec((1, 1) + time_mats.shape[2:], time_block),
                in_vmem,
            ],
            out_specs=[pl.BlockSpec((size, rows * EF), lambda b, w: (0, b))] * 4,
            scratch_shapes=[
                pltpu.VMEM((tall, nlon // 4), jnp.bfloat16),
                pltpu.VMEM((tall, nlon // 4), jnp.bfloat16),
                pltpu.VMEM((tall, nlon // 2), jnp.bfloat16),
            ],
        ),
        out_shape=[out] * 4,
        compiler_params=pltpu.CompilerParams(vmem_limit_bytes=VMEM),
        cost_estimate=SHORT,
        name="longitude_time",
    )(where, frames, *tables, pltpu.with_memory_space_constraint(time_mats, pltpu.HBM), place)


def degree_factors(orders, level):
    level_sq = level * level
    order_sq = orders * orders
    lower = level - 1.0
    rising = jnp.sqrt(
        jnp.maximum(4.0 * level_sq - 1.0, 0.0) / jnp.maximum(level_sq - order_sq, 1.0)
    )
    falling = jnp.sqrt(
        jnp.maximum(lower * lower - order_sq, 0.0) / jnp.maximum(4.0 * lower * lower - 1.0, 1.0)
    )
    return rising, rising * falling


def polynomial_kernel(half, begin, orders_ref, growth_ref, rows_ref, out, token, state):
    step = pl.program_id(0)
    base = begin + step * SPAN
    order_count = growth_ref.shape[1]

    def spread(row):
        return jnp.broadcast_to(row, (GROUP, row.shape[1]))

    @pl.when(step == 0)
    def _():
        steps_k = lax.broadcasted_iota(jnp.int32, (GROUP, order_count), 1).astype(jnp.float32) + 1.0
        order = orders_ref[:, :1]
        growth = jnp.sum(
            jnp.where(steps_k <= order, spread(growth_ref[...]), 0.0), axis=1, keepdims=True
        )
        lognorm = 0.5 * math.log(0.5) + 0.5 * growth + order * spread(rows_ref[1:2])
        start = jnp.where(lognorm >= -60.0, jnp.exp(jnp.maximum(lognorm, -60.0)), 0.0)
        token[...] = jnp.zeros_like(token)
        state[0] = jnp.zeros_like(start)
        state[1] = jnp.zeros_like(start)
        state[2] = start * spread(rows_ref[2:3])

    x = spread(rows_ref[0:1])

    def run(begins):
        level = (lax.broadcasted_iota(jnp.int32, (GROUP, SPAN), 1) + base).astype(jnp.float32)
        rise, fall = degree_factors(orders_ref[...], level)
        older, last = state[0], state[1]
        first = pl.multiple_of(step * SPAN * GROUP, SPAN * GROUP)
        for at in range(0, SPAN, 2):
            made = []
            for i in (at, at + 1):
                new = (rise[:, i : i + 1] * x) * last - fall[:, i : i + 1] * older
                if begins:
                    here = jnp.where(orders_ref[...] == (base + i).astype(jnp.float32), 1.0, 0.0)
                    new = new + here[:, :1] * state[2]
                older, last = last, new
                made.append(new)
            both = jnp.concatenate(made, axis=0).astype(jnp.bfloat16)
            out[pl.ds(first + GROUP * at, 2 * GROUP), :] = both
        state[0], state[1] = older, last

    @pl.when(step < half)
    def _():
        run(True)

    @pl.when(step >= half)
    def _():
        run(False)


def polynomials(orders, which, order_count, nlat, rows_each, parts):
    nlat_count = nlat * rows_each
    half = order_count // 2 // SPAN
    rows = np.arange(nlat_count // 2).reshape(nlat // 2, rows_each)[which * nlat // 4 :]
    rows = np.concatenate(
        [rows[:, at * ROWS : (at + count) * ROWS].reshape(-1) for at, count in parts]
    )
    begin = which * order_count // 2
    colatitude = (rows.astype(np.float32) + np.float32(0.5)) * np.float32(math.pi / nlat_count)
    sine = np.sin(colatitude)
    weight = sine * np.float32(math.pi / nlat_count) * np.float32(math.sqrt(nlat_count))
    row_values = np.stack([np.cos(colatitude), np.log(sine), weight])
    growth = np.log1p(np.float32(0.5) / np.arange(1, order_count + 1, dtype=np.float32))[None, :]
    orders = jnp.broadcast_to(orders.astype(jnp.float32)[:, None], (GROUP, 128))

    def fixed(shape):
        return pl.BlockSpec(shape, lambda s: (0,) * len(shape))

    return pl.pallas_call(
        partial(polynomial_kernel, half, begin),
        grid=((L - begin) // SPAN,),
        in_specs=[fixed(orders.shape), fixed(growth.shape), fixed(row_values.shape)],
        out_specs=[pl.BlockSpec(memory_space=pltpu.VMEM), fixed((GROUP, 128))],
        out_shape=[
            jax.ShapeDtypeStruct(((L - begin) * GROUP, rows.size), jnp.bfloat16),
            jax.ShapeDtypeStruct((GROUP, 128), jnp.float32),
        ],
        scratch_shapes=[pltpu.VMEM((3, GROUP, rows.size), jnp.float32)],
        compiler_params=pltpu.CompilerParams(vmem_limit_bytes=VMEM_LEGENDRE),
        cost_estimate=SHORT,
        name="legendre",
    )(orders, jnp.asarray(growth), jnp.asarray(row_values))


def swap_groups(x):
    sub = lax.broadcasted_iota(jnp.int32, x.shape, 1)
    lane = lax.broadcasted_iota(jnp.int32, x.shape, 2) // EF
    for bit in (1, 2, 4):
        down = pltpu.roll(pltpu.roll(x, 8 - bit, 1), EF * bit, 2)
        up = pltpu.roll(pltpu.roll(x, bit, 1), 128 - EF * bit, 2)
        sub_on, lane_on = (sub & bit) != 0, (lane & bit) != 0
        x = jnp.where(sub_on == lane_on, x, jnp.where(sub_on, up, down))
    return x


def contract_kernel(g, half, last, nlat, lanes_at, here_ref, *refs):
    z_refs, (parity_ref, p_ref), refs = refs[:nlat], refs[nlat : nlat + 2], refs[nlat + 2 :]
    acc_ref = refs[0] if len(refs) == 4 else None
    out_ref, z_all, w_ref = refs[-3:]
    step = pl.program_id(0)
    lanes = z_all.shape[2]
    span = out_ref.shape[-1] if last else out_ref.shape[0]

    @pl.when(step == 0)
    def _():
        for n, z_ref in enumerate(z_refs):
            z_all[n] = z_ref[...]

        def source(s):
            return z_all[s ^ here_ref[0]].astype(jnp.float32)[g * GROUP : (g + 1) * GROUP]

        for part, sign in ((0, 1.0), (1, -1.0)):
            pieces = []
            for s in range(g * nlat // 4, nlat // 2):
                both = source(s) + sign * source(nlat - 1 - s)
                pieces += [both[:, i : i + 128] for i in range(0, lanes, 128)]
            block = swap_groups(jnp.stack(pieces, axis=0))
            w_ref[:, part * 128 : (part + 1) * 128] = block.reshape(
                len(pieces) * GROUP, 128
            ).astype(jnp.bfloat16)

    sub = lax.broadcasted_iota(jnp.int32, (GROUP, 128), 0)
    lane = lax.broadcasted_iota(jnp.int32, (GROUP, 128), 1) // EF
    odd = [((parity_ref[...] + u) & 1) == 1 for u in range(2)]

    def own_columns(first):
        tile = 4 * GROUP * GROUP
        out = []
        for i in range(0, span * GROUP, tile):
            rows = p_ref[pl.ds(first + i, tile), lanes_at : lanes_at + w_ref.shape[0]]
            full = product(rows, w_ref[...]).reshape(4, GROUP, GROUP, 256)
            kept = None
            for n in range(GROUP):
                one = jnp.where(odd[n % 2], full[:, n, :, 128:], full[:, n, :, :128])
                if n == 0:
                    kept = one
                else:
                    kept = jnp.where(((sub - lane) & 7) == n, pltpu.roll(one, n, 1), kept)
            for bit in (1, 2, 4):
                kept = jnp.where((lane & bit) != 0, pltpu.roll(kept, GROUP - bit, 1), kept)
            out.append(kept.reshape(4 * GROUP, 128))
        return jnp.concatenate(out, axis=0)

    def run():
        value = own_columns(pl.multiple_of((step - half) * span * GROUP, 256))
        if acc_ref is not None:
            value = value + acc_ref[...]
        if last:
            out_ref[0] = value.T.astype(out_ref.dtype)
        else:
            out_ref[...] = value

    if half:

        @pl.when(step < half)
        def _():
            out_ref[...] = jnp.zeros_like(out_ref)

        pl.when(step >= half)(run)
    else:
        run()


def contract_chunk(g, last, here, z, parity, p, lanes_at, lanes, acc, begin, ntm):
    each = L // ntm
    span = min(SPAN_OUT, each)
    half = begin // span if last else 0
    if last:
        steps = L // span
        per = each // span
        out_shape = jax.ShapeDtypeStruct((ntm, 128, each), jnp.bfloat16)
        out_spec = pl.BlockSpec(
            (1, 128, span), lambda s, here_ref: ((s // per) ^ here_ref[1], 0, s % per)
        )
    else:
        steps = (L - begin) // span
        out_shape = jax.ShapeDtypeStruct((L - begin, 128), jnp.float32)
        out_spec = pl.BlockSpec((span, 128), lambda s, _: (s, 0))
    acc_spec = pl.BlockSpec((span, 128), lambda s, _: (jnp.maximum(s - half, 0), 0))
    return pl.pallas_call(
        partial(contract_kernel, g, half, last, len(z), lanes_at),
        grid_spec=pltpu.PrefetchScalarGridSpec(
            num_scalar_prefetch=1,
            grid=(steps,),
            in_specs=[pl.BlockSpec(x.shape, lambda s, _: (0, 0)) for x in z]
            + [pl.BlockSpec(parity.shape, lambda s, _: (0, 0))]
            + [pl.BlockSpec(memory_space=pltpu.VMEM)]
            + [acc_spec] * (acc is not None),
            out_specs=out_spec,
            scratch_shapes=[
                pltpu.VMEM((len(z),) + z[0].shape, jnp.bfloat16),
                pltpu.VMEM((lanes, 256), jnp.bfloat16),
            ],
        ),
        out_shape=out_shape,
        compiler_params=pltpu.CompilerParams(vmem_limit_bytes=VMEM_SUM),
        cost_estimate=SHORT,
        name="latitude_sum",
    )(here, *z, parity, p, *([acc] if acc is not None else []))


def arrange_kernel(owned, here_ref, orders_ref, *refs):
    out_ref = refs[-1]
    count = (len(refs) - 1) // 2
    for offset in range(count):
        source = offset ^ here_ref[1]
        low, high = (refs[g * count + offset][...].astype(jnp.float32) for g in range(2))
        for i in range(owned):
            first = orders_ref[((here_ref[0] * count + source) * owned + i) * 2]
            in_order = first < orders_ref.shape[0] // 2
            for e in range(2):
                a, b = low[i * EF + e * F :][:F], high[i * EF + e * F :][:F]
                slot = (source * owned + i) * 2
                out_ref[e, slot] = jnp.where(in_order, a, b)
                out_ref[e, slot + 1] = jnp.where(in_order, b, a)


def arrange(here, owner_map, low, high, owned):
    ntm, each = len(low), low[0].shape[1]
    return pl.pallas_call(
        partial(arrange_kernel, owned),
        grid_spec=pltpu.PrefetchScalarGridSpec(
            num_scalar_prefetch=2,
            grid=(1,),
            in_specs=[pl.BlockSpec((128, each), lambda s, h, f: (0, 0))] * (2 * ntm),
            out_specs=pl.BlockSpec((2, ntm * owned * 2, F, each), lambda s, h, f: (0, 0, 0, 0)),
        ),
        out_shape=jax.ShapeDtypeStruct((2, ntm * owned * 2, F, each), jnp.float32),
        name="slot_order",
    )(here, owner_map, *low, *high)


def swap_with(x, axis, offset):
    count = lax.axis_size(axis)
    return lax.ppermute(x, axis, [(i, i ^ offset) for i in range(count)])


def both_sums(keep_a, got_a, keep_b, got_b):
    return [
        k[...].astype(jnp.float32) + g[...].astype(jnp.float32)
        for k, g in ((keep_a, got_a), (keep_b, got_b))
    ]


def halve_kernel(keep_a, got_a, keep_b, got_b, *outs):
    outs = outs[-4:]
    for n, total in enumerate(both_sums(keep_a, got_a, keep_b, got_b)):
        middle = total.shape[0] // 2
        outs[2 * n][...] = total[:middle]
        outs[2 * n + 1][...] = total[middle:].astype(jnp.bfloat16)


def finish_kernel(keep_a, got_a, keep_b, got_b, *outs):
    total_a, total_b = both_sums(keep_a, got_a, keep_b, got_b)
    owned = total_a.shape[0] // len(outs)
    for n, out in enumerate(outs):
        at = slice(n * owned, (n + 1) * owned)
        out[...] = jnp.concatenate([total_a[at], total_b[at]], axis=0).astype(jnp.bfloat16)


def in_columns(kernel, name, arrays, out_rows, out_types, early=()):
    width = arrays[0].shape[1]
    lanes = min(2048, width)

    def spec(rows):
        return pl.BlockSpec((rows, lanes), lambda i: (0, i))

    return pl.pallas_call(
        kernel,
        grid=(width // lanes,),
        in_specs=[spec(x.shape[0]) for x in arrays]
        + [pl.BlockSpec(x.shape, lambda i: (0, 0)) for x in early],
        out_specs=[spec(rows) for rows in out_rows],
        out_shape=[
            jax.ShapeDtypeStruct((rows, width), dtype) for rows, dtype in zip(out_rows, out_types)
        ],
        compiler_params=pltpu.CompilerParams(vmem_limit_bytes=VMEM),
        cost_estimate=SHORT,
        name=name,
    )(*arrays, *early)


def reduce_over_time(pieces, bits_a, bits_b, nlat, early):
    keep_a, send_a, keep_b, send_b = pieces
    for i, (bit_a, bit_b) in enumerate(zip(bits_a, bits_b)):
        got_a, got_b = swap_with(send_a, "tm", 1 << bit_a), swap_with(send_b, "tm", 1 << bit_b)
        arrays = [keep_a, got_a, keep_b, got_b]
        rows = keep_a.shape[0]
        if i < len(bits_a) - 1:
            keep_a, send_a, keep_b, send_b = in_columns(
                halve_kernel, "sum_step", arrays, [rows // 2] * 4, [jnp.float32, jnp.bfloat16] * 2,
                early if i == 0 else (),
            )
    owned = rows // nlat
    if owned % GROUP == 0:
        band = in_columns(
            finish_kernel, "sum_end", arrays, [2 * owned] * nlat, [jnp.bfloat16] * nlat
        )
    else:
        total_a, total_b = both_sums(*arrays)
        band = [
            jnp.concatenate([x[n * owned : (n + 1) * owned] for x in (total_a, total_b)]).astype(
                jnp.bfloat16
            )
            for n in range(nlat)
        ]
    return band, send_a


def after(x, *others):
    return lax.optimization_barrier((x,) + others)[0]


def from_here(orders, bits, my_tm, my_lat):
    levels, lat_levels = len(bits), orders.shape[1].bit_length() - 1
    x = orders.reshape((2,) * (levels + lat_levels) + orders.shape[2:])
    for axis in range(levels + lat_levels):
        here = my_tm >> (levels - 1 - axis) if axis < levels else my_lat >> (
            levels + lat_levels - 1 - axis
        )
        x = jnp.where(here & 1 == 1, jnp.flip(x, axis), x)
    order = [levels - 1 - bit for bit in bits] + list(range(levels, x.ndim))
    return x.transpose(order).reshape(-1)


def exchange(band, owned):
    out = []
    for offset, piece in enumerate(band):
        if offset:
            piece = swap_with(piece, "lat", offset)
        if owned < GROUP:
            width = piece.shape[1]
            piece = jnp.pad(
                piece.reshape(2, owned, width), ((0, 0), (0, GROUP - owned), (0, 0))
            ).reshape(2 * GROUP, width)
        out.append(piece)
    return out


def shards(frames, owner_map):
    frame_count, row_count, nlon = frames.shape
    order_count = owner_map.shape[0]
    nlat, ntm = lax.axis_size("lat"), lax.axis_size("tm")
    my_tm, my_lat = lax.axis_index("tm"), lax.axis_index("lat")
    south = my_lat >= nlat // 2
    levels = ntm.bit_length() - 1
    bits_a = list(range(levels))
    bits_b = bits_a[-1:] + bits_a[:-1]

    pairs = owner_map.reshape(nlat, ntm, -1, 2)
    owned = pairs.shape[2]
    small, large = jnp.min(pairs, axis=3), jnp.max(pairs, axis=3)
    wanted = jnp.concatenate(
        [
            from_here(x.transpose(1, 0, 2), b, my_tm, my_lat)
            for x, b in ((small, bits_a), (large, bits_b))
        ]
    )
    wanted = table_column(wanted, order_count)
    place = (wanted[:, None] == jnp.arange(order_count, dtype=jnp.int32)[None, :]).astype(
        jnp.bfloat16
    )
    tables = [jnp.asarray(t) for t in longitude_tables(nlon, order_count)]
    time_mats = jnp.asarray(time_matrices(frame_count, ntm))
    where = jnp.stack([south.astype(jnp.int32), my_tm.astype(jnp.int32)])

    mine = lax.dynamic_slice(pairs, (my_lat, my_tm, 0, 0), (1, 1, owned, 2))[0, 0]
    mine = jnp.stack([jnp.min(mine, axis=1), jnp.max(mine, axis=1)])
    mine = jnp.pad(mine, ((0, 0), (0, GROUP - owned)), mode="edge")
    parity = jnp.broadcast_to(mine[:, :, None], (2, GROUP, 128))
    here = jnp.stack([my_lat.astype(jnp.int32), my_tm.astype(jnp.int32)])

    quarter = row_count // ROWS // 4
    parts = [(sum(QUARTERS[:i]) * quarter, n * quarter) for i, n in enumerate(QUARTERS)]
    pieces = []
    for part in parts:
        if pieces:
            where = after(where, pieces[-1][0])
        pieces.append(transform_chunk(part, where, frames, tables, time_mats, place))
    bands, early, waits = [], [], []
    for i, piece in enumerate(pieces):
        if i == len(pieces) - 1:
            made = [
                polynomials(after(mine[g], *waits), g, order_count, nlat, row_count, parts)
                for g in range(2)
            ]
            early = [token for _, token in made]
        band, sent = reduce_over_time(piece, bits_a, bits_b, nlat, early)
        waits = [sent, pieces[-1][0]]
        bands.append(exchange(band, owned))
    lanes_at, acc = [0, 0], [None, None]
    spectra = []
    for i, (band, (_, blocks)) in enumerate(zip(bands, parts)):
        last = i == len(parts) - 1
        if i:
            band = [after(band[0], *acc)] + band[1:]
        for g in (1, 0):
            lanes = (nlat // 2 - g * nlat // 4) * blocks * ROWS
            acc[g] = contract_chunk(
                g, last, here, band, parity[g], made[g][0], lanes_at[g], lanes, acc[g],
                g * order_count // 2, ntm,
            )
            lanes_at[g] += lanes
    spectra = [[x[0]] + [swap_with(x[d], "tm", d) for d in range(1, ntm)] for x in acc]
    return arrange(here, owner_map, *spectra, owned)


def solution(mesh):
    return jax.shard_map(
        shards,
        mesh=mesh,
        in_specs=(P("tm", "lat", None), P()),
        out_specs=P(None, "lat", None, "tm"),
        check_vma=False,
    )
```

time: 1580 us -> 117 us (0.07)
  loops' own time: 668 us -> 0 us
  other arithmetic: 466 us -> 1.77 us
  local copies, waits for them, and re-layouts: 161 us -> 9.09 us
  matrix products: 119 us -> 0 us
  waiting for transfers between devices: 115 us -> 6.9 us
  Pallas kernels: 0 us -> 59.6 us
  starting transfers between devices: 4.6 us -> 38.7 us
  blocking collectives: 16.6 us -> 0 us
    another operation x9 -> x0, loops' own time: 668 us -> none  [the longest x8 668 us: one_span(): lax.scan(stepper, state, offset + jnp.arange(span_len, dtype=jnp.int32),...]
    while x960 -> x0, other arithmetic: 363 us -> none
    dot_general x10 -> x0, matrix products: 119 us -> none  [the longest x8 68.4 us: one_span(): jnp.einsum('ekfr,lkr->ekfl', band, polynomials, preferred_element_type=jn...]
    unnamed x2 -> x0, waiting for transfers between devices: 89.3 us -> none
    dynamic_update_slice x64 -> x0, local copies, waits for them, and re-layouts: 68.1 us -> none  [one_span(): lax.scan(stepper, state, offset + jnp.arange(span_len, dtype=jnp.int32),...]
    pallas_call x0 -> x13, Pallas kernels: none -> 59.6 us  [the longest x2 31.7 us: transform_chunk(): pl.pallas_call(transform_kernel, grid_spec=pltpu.PrefetchScalarGridSpec(n...]
    slice x64 -> x0, local copies, waits for them, and re-layouts: 45.9 us -> none  [one_span(): lax.scan(stepper, state, offset + jnp.arange(span_len, dtype=jnp.int32),...]
    concatenate x64 -> x0, other arithmetic: 42.8 us -> none  [one_span(): lax.scan(stepper, state, offset + jnp.arange(span_len, dtype=jnp.int32),...]
  transfers between devices with their start and end apart: 2 -> 28, of which waited for: 2 -> 6; matrix products, arithmetic and copies ran while one was open for 0% -> 1% of each run, Pallas kernels for 0% -> 31%
where the time goes in v2:
time: 117 us; the launch traced here: 116 us
  Pallas kernels  59.6 us (51%)
  starting transfers between devices  38.7 us (33%)
  local copies, waits for them, and re-layouts  9.09 us (8%)
  waiting for transfers between devices  6.9 us (6%)
  other arithmetic  1.77 us (2%)
    ppermute x28, starting transfers between devices, swap_with(): return lax.ppermute(x, axis, [(i, i ^ offset) for i in range(count)])  38.7 us
    pallas_call x2, Pallas kernels, transform_chunk(): pl.pallas_call(transform_kernel, grid_spec=pltpu.PrefetchScalarGridSpec(n...  31.7 us
    pallas_call x4, Pallas kernels, contract_chunk(): pl.pallas_call(partial(contract_kernel, g, half, last, len(z), lanes_at),...  13.9 us
    pallas_call x2, Pallas kernels, polynomials(): pl.pallas_call(partial(polynomial_kernel, half, begin), grid=((L - begin)...  10.5 us
    ppermute x28, waiting for transfers between devices, swap_with(): return lax.ppermute(x, axis, [(i, i ^ offset) for i in range(count)])  6.9 us
    unnamed x35, local copies, waits for them, and re-layouts  6.41 us
    pallas_call x1, Pallas kernels, arrange(): pl.pallas_call(partial(arrange_kernel, owned), grid_spec=pltpu.PrefetchSc...  2.81 us
  transfers between devices with their start and end apart: 28, of which 6 were waited for; matrix products, arithmetic and copies ran while one was open for 1% of the time, Pallas kernels for 31%

profile of v2, /device:TPU:0, one launch (start us, length us, event | category | flops | bytes accessed | tf_op | source)
XLA Modules:
  0.0 116.4 jit_solution(4340648031355953035)
XLA Ops:
  0.0 0.8 reshape.213
  0.8 1.2 %fusion.9 = (s32[8,4,8]{2,1,0:T(4,128)S(1)}, s32[8,4,8]{2,1,0:T(4,128)S(1)}) fusion(s32[8,4,8,2]{3,2,1,0:T(8,128)S(1)} %reshape.213), kind=kLoop, calls=%fused_computation.49 | loop fusion | flops 512 | bytes 4096 | tf_op jit(solution)/shard_map/reduce_max | solution.py:514
  2.8 1.6 %copy-done = bf16[2048,512]{1,0:T(8,128)(2,1)S(1)} copy-done((bf16[2048,512]{1,0:T(8,128)(2,1)S(1)}, bf16[2048,512]{1,0:T(8,128)(2,1)}, u32[]{:S(2)}) %copy-start) | copy-done | bytes 2097176
  4.4 1.0 copy-done.1
  5.4 1.0 copy-done.2
  6.5 15.9 %longitude_time.2 = (bf16[128,2048]{1,0:T(8,128)(2,1)}, bf16[128,2048]{1,0:T(8,128)(2,1)}, bf16[128,2048]{1,0:T(8,128)(2,1)}, bf16[128,2048]{1,0:T(8,128)(2,1)}) custom-call(s32[2]{0:T(128)S(1)} %pad_add_fusion.1.where_ref, bf16[16,256,4096]{2,1,0:T(8,128)(2,1)} %frames_ref.3, bf16[1024,256]{1,0:T(8,128)(2,1)S(1)} %copy-done.2, ...), custom_call_target="tpu_custom_call" | custom-call | flops 1000000 | bytes 100000 | tf_op jit(solution)/shard_map/longitude_time/pallas_call | solution.py:124
  22.4 2.9 %collective-permute-start.2 = (bf16[128,2048]{1,0:T(8,128)(2,1)}, bf16[128,2048]{1,0:T(8,128)(2,1)S(1)}, u32[]{:S(2)}, u32[]{:S(2)}) collective-permute-start(bf16[128,2048]{1,0:T(8,128)(2,1)} %get-tuple-element.51), channel_id=1, source_target_pairs={{0,8},{8,0},{16,24},{24,16},{1,9},{9,1},{17,25},{25,17},{2,10},{10... | collective-permute-start | bytes 1572872 | tf_op jit(solution)/shard_map/ppermute | solution.py:397
  25.3 1.5 %collective-permute-start.3 = (bf16[128,2048]{1,0:T(8,128)(2,1)}, bf16[128,2048]{1,0:T(8,128)(2,1)S(1)}, u32[]{:S(2)}, u32[]{:S(2)}) collective-permute-start(bf16[128,2048]{1,0:T(8,128)(2,1)} %get-tuple-element.53), channel_id=1, source_target_pairs={{0,16},{8,24},{16,0},{24,8},{1,17},{9,25},{17,1},{25,9},{2,18},{10... | collective-permute-start | bytes 1572872 | tf_op jit(solution)/shard_map/ppermute | solution.py:397
  26.9 15.8 %longitude_time.3 = (bf16[128,2048]{1,0:T(8,128)(2,1)}, bf16[128,2048]{1,0:T(8,128)(2,1)}, bf16[128,2048]{1,0:T(8,128)(2,1)}, bf16[128,2048]{1,0:T(8,128)(2,1)}) custom-call(s32[2]{0:T(128)S(1)} %pad_add_fusion.1.where_ref, bf16[16,256,4096]{2,1,0:T(8,128)(2,1)} %frames_ref.3, bf16[1024,256]{1,0:T(8,128)(2,1)S(1)} %copy-done.2, ...), custom_call_target="tpu_custom_call" | custom-call | flops 1000000 | bytes 100000 | tf_op jit(solution)/shard_map/longitude_time/pallas_call | solution.py:124
  42.7 0.5 collective-permute-start
  43.5 0.2 sum_step.2
  43.7 2.0 %collective-permute-start.7 = (bf16[64,2048]{1,0:T(8,128)(2,1)S(1)}, bf16[64,2048]{1,0:T(8,128)(2,1)S(1)}, u32[]{:S(2)}, u32[]{:S(2)}) collective-permute-start(bf16[64,2048]{1,0:T(8,128)(2,1)S(1)} %get-tuple-element.66), channel_id=1, source_target_pairs={{0,8},{8,0},{16,24},{24,16},{1,9},{9,1},{17,25},{25,17},{2,10},{10... | collective-permute-start | bytes 786440 | tf_op jit(solution)/shard_map/ppermute | solution.py:397
  45.7 1.5 %collective-permute-start.6 = (bf16[64,2048]{1,0:T(8,128)(2,1)S(1)}, bf16[64,2048]{1,0:T(8,128)(2,1)S(1)}, u32[]{:S(2)}, u32[]{:S(2)}) collective-permute-start(bf16[64,2048]{1,0:T(8,128)(2,1)S(1)} %get-tuple-element.54), channel_id=1, source_target_pairs={{0,16},{8,24},{16,0},{24,8},{1,17},{9,25},{17,1},{25,9},{2,18},{10... | collective-permute-start | bytes 786440 | tf_op jit(solution)/shard_map/ppermute | solution.py:397
  47.3 3.6 %legendre.3 = (bf16[6144,512]{1,0:T(8,128)(2,1)S(1)}, f32[8,128]{1,0:T(8,128)S(1)}) custom-call(f32[8,128]{1,0:T(8,128)S(1)} %broadcast_in_dim.9.orders_ref, f32[1,512]{1,0:T(1,128)S(1)} %copy-done.10, f32[3,512]{1,0:T(4,128)S(1)} %copy-done.9), custom_call_target="tpu_custom_call" | custom-call | flops 1000000 | bytes 100000 | tf_op jit(solution)/shard_map/legendre/pallas_call | solution.py:231
  51.0 6.9 %legendre.2 = (bf16[8192,1024]{1,0:T(8,128)(2,1)S(1)}, f32[8,128]{1,0:T(8,128)S(1)}) custom-call(f32[8,128]{1,0:T(8,128)S(1)} %broadcast_in_dim.8.orders_ref, f32[1,512]{1,0:T(1,128)S(1)} %copy-done.10, f32[3,1024]{1,0:T(4,128)S(1)} %copy-done.7), custom_call_target="tpu_custom_call" | custom-call | flops 1000000 | bytes 100000 | tf_op jit(solution)/shard_map/legendre/pallas_call | solution.py:231
  58.0 0.4 collective-permute-done.1.got_b
  58.3 1.0 copy-done.3
  59.4 1.0 copy-done.4
  60.6 0.2 collective-permute-start.4
  60.9 1.8 %collective-permute-start.5 = (bf16[64,2048]{1,0:T(8,128)(2,1)S(1)}, bf16[64,2048]{1,0:T(8,128)(2,1)S(1)}, u32[]{:S(2)}, u32[]{:S(2)}) collective-permute-start(bf16[64,2048]{1,0:T(8,128)(2,1)S(1)} %get-tuple-element.62), channel_id=1, source_target_pairs={{0,8},{8,0},{16,24},{24,16},{1,9},{9,1},{17,25},{25,17},{2,10},{10... | collective-permute-start | bytes 786440 | tf_op jit(solution)/shard_map/ppermute | solution.py:397
  62.9 1.6 %collective-permute-start.9 = (bf16[16,2048]{1,0:T(8,128)(2,1)S(1)}, bf16[16,2048]{1,0:T(8,128)(2,1)S(1)}, u32[]{:S(2)}, u32[]{:S(2)}) collective-permute-start(bf16[16,2048]{1,0:T(8,128)(2,1)S(1)} %get-tuple-element.69), channel_id=1, source_target_pairs={{0,2},{1,3},{2,0},{3,1},{4,6},{5,7},{6,4},{7,5},{8,10},{9,11},{10,... | collective-permute-start | bytes 196616 | tf_op jit(solution)/shard_map/ppermute | solution.py:397
  64.8 2.8 %collective-permute-done.4.got_a = bf16[64,2048]{1,0:T(8,128)(2,1)S(1)} collective-permute-done((bf16[64,2048]{1,0:T(8,128)(2,1)S(1)}, bf16[64,2048]{1,0:T(8,128)(2,1)S(1)}, u32[]{:S(2)}, u32[]{:S(2)}) %collective-permute-start.4) | collective-permute-done | bytes 262176 | tf_op jit(solution)/shard_map/ppermute | solution.py:397
  67.5 2.6 %collective-permute-start.11 = (bf16[16,2048]{1,0:T(8,128)(2,1)S(1)}, bf16[16,2048]{1,0:T(8,128)(2,1)S(1)}, u32[]{:S(2)}, u32[]{:S(2)}) collective-permute-start(bf16[16,2048]{1,0:T(8,128)(2,1)S(1)} %get-tuple-element.71), channel_id=1, source_target_pairs={{0,4},{1,5},{2,6},{3,7},{4,0},{5,1},{6,2},{7,3},{8,12},{9,13},{10,... | collective-permute-start | bytes 196616 | tf_op jit(solution)/shard_map/ppermute | solution.py:397
  70.2 1.4 %collective-permute-start.13 = (bf16[16,2048]{1,0:T(8,128)(2,1)S(1)}, bf16[16,2048]{1,0:T(8,128)(2,1)S(1)}, u32[]{:S(2)}, u32[]{:S(2)}) collective-permute-start(bf16[16,2048]{1,0:T(8,128)(2,1)S(1)} %get-tuple-element.73), channel_id=1, source_target_pairs={{0,6},{1,7},{2,4},{3,5},{4,2},{5,3},{6,0},{7,1},{8,14},{9,15},{10,... | collective-permute-start | bytes 196616 | tf_op jit(solution)/shard_map/ppermute | solution.py:397
  71.6 2.4 %collective-permute-start.14 = (bf16[16,2048]{1,0:T(8,128)(2,1)S(1)}, bf16[16,2048]{1,0:T(8,128)(2,1)S(1)}, u32[]{:S(2)}, u32[]{:S(2)}) collective-permute-start(bf16[16,2048]{1,0:T(8,128)(2,1)S(1)} %get-tuple-element.74), channel_id=1, source_target_pairs={{0,7},{1,6},{2,5},{3,4},{4,3},{5,2},{6,1},{7,0},{8,15},{9,14},{10,... | collective-permute-start | bytes 196616 | tf_op jit(solution)/shard_map/ppermute | solution.py:397
  74.2 4.5 %collective-permute-start.16 = (bf16[16,2048]{1,0:T(8,128)(2,1)S(1)}, bf16[16,2048]{1,0:T(8,128)(2,1)S(1)}, u32[]{:S(2)}, u32[]{:S(2)}) collective-permute-start(bf16[16,2048]{1,0:T(8,128)(2,1)S(1)} %get-tuple-element.79), channel_id=1, source_target_pairs={{0,2},{1,3},{2,0},{3,1},{4,6},{5,7},{6,4},{7,5},{8,10},{9,11},{10,... | collective-permute-start | bytes 196616 | tf_op jit(solution)/shard_map/ppermute | solution.py:397
  78.8 4.7 %collective-permute-start.18 = (bf16[16,2048]{1,0:T(8,128)(2,1)S(1)}, bf16[16,2048]{1,0:T(8,128)(2,1)S(1)}, u32[]{:S(2)}, u32[]{:S(2)}) collective-permute-start(bf16[16,2048]{1,0:T(8,128)(2,1)S(1)} %get-tuple-element.81), channel_id=1, source_target_pairs={{0,4},{1,5},{2,6},{3,7},{4,0},{5,1},{6,2},{7,3},{8,12},{9,13},{10,... | collective-permute-start | bytes 196616 | tf_op jit(solution)/shard_map/ppermute | solution.py:397
  83.5 0.4 collective-permute-start.19
  83.9 2.2 %collective-permute-start.20 = (bf16[16,2048]{1,0:T(8,128)(2,1)S(1)}, bf16[16,2048]{1,0:T(8,128)(2,1)S(1)}, u32[]{:S(2)}, u32[]{:S(2)}) collective-permute-start(bf16[16,2048]{1,0:T(8,128)(2,1)S(1)} %get-tuple-element.83), channel_id=1, source_target_pairs={{0,6},{1,7},{2,4},{3,5},{4,2},{5,3},{6,0},{7,1},{8,14},{9,15},{10,... | collective-permute-start | bytes 196616 | tf_op jit(solution)/shard_map/ppermute | solution.py:397
  86.1 0.7 collective-permute-start.21
  86.9 2.4 %latitude_sum.5.refs_10_ = f32[768,128]{1,0:T(8,128)S(1)} custom-call(s32[2]{0:T(128)S(1)} %pad_add_fusion.here_ref, bf16[16,2048]{1,0:T(8,128)(2,1)S(1)} %get-tuple-element.67.refs_0_, bf16[16,2048]{1,0:T(8,128)(2,1)S(1)} %collective-permute-done.8.refs_1_, bf16[16,2048]{1,0:T(8,128)(2,1)S(1)} %collective-permute-done.9.refs_2_, ...), custom_call_target="tpu_custom_call" | custom-call | flops 1000000 | bytes 100000 | tf_op jit(solution)/shard_map/latitude_sum/pallas_call | solution.py:342
  89.4 4.4 %latitude_sum.4.refs_10_ = f32[1024,128]{1,0:T(8,128)S(1)} custom-call(s32[2]{0:T(128)S(1)} %pad_add_fusion.here_ref, bf16[16,2048]{1,0:T(8,128)(2,1)S(1)} %get-tuple-element.67.refs_0_, bf16[16,2048]{1,0:T(8,128)(2,1)S(1)} %collective-permute-done.8.refs_1_, bf16[16,2048]{1,0:T(8,128)(2,1)S(1)} %collective-permute-done.9.refs_2_, ...), custom_call_target="tpu_custom_call" | custom-call | flops 1000000 | bytes 100000 | tf_op jit(solution)/shard_map/latitude_sum/pallas_call | solution.py:342
  93.8 4.5 %latitude_sum.6 = bf16[4,128,256]{2,1,0:T(8,128)(2,1)S(1)} custom-call(s32[2]{0:T(128)S(1)} %pad_add_fusion.here_ref, bf16[16,2048]{1,0:T(8,128)(2,1)S(1)} %get-tuple-element.77.refs_0_, bf16[16,2048]{1,0:T(8,128)(2,1)S(1)} %collective-permute-done.15.refs_1_, bf16[16,2048]{1,0:T(8,128)(2,1)S(1)} %collective-permute-done.16.refs_2_, ...), custom_call_target="tpu_custom_call" | custom-call | flops 1000000 | bytes 100000 | tf_op jit(solution)/shard_map/latitude_sum/pallas_call | solution.py:342
  98.3 0.6 slice_bitcast_fusion.4
  99.0 1.7 %collective-permute-start.24 = (bf16[128,256]{1,0:T(8,128)(2,1)S(1)}, bf16[128,256]{1,0:T(8,128)(2,1)S(1)}, u32[]{:S(2)}, u32[]{:S(2)}) collective-permute-start(bf16[128,256]{1,0:T(8,128)(2,1)S(1)} %get-tuple-element.93), channel_id=1, source_target_pairs={{0,24},{8,16},{16,8},{24,0},{1,25},{9,17},{17,9},{25,1},{2,26},{10... | collective-permute-start | bytes 196616 | tf_op jit(solution)/shard_map/ppermute | solution.py:397
  100.6 2.6 %latitude_sum.7 = bf16[4,128,256]{2,1,0:T(8,128)(2,1)S(1)} custom-call(s32[2]{0:T(128)S(1)} %pad_add_fusion.here_ref, bf16[16,2048]{1,0:T(8,128)(2,1)S(1)} %get-tuple-element.77.refs_0_, bf16[16,2048]{1,0:T(8,128)(2,1)S(1)} %collective-permute-done.15.refs_1_, bf16[16,2048]{1,0:T(8,128)(2,1)S(1)} %collective-permute-done.16.refs_2_, ...), custom_call_target="tpu_custom_call" | custom-call | flops 1000000 | bytes 100000 | tf_op jit(solution)/shard_map/latitude_sum/pallas_call | solution.py:342
  103.3 0.6 slice_bitcast_fusion
  103.9 1.3 %collective-permute-start.23 = (bf16[128,256]{1,0:T(8,128)(2,1)S(1)}, bf16[128,256]{1,0:T(8,128)(2,1)S(1)}, u32[]{:S(2)}, u32[]{:S(2)}) collective-permute-start(bf16[128,256]{1,0:T(8,128)(2,1)S(1)} %get-tuple-element.94), channel_id=1, source_target_pairs={{0,16},{8,24},{16,0},{24,8},{1,17},{9,25},{17,1},{25,9},{2,18},{10... | collective-permute-start | bytes 196616 | tf_op jit(solution)/shard_map/ppermute | solution.py:397
  105.2 0.5 collective-permute-start.22
  105.7 1.7 %collective-permute-start.27 = (bf16[128,256]{1,0:T(8,128)(2,1)S(1)}, bf16[128,256]{1,0:T(8,128)(2,1)S(1)}, u32[]{:S(2)}, u32[]{:S(2)}) collective-permute-start(bf16[128,256]{1,0:T(8,128)(2,1)S(1)} %get-tuple-element.89), channel_id=1, source_target_pairs={{0,24},{8,16},{16,8},{24,0},{1,25},{9,17},{17,9},{25,1},{2,26},{10... | collective-permute-start | bytes 196616 | tf_op jit(solution)/shard_map/ppermute | solution.py:397
  107.4 1.3 %collective-permute-start.26 = (bf16[128,256]{1,0:T(8,128)(2,1)S(1)}, bf16[128,256]{1,0:T(8,128)(2,1)S(1)}, u32[]{:S(2)}, u32[]{:S(2)}) collective-permute-start(bf16[128,256]{1,0:T(8,128)(2,1)S(1)} %get-tuple-element.90), channel_id=1, source_target_pairs={{0,16},{8,24},{16,0},{24,8},{1,17},{9,25},{17,1},{25,9},{2,18},{10... | collective-permute-start | bytes 196616 | tf_op jit(solution)/shard_map/ppermute | solution.py:397
  108.7 0.5 collective-permute-start.25
  109.2 0.9 collective-permute-done.22.refs_1_
  110.1 1.3 %collective-permute-done.27.refs_7_ = bf16[128,256]{1,0:T(8,128)(2,1)S(1)} collective-permute-done((bf16[128,256]{1,0:T(8,128)(2,1)S(1)}, bf16[128,256]{1,0:T(8,128)(2,1)S(1)}, u32[]{:S(2)}, u32[]{:S(2)}) %collective-permute-start.27) | collective-permute-done | bytes 65568 | tf_op jit(solution)/shard_map/ppermute | solution.py:397
  111.4 1.1 collective-permute-done.26.refs_6_
  112.5 0.4 collective-permute-done.25.refs_5_
  113.1 0.4 copy-done.16
  113.6 2.8 %slot_order.1 = f32[2,64,8,256]{3,2,1,0:T(8,128)} custom-call(s32[2]{0:T(128)} %copy-done.8, s32[512]{0:T(512)} %orders_ref.1, bf16[128,256]{1,0:T(8,128)(2,1)} %get-tuple-element.96.refs_0_, bf16[128,256]{1,0:T(8,128)(2,1)} %copy-done.13, bf16[128,256]{1,0:T(8,128)(2,1)} %copy-done.12, bf16[128,256]{1,0:T(8,128)(2,1)} %copy-done.11, ...), custom_call_target="tpu_custom_call" | custom-call | tf_op jit(solution)/shard_map/slot_order/pallas_call | solution.py:382
  (89 shorter events, 2.4 us)
Async XLA Ops:
  2.8 1.6 %copy-start = (bf16[2048,512]{1,0:T(8,128)(2,1)S(1)}, bf16[2048,512]{1,0:T(8,128)(2,1)}, u32[]{:S(2)}) copy-start(bf16[2048,512]{1,0:T(8,128)(2,1)} %constant.89.clone.odd_ref) | copy-start | bytes 6291460
  4.4 1.0 copy-start.1
  5.4 1.0 copy-start.2
  22.4 21.0 %collective-permute-start.2 = (bf16[128,2048]{1,0:T(8,128)(2,1)}, bf16[128,2048]{1,0:T(8,128)(2,1)S(1)}, u32[]{:S(2)}, u32[]{:S(2)}) collective-permute-start(bf16[128,2048]{1,0:T(8,128)(2,1)} %get-tuple-element.51), channel_id=1, source_target_pairs={{0,8},{8,0},{16,24},{24,16},{1,9},{9,1},{17,25},{25,17},{2,10},{10... | collective-permute-start | bytes 1572872 | tf_op jit(solution)/shard_map/ppermute | solution.py:397
  25.3 18.1 %collective-permute-start.3 = (bf16[128,2048]{1,0:T(8,128)(2,1)}, bf16[128,2048]{1,0:T(8,128)(2,1)S(1)}, u32[]{:S(2)}, u32[]{:S(2)}) collective-permute-start(bf16[128,2048]{1,0:T(8,128)(2,1)} %get-tuple-element.53), channel_id=1, source_target_pairs={{0,16},{8,24},{16,0},{24,8},{1,17},{9,25},{17,1},{25,9},{2,18},{10... | collective-permute-start | bytes 1572872 | tf_op jit(solution)/shard_map/ppermute | solution.py:397
  26.9 16.6 %copy-start.5 = (bf16[128,2048]{1,0:T(8,128)(2,1)S(1)}, bf16[128,2048]{1,0:T(8,128)(2,1)}, u32[]{:S(2)}) copy-start(bf16[128,2048]{1,0:T(8,128)(2,1)} %get-tuple-element.45.keep_a) | copy-start | bytes 1572868
  26.9 16.6 %copy-start.6 = (bf16[128,2048]{1,0:T(8,128)(2,1)S(1)}, bf16[128,2048]{1,0:T(8,128)(2,1)}, u32[]{:S(2)}) copy-start(bf16[128,2048]{1,0:T(8,128)(2,1)} %get-tuple-element.52.keep_b) | copy-start | bytes 1572868
  26.9 20.5 %copy-start.9 = (f32[3,512]{1,0:T(4,128)S(1)}, f32[3,512]{1,0:T(4,128)}, u32[]{:S(2)}) copy-start(f32[3,512]{1,0:T(4,128)} %constant.93.clone.rows_ref) | copy-start | bytes 18436
  26.9 20.5 %copy-start.10 = (f32[1,512]{1,0:T(1,128)S(1)}, f32[1,512]{1,0:T(1,128)}, u32[]{:S(2)}) copy-start(f32[1,512]{1,0:T(1,128)} %constant.91.clone.growth_ref) | copy-start | bytes 6148
  26.9 24.2 %copy-start.7 = (f32[3,1024]{1,0:T(4,128)S(1)}, f32[3,1024]{1,0:T(4,128)}, u32[]{:S(2)}) copy-start(f32[3,1024]{1,0:T(4,128)} %constant.92.clone.rows_ref) | copy-start | bytes 36868
  42.7 15.2 %collective-permute-start = (bf16[128,2048]{1,0:T(8,128)(2,1)}, bf16[128,2048]{1,0:T(8,128)(2,1)S(1)}, u32[]{:S(2)}, u32[]{:S(2)}) collective-permute-start(bf16[128,2048]{1,0:T(8,128)(2,1)} %get-tuple-element.48), channel_id=1, source_target_pairs={{0,8},{8,0},{16,24},{24,16},{1,9},{9,1},{17,25},{25,17},{2,10},{10... | collective-permute-start | bytes 1572872 | tf_op jit(solution)/shard_map/ppermute | solution.py:397
  43.2 15.1 %collective-permute-start.1 = (bf16[128,2048]{1,0:T(8,128)(2,1)}, bf16[128,2048]{1,0:T(8,128)(2,1)S(1)}, u32[]{:S(2)}, u32[]{:S(2)}) collective-permute-start(bf16[128,2048]{1,0:T(8,128)(2,1)} %get-tuple-element.50), channel_id=1, source_target_pairs={{0,16},{8,24},{16,0},{24,8},{1,17},{9,25},{17,1},{25,9},{2,18},{10... | collective-permute-start | bytes 1572872 | tf_op jit(solution)/shard_map/ppermute | solution.py:397
  43.7 19.0 %collective-permute-start.7 = (bf16[64,2048]{1,0:T(8,128)(2,1)S(1)}, bf16[64,2048]{1,0:T(8,128)(2,1)S(1)}, u32[]{:S(2)}, u32[]{:S(2)}) collective-permute-start(bf16[64,2048]{1,0:T(8,128)(2,1)S(1)} %get-tuple-element.66), channel_id=1, source_target_pairs={{0,8},{8,0},{16,24},{24,16},{1,9},{9,1},{17,25},{25,17},{2,10},{10... | collective-permute-start | bytes 786440 | tf_op jit(solution)/shard_map/ppermute | solution.py:397
  45.7 17.0 %collective-permute-start.6 = (bf16[64,2048]{1,0:T(8,128)(2,1)S(1)}, bf16[64,2048]{1,0:T(8,128)(2,1)S(1)}, u32[]{:S(2)}, u32[]{:S(2)}) collective-permute-start(bf16[64,2048]{1,0:T(8,128)(2,1)S(1)} %get-tuple-element.54), channel_id=1, source_target_pairs={{0,16},{8,24},{16,0},{24,8},{1,17},{9,25},{17,1},{25,9},{2,18},{10... | collective-permute-start | bytes 786440 | tf_op jit(solution)/shard_map/ppermute | solution.py:397
  58.3 1.0 copy-start.3
  59.4 1.0 copy-start.4
  60.6 6.9 %collective-permute-start.4 = (bf16[64,2048]{1,0:T(8,128)(2,1)S(1)}, bf16[64,2048]{1,0:T(8,128)(2,1)S(1)}, u32[]{:S(2)}, u32[]{:S(2)}) collective-permute-start(bf16[64,2048]{1,0:T(8,128)(2,1)S(1)} %get-tuple-element.60), channel_id=1, source_target_pairs={{0,16},{8,24},{16,0},{24,8},{1,17},{9,25},{17,1},{25,9},{2,18},{10... | collective-permute-start | bytes 786440 | tf_op jit(solution)/shard_map/ppermute | solution.py:397
  60.9 9.3 %collective-permute-start.5 = (bf16[64,2048]{1,0:T(8,128)(2,1)S(1)}, bf16[64,2048]{1,0:T(8,128)(2,1)S(1)}, u32[]{:S(2)}, u32[]{:S(2)}) collective-permute-start(bf16[64,2048]{1,0:T(8,128)(2,1)S(1)} %get-tuple-element.62), channel_id=1, source_target_pairs={{0,8},{8,0},{16,24},{24,16},{1,9},{9,1},{17,25},{25,17},{2,10},{10... | collective-permute-start | bytes 786440 | tf_op jit(solution)/shard_map/ppermute | solution.py:397
  62.8 7.4 %collective-permute-start.8 = (bf16[16,2048]{1,0:T(8,128)(2,1)S(1)}, bf16[16,2048]{1,0:T(8,128)(2,1)S(1)}, u32[]{:S(2)}, u32[]{:S(2)}) collective-permute-start(bf16[16,2048]{1,0:T(8,128)(2,1)S(1)} %get-tuple-element.68), channel_id=1, source_target_pairs={{0,1},{1,0},{2,3},{3,2},{4,5},{5,4},{6,7},{7,6},{8,9},{9,8},{10,11... | collective-permute-start | bytes 196616 | tf_op jit(solution)/shard_map/ppermute | solution.py:397
  62.9 8.8 %collective-permute-start.9 = (bf16[16,2048]{1,0:T(8,128)(2,1)S(1)}, bf16[16,2048]{1,0:T(8,128)(2,1)S(1)}, u32[]{:S(2)}, u32[]{:S(2)}) collective-permute-start(bf16[16,2048]{1,0:T(8,128)(2,1)S(1)} %get-tuple-element.69), channel_id=1, source_target_pairs={{0,2},{1,3},{2,0},{3,1},{4,6},{5,7},{6,4},{7,5},{8,10},{9,11},{10,... | collective-permute-start | bytes 196616 | tf_op jit(solution)/shard_map/ppermute | solution.py:397
  64.5 9.5 %collective-permute-start.10 = (bf16[16,2048]{1,0:T(8,128)(2,1)S(1)}, bf16[16,2048]{1,0:T(8,128)(2,1)S(1)}, u32[]{:S(2)}, u32[]{:S(2)}) collective-permute-start(bf16[16,2048]{1,0:T(8,128)(2,1)S(1)} %get-tuple-element.70), channel_id=1, source_target_pairs={{0,3},{1,2},{2,1},{3,0},{4,7},{5,6},{6,5},{7,4},{8,11},{9,10},{10,... | collective-permute-start | bytes 196616 | tf_op jit(solution)/shard_map/ppermute | solution.py:397
  67.5 6.7 %collective-permute-start.11 = (bf16[16,2048]{1,0:T(8,128)(2,1)S(1)}, bf16[16,2048]{1,0:T(8,128)(2,1)S(1)}, u32[]{:S(2)}, u32[]{:S(2)}) collective-permute-start(bf16[16,2048]{1,0:T(8,128)(2,1)S(1)} %get-tuple-element.71), channel_id=1, source_target_pairs={{0,4},{1,5},{2,6},{3,7},{4,0},{5,1},{6,2},{7,3},{8,12},{9,13},{10,... | collective-permute-start | bytes 196616 | tf_op jit(solution)/shard_map/ppermute | solution.py:397
  70.1 8.7 %collective-permute-start.12 = (bf16[16,2048]{1,0:T(8,128)(2,1)S(1)}, bf16[16,2048]{1,0:T(8,128)(2,1)S(1)}, u32[]{:S(2)}, u32[]{:S(2)}) collective-permute-start(bf16[16,2048]{1,0:T(8,128)(2,1)S(1)} %get-tuple-element.72), channel_id=1, source_target_pairs={{0,5},{1,4},{2,7},{3,6},{4,1},{5,0},{6,3},{7,2},{8,13},{9,12},{10,... | collective-permute-start | bytes 196616 | tf_op jit(solution)/shard_map/ppermute | solution.py:397
  70.2 8.6 %collective-permute-start.13 = (bf16[16,2048]{1,0:T(8,128)(2,1)S(1)}, bf16[16,2048]{1,0:T(8,128)(2,1)S(1)}, u32[]{:S(2)}, u32[]{:S(2)}) collective-permute-start(bf16[16,2048]{1,0:T(8,128)(2,1)S(1)} %get-tuple-element.73), channel_id=1, source_target_pairs={{0,6},{1,7},{2,4},{3,5},{4,2},{5,3},{6,0},{7,1},{8,14},{9,15},{10,... | collective-permute-start | bytes 196616 | tf_op jit(solution)/shard_map/ppermute | solution.py:397
  71.6 11.8 %collective-permute-start.14 = (bf16[16,2048]{1,0:T(8,128)(2,1)S(1)}, bf16[16,2048]{1,0:T(8,128)(2,1)S(1)}, u32[]{:S(2)}, u32[]{:S(2)}) collective-permute-start(bf16[16,2048]{1,0:T(8,128)(2,1)S(1)} %get-tuple-element.74), channel_id=1, source_target_pairs={{0,7},{1,6},{2,5},{3,4},{4,3},{5,2},{6,1},{7,0},{8,15},{9,14},{10,... | collective-permute-start | bytes 196616 | tf_op jit(solution)/shard_map/ppermute | solution.py:397
  74.0 9.9 %collective-permute-start.15 = (bf16[16,2048]{1,0:T(8,128)(2,1)S(1)}, bf16[16,2048]{1,0:T(8,128)(2,1)S(1)}, u32[]{:S(2)}, u32[]{:S(2)}) collective-permute-start(bf16[16,2048]{1,0:T(8,128)(2,1)S(1)} %get-tuple-element.78), channel_id=1, source_target_pairs={{0,1},{1,0},{2,3},{3,2},{4,5},{5,4},{6,7},{7,6},{8,9},{9,8},{10,11... | collective-permute-start | bytes 196616 | tf_op jit(solution)/shard_map/ppermute | solution.py:397
  74.2 11.8 %collective-permute-start.16 = (bf16[16,2048]{1,0:T(8,128)(2,1)S(1)}, bf16[16,2048]{1,0:T(8,128)(2,1)S(1)}, u32[]{:S(2)}, u32[]{:S(2)}) collective-permute-start(bf16[16,2048]{1,0:T(8,128)(2,1)S(1)} %get-tuple-element.79), channel_id=1, source_target_pairs={{0,2},{1,3},{2,0},{3,1},{4,6},{5,7},{6,4},{7,5},{8,10},{9,11},{10,... | collective-permute-start | bytes 196616 | tf_op jit(solution)/shard_map/ppermute | solution.py:397
  78.8 15.0 %collective-permute-start.17 = (bf16[16,2048]{1,0:T(8,128)(2,1)S(1)}, bf16[16,2048]{1,0:T(8,128)(2,1)S(1)}, u32[]{:S(2)}, u32[]{:S(2)}) collective-permute-start(bf16[16,2048]{1,0:T(8,128)(2,1)S(1)} %get-tuple-element.80), channel_id=1, source_target_pairs={{0,3},{1,2},{2,1},{3,0},{4,7},{5,6},{6,5},{7,4},{8,11},{9,10},{10,... | collective-permute-start | bytes 196616 | tf_op jit(solution)/shard_map/ppermute | solution.py:397
  78.8 15.0 %collective-permute-start.18 = (bf16[16,2048]{1,0:T(8,128)(2,1)S(1)}, bf16[16,2048]{1,0:T(8,128)(2,1)S(1)}, u32[]{:S(2)}, u32[]{:S(2)}) collective-permute-start(bf16[16,2048]{1,0:T(8,128)(2,1)S(1)} %get-tuple-element.81), channel_id=1, source_target_pairs={{0,4},{1,5},{2,6},{3,7},{4,0},{5,1},{6,2},{7,3},{8,12},{9,13},{10,... | collective-permute-start | bytes 196616 | tf_op jit(solution)/shard_map/ppermute | solution.py:397
  83.5 10.3 %collective-permute-start.19 = (bf16[16,2048]{1,0:T(8,128)(2,1)S(1)}, bf16[16,2048]{1,0:T(8,128)(2,1)S(1)}, u32[]{:S(2)}, u32[]{:S(2)}) collective-permute-start(bf16[16,2048]{1,0:T(8,128)(2,1)S(1)} %get-tuple-element.82), channel_id=1, source_target_pairs={{0,5},{1,4},{2,7},{3,6},{4,1},{5,0},{6,3},{7,2},{8,13},{9,12},{10,... | collective-permute-start | bytes 196616 | tf_op jit(solution)/shard_map/ppermute | solution.py:397
  83.9 9.9 %collective-permute-start.20 = (bf16[16,2048]{1,0:T(8,128)(2,1)S(1)}, bf16[16,2048]{1,0:T(8,128)(2,1)S(1)}, u32[]{:S(2)}, u32[]{:S(2)}) collective-permute-start(bf16[16,2048]{1,0:T(8,128)(2,1)S(1)} %get-tuple-element.83), channel_id=1, source_target_pairs={{0,6},{1,7},{2,4},{3,5},{4,2},{5,3},{6,0},{7,1},{8,14},{9,15},{10,... | collective-permute-start | bytes 196616 | tf_op jit(solution)/shard_map/ppermute | solution.py:397
  86.1 7.7 %collective-permute-start.21 = (bf16[16,2048]{1,0:T(8,128)(2,1)S(1)}, bf16[16,2048]{1,0:T(8,128)(2,1)S(1)}, u32[]{:S(2)}, u32[]{:S(2)}) collective-permute-start(bf16[16,2048]{1,0:T(8,128)(2,1)S(1)} %get-tuple-element.84), channel_id=1, source_target_pairs={{0,7},{1,6},{2,5},{3,4},{4,3},{5,2},{6,1},{7,0},{8,15},{9,14},{10,... | collective-permute-start | bytes 196616 | tf_op jit(solution)/shard_map/ppermute | solution.py:397
  86.8 13.8 %copy-start.8 = (s32[2]{0:T(128)}, s32[2]{0:T(128)S(1)}, u32[]{:S(2)}) copy-start(s32[2]{0:T(128)S(1)} %pad_add_fusion.here_ref) | copy-start | bytes 28
  99.0 9.7 %collective-permute-start.24 = (bf16[128,256]{1,0:T(8,128)(2,1)S(1)}, bf16[128,256]{1,0:T(8,128)(2,1)S(1)}, u32[]{:S(2)}, u32[]{:S(2)}) collective-permute-start(bf16[128,256]{1,0:T(8,128)(2,1)S(1)} %get-tuple-element.93), channel_id=1, source_target_pairs={{0,24},{8,16},{16,8},{24,0},{1,25},{9,17},{17,9},{25,1},{2,26},{10... | collective-permute-start | bytes 196616 | tf_op jit(solution)/shard_map/ppermute | solution.py:397
  103.9 5.3 %collective-permute-start.23 = (bf16[128,256]{1,0:T(8,128)(2,1)S(1)}, bf16[128,256]{1,0:T(8,128)(2,1)S(1)}, u32[]{:S(2)}, u32[]{:S(2)}) collective-permute-start(bf16[128,256]{1,0:T(8,128)(2,1)S(1)} %get-tuple-element.94), channel_id=1, source_target_pairs={{0,16},{8,24},{16,0},{24,8},{1,17},{9,25},{17,1},{25,9},{2,18},{10... | collective-permute-start | bytes 196616 | tf_op jit(solution)/shard_map/ppermute | solution.py:397
  105.2 4.9 %collective-permute-start.22 = (bf16[128,256]{1,0:T(8,128)(2,1)S(1)}, bf16[128,256]{1,0:T(8,128)(2,1)S(1)}, u32[]{:S(2)}, u32[]{:S(2)}) collective-permute-start(bf16[128,256]{1,0:T(8,128)(2,1)S(1)} %get-tuple-element.95), channel_id=1, source_target_pairs={{0,8},{8,0},{16,24},{24,16},{1,9},{9,1},{17,25},{25,17},{2,10},{10... | collective-permute-start | bytes 196616 | tf_op jit(solution)/shard_map/ppermute | solution.py:397
  105.7 5.6 %collective-permute-start.27 = (bf16[128,256]{1,0:T(8,128)(2,1)S(1)}, bf16[128,256]{1,0:T(8,128)(2,1)S(1)}, u32[]{:S(2)}, u32[]{:S(2)}) collective-permute-start(bf16[128,256]{1,0:T(8,128)(2,1)S(1)} %get-tuple-element.89), channel_id=1, source_target_pairs={{0,24},{8,16},{16,8},{24,0},{1,25},{9,17},{17,9},{25,1},{2,26},{10... | collective-permute-start | bytes 196616 | tf_op jit(solution)/shard_map/ppermute | solution.py:397
  107.4 5.1 %collective-permute-start.26 = (bf16[128,256]{1,0:T(8,128)(2,1)S(1)}, bf16[128,256]{1,0:T(8,128)(2,1)S(1)}, u32[]{:S(2)}, u32[]{:S(2)}) collective-permute-start(bf16[128,256]{1,0:T(8,128)(2,1)S(1)} %get-tuple-element.90), channel_id=1, source_target_pairs={{0,16},{8,24},{16,0},{24,8},{1,17},{9,25},{17,1},{25,9},{2,18},{10... | collective-permute-start | bytes 196616 | tf_op jit(solution)/shard_map/ppermute | solution.py:397
  108.7 4.3 %copy-start.11 = (bf16[128,256]{1,0:T(8,128)(2,1)}, bf16[128,256]{1,0:T(8,128)(2,1)S(1)}, u32[]{:S(2)}) copy-start(bf16[128,256]{1,0:T(8,128)(2,1)S(1)} %collective-permute-done.24.refs_3_) | copy-start | bytes 196612
  108.7 4.3 %collective-permute-start.25 = (bf16[128,256]{1,0:T(8,128)(2,1)S(1)}, bf16[128,256]{1,0:T(8,128)(2,1)S(1)}, u32[]{:S(2)}, u32[]{:S(2)}) collective-permute-start(bf16[128,256]{1,0:T(8,128)(2,1)S(1)} %get-tuple-element.91), channel_id=1, source_target_pairs={{0,8},{8,0},{16,24},{24,16},{1,9},{9,1},{17,25},{25,17},{2,10},{10... | collective-permute-start | bytes 196616 | tf_op jit(solution)/shard_map/ppermute | solution.py:397
  109.2 3.7 %copy-start.12 = (bf16[128,256]{1,0:T(8,128)(2,1)}, bf16[128,256]{1,0:T(8,128)(2,1)S(1)}, u32[]{:S(2)}) copy-start(bf16[128,256]{1,0:T(8,128)(2,1)S(1)} %collective-permute-done.23.refs_2_) | copy-start | bytes 196612
  110.1 2.9 %copy-start.13 = (bf16[128,256]{1,0:T(8,128)(2,1)}, bf16[128,256]{1,0:T(8,128)(2,1)S(1)}, u32[]{:S(2)}) copy-start(bf16[128,256]{1,0:T(8,128)(2,1)S(1)} %collective-permute-done.22.refs_1_) | copy-start | bytes 196612
  111.4 1.6 %copy-start.14 = (bf16[128,256]{1,0:T(8,128)(2,1)}, bf16[128,256]{1,0:T(8,128)(2,1)S(1)}, u32[]{:S(2)}) copy-start(bf16[128,256]{1,0:T(8,128)(2,1)S(1)} %collective-permute-done.27.refs_7_) | copy-start | bytes 196612
  112.5 0.6 copy-start.15
  113.0 0.6 copy-start.16

commit v3 on v2

--- a/solution.py
+++ b/solution.py
@@ -119,7 +119,6 @@
 
     out = pltpu.HBM((size, blocks * WIDE), jnp.bfloat16)
     tall = frame_count * rows
-    flops = 2 * steps * tall * order_count * (3 * nlon // 4 + 2 * WIDE + order_count)
     in_vmem = pl.BlockSpec(memory_space=pltpu.VMEM)
     return pl.pallas_call(
         transform_kernel,
@@ -255,26 +254,23 @@
     return x
 
 
-def contract_kernel(g, half, last, nlat, lanes_at, here_ref, *refs):
-    z_refs, (parity_ref, p_ref), refs = refs[:nlat], refs[nlat : nlat + 2], refs[nlat + 2 :]
-    acc_ref = refs[0] if len(refs) == 4 else None
-    out_ref, z_all, w_ref = refs[-3:]
-    step = pl.program_id(0)
+def contract_kernel(halves, last, has_acc, nlat, span, lanes_at, here_ref, *refs):
+    z_refs, parity_ref, p_refs = refs[:nlat], refs[nlat], refs[nlat + 1 : nlat + 3]
+    refs = refs[nlat + 3 :]
+    acc_refs, refs = (refs[:2], refs[2:]) if has_acc else ((), refs)
+    out_refs, (z_all, *w_refs) = refs[:-3], refs[-3:]
     lanes = z_all.shape[2]
-    span = out_ref.shape[-1] if last else out_ref.shape[0]
-
-    @pl.when(step == 0)
-    def _():
-        for n, z_ref in enumerate(z_refs):
-            z_all[n] = z_ref[...]
-
-        def source(s):
-            return z_all[s ^ here_ref[0]].astype(jnp.float32)[g * GROUP : (g + 1) * GROUP]
-
+    for n, z_ref in enumerate(z_refs):
+        z_all[n] = z_ref[...]
+
+    def source(s, g):
+        return z_all[s ^ here_ref[0]].astype(jnp.float32)[g * GROUP : (g + 1) * GROUP]
+
+    for g, w_ref in enumerate(w_refs):
         for part, sign in ((0, 1.0), (1, -1.0)):
             pieces = []
             for s in range(g * nlat // 4, nlat // 2):
-                both = source(s) + sign * source(nlat - 1 - s)
+                both = source(s, g) + sign * source(nlat - 1 - s, g)
                 pieces += [both[:, i : i + 128] for i in range(0, lanes, 128)]
             block = swap_groups(jnp.stack(pieces, axis=0))
             w_ref[:, part * 128 : (part + 1) * 128] = block.reshape(
@@ -283,14 +279,15 @@
 
     sub = lax.broadcasted_iota(jnp.int32, (GROUP, 128), 0)
     lane = lax.broadcasted_iota(jnp.int32, (GROUP, 128), 1) // EF
-    odd = [((parity_ref[...] + u) & 1) == 1 for u in range(2)]
-
-    def own_columns(first):
-        tile = 4 * GROUP * GROUP
+
+    def own_columns(g, first):
+        odd = [((parity_ref[g] + u) & 1) == 1 for u in range(2)]
+        many = 16 if span % 128 == 0 else 4
+        tile = many * GROUP * GROUP
         out = []
         for i in range(0, span * GROUP, tile):
-            rows = p_ref[pl.ds(first + i, tile), lanes_at : lanes_at + w_ref.shape[0]]
-            full = product(rows, w_ref[...]).reshape(4, GROUP, GROUP, 256)
+            rows = p_refs[g][pl.ds(first + i, tile), lanes_at[g] : lanes_at[g] + w_refs[g].shape[0]]
+            full = product(rows, w_refs[g][...]).reshape(many, GROUP, GROUP, 256)
             kept = None
             for n in range(GROUP):
                 one = jnp.where(odd[n % 2], full[:, n, :, 128:], full[:, n, :, :128])
@@ -300,73 +297,77 @@
                     kept = jnp.where(((sub - lane) & 7) == n, pltpu.roll(one, n, 1), kept)
             for bit in (1, 2, 4):
                 kept = jnp.where((lane & bit) != 0, pltpu.roll(kept, GROUP - bit, 1), kept)
-            out.append(kept.reshape(4 * GROUP, 128))
+            out.append(kept.reshape(many * GROUP, 128))
         return jnp.concatenate(out, axis=0)
 
-    def run():
-        value = own_columns(pl.multiple_of((step - half) * span * GROUP, 256))
-        if acc_ref is not None:
-            value = value + acc_ref[...]
-        if last:
-            out_ref[0] = value.T.astype(out_ref.dtype)
-        else:
-            out_ref[...] = value
-
-    if half:
-
-        @pl.when(step < half)
-        def _():
-            out_ref[...] = jnp.zeros_like(out_ref)
-
-        pl.when(step >= half)(run)
-    else:
-        run()
-
-
-def contract_chunk(g, last, here, z, parity, p, lanes_at, lanes, acc, begin, ntm):
+    def put(step, g, value):
+        per = out_refs[0].shape[1] // span
+        for offset, out_ref in enumerate(out_refs):
+            for i in range(per):
+
+                @pl.when(((step // per) ^ here_ref[1] == offset) & (step % per == i))
+                def _():
+                    out_ref[g * 128 : (g + 1) * 128, i * span : (i + 1) * span] = value
+
+    for g, half in enumerate(halves):
+        if last and half:
+
+            @pl.loop(0, half)
+            def _(step):
+                put(step, g, jnp.zeros((128, span), jnp.bfloat16))
+
+        @pl.loop(half, L // span)
+        def _(step):
+            value = own_columns(g, pl.multiple_of((step - half) * span * GROUP, 256))
+            at = pl.ds(pl.multiple_of((step - half) * span, span), span)
+            if has_acc:
+                value = value + acc_refs[g][at, :]
+            if last:
+                put(step, g, value.T.astype(jnp.bfloat16))
+            else:
+                out_refs[g][at, :] = value
+
+
+def contract_chunk(last, here, z, parity, p, lanes_at, lanes, acc, begins, ntm):
     each = L // ntm
     span = min(SPAN_OUT, each)
-    half = begin // span if last else 0
     if last:
-        steps = L // span
-        per = each // span
-        out_shape = jax.ShapeDtypeStruct((ntm, 128, each), jnp.bfloat16)
-        out_spec = pl.BlockSpec(
-            (1, 128, span), lambda s, here_ref: ((s // per) ^ here_ref[1], 0, s % per)
-        )
+        out_shape = [jax.ShapeDtypeStruct((256, each), jnp.bfloat16)] * ntm
     else:
-        steps = (L - begin) // span
-        out_shape = jax.ShapeDtypeStruct((L - begin, 128), jnp.float32)
-        out_spec = pl.BlockSpec((span, 128), lambda s, _: (s, 0))
-    acc_spec = pl.BlockSpec((span, 128), lambda s, _: (jnp.maximum(s - half, 0), 0))
+        out_shape = [jax.ShapeDtypeStruct((L - begin, 128), jnp.float32) for begin in begins]
+
+    def whole(x):
+        return pl.BlockSpec(x.shape, lambda s, _: (0,) * len(x.shape))
+
+    halves = [begin // span for begin in begins]
     return pl.pallas_call(
-        partial(contract_kernel, g, half, last, len(z), lanes_at),
+        partial(contract_kernel, halves, last, bool(acc), len(z), span, lanes_at),
         grid_spec=pltpu.PrefetchScalarGridSpec(
             num_scalar_prefetch=1,
-            grid=(steps,),
-            in_specs=[pl.BlockSpec(x.shape, lambda s, _: (0, 0)) for x in z]
-            + [pl.BlockSpec(parity.shape, lambda s, _: (0, 0))]
-            + [pl.BlockSpec(memory_space=pltpu.VMEM)]
-            + [acc_spec] * (acc is not None),
-            out_specs=out_spec,
+            grid=(1,),
+            in_specs=[whole(x) for x in (*z, parity)]
+            + [pl.BlockSpec(memory_space=pltpu.VMEM)] * 2
+            + [whole(x) for x in acc],
+            out_specs=[whole(x) for x in out_shape],
             scratch_shapes=[
                 pltpu.VMEM((len(z),) + z[0].shape, jnp.bfloat16),
-                pltpu.VMEM((lanes, 256), jnp.bfloat16),
+                *(pltpu.VMEM((n, 256), jnp.bfloat16) for n in lanes),
             ],
         ),
         out_shape=out_shape,
         compiler_params=pltpu.CompilerParams(vmem_limit_bytes=VMEM_SUM),
         cost_estimate=SHORT,
         name="latitude_sum",
-    )(here, *z, parity, p, *([acc] if acc is not None else []))
+    )(here, *z, parity, *p, *acc)
 
 
 def arrange_kernel(owned, here_ref, orders_ref, *refs):
     out_ref = refs[-1]
-    count = (len(refs) - 1) // 2
+    count = len(refs) - 1
     for offset in range(count):
         source = offset ^ here_ref[1]
-        low, high = (refs[g * count + offset][...].astype(jnp.float32) for g in range(2))
+        sums = refs[offset][...].astype(jnp.float32)
+        low, high = sums[:128], sums[128:]
         for i in range(owned):
             first = orders_ref[((here_ref[0] * count + source) * owned + i) * 2]
             in_order = first < orders_ref.shape[0] // 2
@@ -377,19 +378,19 @@
                 out_ref[e, slot + 1] = jnp.where(in_order, b, a)
 
 
-def arrange(here, owner_map, low, high, owned):
-    ntm, each = len(low), low[0].shape[1]
+def arrange(here, owner_map, sums, owned):
+    ntm, each = len(sums), sums[0].shape[1]
     return pl.pallas_call(
         partial(arrange_kernel, owned),
         grid_spec=pltpu.PrefetchScalarGridSpec(
             num_scalar_prefetch=2,
             grid=(1,),
-            in_specs=[pl.BlockSpec((128, each), lambda s, h, f: (0, 0))] * (2 * ntm),
+            in_specs=[pl.BlockSpec((256, each), lambda s, h, f: (0, 0))] * ntm,
             out_specs=pl.BlockSpec((2, ntm * owned * 2, F, each), lambda s, h, f: (0, 0, 0, 0)),
         ),
         out_shape=jax.ShapeDtypeStruct((2, ntm * owned * 2, F, each), jnp.float32),
         name="slot_order",
-    )(here, owner_map, *low, *high)
+    )(here, owner_map, *sums)
 
 
 def swap_with(x, axis, offset):
@@ -422,7 +423,7 @@
 
 def in_columns(kernel, name, arrays, out_rows, out_types, early=()):
     width = arrays[0].shape[1]
-    lanes = min(2048, width)
+    lanes = width
 
     def spec(rows):
         return pl.BlockSpec((rows, lanes), lambda i: (0, i))
@@ -485,9 +486,10 @@
     return x.transpose(order).reshape(-1)
 
 
-def exchange(band, owned):
-    out = []
-    for offset, piece in enumerate(band):
+def exchange(band, owned, offsets):
+    out = {}
+    for offset in offsets:
+        piece = band[offset]
         if offset:
             piece = swap_with(piece, "lat", offset)
         if owned < GROUP:
@@ -495,8 +497,8 @@
             piece = jnp.pad(
                 piece.reshape(2, owned, width), ((0, 0), (0, GROUP - owned), (0, 0))
             ).reshape(2 * GROUP, width)
-        out.append(piece)
-    return out
+        out[offset] = piece
+    return [out[offset] for offset in sorted(out)]
 
 
 def shards(frames, owner_map):
@@ -549,22 +551,20 @@
             early = [token for _, token in made]
         band, sent = reduce_over_time(piece, bits_a, bits_b, nlat, early)
         waits = [sent, pieces[-1][0]]
-        bands.append(exchange(band, owned))
-    lanes_at, acc = [0, 0], [None, None]
-    spectra = []
+        bands.append(band)
+    lanes_at, acc = (0, 0), ()
     for i, (band, (_, blocks)) in enumerate(zip(bands, parts)):
-        last = i == len(parts) - 1
-        if i:
-            band = [after(band[0], *acc)] + band[1:]
-        for g in (1, 0):
-            lanes = (nlat // 2 - g * nlat // 4) * blocks * ROWS
-            acc[g] = contract_chunk(
-                g, last, here, band, parity[g], made[g][0], lanes_at[g], lanes, acc[g],
-                g * order_count // 2, ntm,
-            )
-            lanes_at[g] += lanes
-    spectra = [[x[0]] + [swap_with(x[d], "tm", d) for d in range(1, ntm)] for x in acc]
-    return arrange(here, owner_map, *spectra, owned)
+        band = exchange(band, owned, range(nlat - 1, -1, -1))
+        if acc:
+            band = [after(band[0], *acc), *band[1:]]
+        lanes = [(nlat // 2 - g * nlat // 4) * blocks * ROWS for g in range(2)]
+        acc = contract_chunk(
+            i == len(parts) - 1, here, band, parity, [m[0] for m in made], lanes_at, lanes,
+            acc, (0, order_count // 2), ntm,
+        )
+        lanes_at = tuple(x + y for x, y in zip(lanes_at, lanes))
+    sums = [acc[0]] + [swap_with(acc[d], "tm", d) for d in range(1, ntm)]
+    return arrange(here, owner_map, sums, owned)
 
 
 def solution(mesh):

time: 117 us -> 116 us (level)
  starting transfers between devices: 38.7 us -> 35.3 us
  waiting for transfers between devices: 6.9 us -> 9.81 us
    ppermute x28 -> x25, starting transfers between devices: 38.7 us -> 35.3 us  [swap_with(): return lax.ppermute(x, axis, [(i, i ^ offset) for i in range(count)])]
    ppermute x28 -> x25, waiting for transfers between devices: 6.9 us -> 9.81 us  [swap_with(): return lax.ppermute(x, axis, [(i, i ^ offset) for i in range(count)])]
    pallas_call x4 -> x2, Pallas kernels: 13.9 us -> 12.5 us  [contract_chunk(): pl.pallas_call(partial(contract_kernel, halves, last, bool(acc), len(z),...]
    squeeze x2 -> x0, local copies, waits for them, and re-layouts: 1.28 us -> none  [shards(): x[d]]
    pallas_call x4, Pallas kernels: 0.65 us -> 1.82 us  [in_columns(): pl.pallas_call(kernel, grid=(width // lanes,), in_specs=[spec(x.shape[0])...]
    unnamed x35 -> x31, local copies, waits for them, and re-layouts: 6.41 us -> 7.12 us
  transfers between devices with their start and end apart: 28 -> 25, of which waited for: 6 -> 4; matrix products, arithmetic and copies ran while one was open for 1% -> 0% of each run, Pallas kernels for 31% -> 30%
where the time goes in v3:
time: 116 us; the launch traced here: 115 us
  Pallas kernels  59.4 us (51%)
  starting transfers between devices  35.3 us (30%)
  waiting for transfers between devices  9.81 us (8%)
  local copies, waits for them, and re-layouts  8.45 us (7%)
  other arithmetic  1.78 us (2%)
    ppermute x25, starting transfers between devices, swap_with(): return lax.ppermute(x, axis, [(i, i ^ offset) for i in range(count)])  35.3 us
    pallas_call x2, Pallas kernels, transform_chunk(): pl.pallas_call(transform_kernel, grid_spec=pltpu.PrefetchScalarGridSpec(n...  31.7 us
    pallas_call x2, Pallas kernels, contract_chunk(): pl.pallas_call(partial(contract_kernel, halves, last, bool(acc), len(z),...  12.5 us
    pallas_call x2, Pallas kernels, polynomials(): pl.pallas_call(partial(polynomial_kernel, half, begin), grid=((L - begin)...  10.5 us
    ppermute x25, waiting for transfers between devices, swap_with(): return lax.ppermute(x, axis, [(i, i ^ offset) for i in range(count)])  9.81 us
    unnamed x31, local copies, waits for them, and re-layouts  7.12 us
    pallas_call x1, Pallas kernels, arrange(): pl.pallas_call(partial(arrange_kernel, owned), grid_spec=pltpu.PrefetchSc...  2.84 us
  transfers between devices with their start and end apart: 25, of which 4 were waited for; matrix products, arithmetic and copies ran while one was open for 0% of the time, Pallas kernels for 30%

profile of v3, /device:TPU:0, one launch (start us, length us, event | category | flops | bytes accessed | tf_op | source)
XLA Modules:
  0.0 115.1 jit_solution(13434384333844632419)
XLA Ops:
  0.0 0.8 reshape.207
  0.8 1.2 %fusion.9 = (s32[8,4,8]{2,1,0:T(4,128)S(1)}, s32[8,4,8]{2,1,0:T(4,128)S(1)}) fusion(s32[8,4,8,2]{3,2,1,0:T(8,128)S(1)} %reshape.207), kind=kLoop, calls=%fused_computation.42 | loop fusion | flops 512 | bytes 4096 | tf_op jit(solution)/shard_map/reduce_max | solution.py:516
  2.2 0.1 concatenate.39
  2.4 0.1 concatenate.38
  2.6 0.2 fusion.place_ref
  2.8 1.6 %copy-done = bf16[2048,512]{1,0:T(8,128)(2,1)S(1)} copy-done((bf16[2048,512]{1,0:T(8,128)(2,1)S(1)}, bf16[2048,512]{1,0:T(8,128)(2,1)}, u32[]{:S(2)}) %copy-start) | copy-done | bytes 2097176
  4.4 1.0 copy-done.1
  5.4 1.0 copy-done.2
  6.5 15.9 %longitude_time.2 = (bf16[128,2048]{1,0:T(8,128)(2,1)}, bf16[128,2048]{1,0:T(8,128)(2,1)}, bf16[128,2048]{1,0:T(8,128)(2,1)}, bf16[128,2048]{1,0:T(8,128)(2,1)}) custom-call(s32[2]{0:T(128)S(1)} %pad_add_fusion.2.where_ref, bf16[16,256,4096]{2,1,0:T(8,128)(2,1)} %frames_ref.3, bf16[1024,256]{1,0:T(8,128)(2,1)S(1)} %copy-done.2, ...), custom_call_target="tpu_custom_call" | custom-call | flops 1000000 | bytes 100000 | tf_op jit(solution)/shard_map/longitude_time/pallas_call | solution.py:123
  22.4 2.9 %collective-permute-start.2 = (bf16[128,2048]{1,0:T(8,128)(2,1)}, bf16[128,2048]{1,0:T(8,128)(2,1)S(1)}, u32[]{:S(2)}, u32[]{:S(2)}) collective-permute-start(bf16[128,2048]{1,0:T(8,128)(2,1)} %get-tuple-element.57), channel_id=1, source_target_pairs={{0,8},{8,0},{16,24},{24,16},{1,9},{9,1},{17,25},{25,17},{2,10},{10... | collective-permute-start | bytes 1572872 | tf_op jit(solution)/shard_map/ppermute | solution.py:398
  25.3 1.5 %collective-permute-start.3 = (bf16[128,2048]{1,0:T(8,128)(2,1)}, bf16[128,2048]{1,0:T(8,128)(2,1)S(1)}, u32[]{:S(2)}, u32[]{:S(2)}) collective-permute-start(bf16[128,2048]{1,0:T(8,128)(2,1)} %get-tuple-element.59), channel_id=1, source_target_pairs={{0,16},{8,24},{16,0},{24,8},{1,17},{9,25},{17,1},{25,9},{2,18},{10... | collective-permute-start | bytes 1572872 | tf_op jit(solution)/shard_map/ppermute | solution.py:398
  26.9 15.9 %longitude_time.3 = (bf16[128,2048]{1,0:T(8,128)(2,1)}, bf16[128,2048]{1,0:T(8,128)(2,1)}, bf16[128,2048]{1,0:T(8,128)(2,1)}, bf16[128,2048]{1,0:T(8,128)(2,1)}) custom-call(s32[2]{0:T(128)S(1)} %pad_add_fusion.2.where_ref, bf16[16,256,4096]{2,1,0:T(8,128)(2,1)} %frames_ref.3, bf16[1024,256]{1,0:T(8,128)(2,1)S(1)} %copy-done.2, ...), custom_call_target="tpu_custom_call" | custom-call | flops 1000000 | bytes 100000 | tf_op jit(solution)/shard_map/longitude_time/pallas_call | solution.py:123
  42.7 0.5 collective-permute-start
  43.3 0.1 dynamic-slice_reduce_fusion
  43.5 0.2 sum_step.2
  43.7 2.0 %collective-permute-start.7 = (bf16[64,2048]{1,0:T(8,128)(2,1)S(1)}, bf16[64,2048]{1,0:T(8,128)(2,1)S(1)}, u32[]{:S(2)}, u32[]{:S(2)}) collective-permute-start(bf16[64,2048]{1,0:T(8,128)(2,1)S(1)} %get-tuple-element.72), channel_id=1, source_target_pairs={{0,8},{8,0},{16,24},{24,16},{1,9},{9,1},{17,25},{25,17},{2,10},{10... | collective-permute-start | bytes 786440 | tf_op jit(solution)/shard_map/ppermute | solution.py:398
  45.7 1.5 %collective-permute-start.6 = (bf16[64,2048]{1,0:T(8,128)(2,1)S(1)}, bf16[64,2048]{1,0:T(8,128)(2,1)S(1)}, u32[]{:S(2)}, u32[]{:S(2)}) collective-permute-start(bf16[64,2048]{1,0:T(8,128)(2,1)S(1)} %get-tuple-element.60), channel_id=1, source_target_pairs={{0,16},{8,24},{16,0},{24,8},{1,17},{9,25},{17,1},{25,9},{2,18},{10... | collective-permute-start | bytes 786440 | tf_op jit(solution)/shard_map/ppermute | solution.py:398
  47.3 3.6 %legendre.3 = (bf16[6144,512]{1,0:T(8,128)(2,1)S(1)}, f32[8,128]{1,0:T(8,128)S(1)}) custom-call(f32[8,128]{1,0:T(8,128)S(1)} %broadcast_in_dim.7.orders_ref, f32[1,512]{1,0:T(1,128)S(1)} %copy-done.10, f32[3,512]{1,0:T(4,128)S(1)} %copy-done.9), custom_call_target="tpu_custom_call" | custom-call | flops 1000000 | bytes 100000 | tf_op jit(solution)/shard_map/legendre/pallas_call | solution.py:230
  51.0 6.9 %legendre.2 = (bf16[8192,1024]{1,0:T(8,128)(2,1)S(1)}, f32[8,128]{1,0:T(8,128)S(1)}) custom-call(f32[8,128]{1,0:T(8,128)S(1)} %broadcast_in_dim.6.orders_ref, f32[1,512]{1,0:T(1,128)S(1)} %copy-done.10, f32[3,1024]{1,0:T(4,128)S(1)} %copy-done.8), custom_call_target="tpu_custom_call" | custom-call | flops 1000000 | bytes 100000 | tf_op jit(solution)/shard_map/legendre/pallas_call | solution.py:230
  58.0 0.5 collective-permute-done.1.got_b
  58.4 1.0 copy-done.3
  59.5 1.0 copy-done.4
  60.5 1.4 %sum_step.3 = (f32[64,2048]{1,0:T(8,128)S(1)}, bf16[64,2048]{1,0:T(8,128)(2,1)S(1)}, f32[64,2048]{1,0:T(8,128)S(1)}, bf16[64,2048]{1,0:T(8,128)(2,1)S(1)}) custom-call(bf16[128,2048]{1,0:T(8,128)(2,1)S(1)} %copy-done.3, bf16[128,2048]{1,0:T(8,128)(2,1)} %collective-permute-done.got_a, bf16[128,2048]{1,0:T(8,128)(2,1)S(1)} %copy-done.4, ...), custom_call_target="tpu_custom_call" | custom-call | flops 1000000 | bytes 100000 | tf_op jit(solution)/shard_map/sum_step/pallas_call | solution.py:431
  61.9 0.1 collective-permute-start.4
  62.1 1.9 %collective-permute-start.5 = (bf16[64,2048]{1,0:T(8,128)(2,1)S(1)}, bf16[64,2048]{1,0:T(8,128)(2,1)S(1)}, u32[]{:S(2)}, u32[]{:S(2)}) collective-permute-start(bf16[64,2048]{1,0:T(8,128)(2,1)S(1)} %get-tuple-element.68), channel_id=1, source_target_pairs={{0,8},{8,0},{16,24},{24,16},{1,9},{9,1},{17,25},{25,17},{2,10},{10... | collective-permute-start | bytes 786440 | tf_op jit(solution)/shard_map/ppermute | solution.py:398
  64.0 0.1 sum_end.3
  64.2 1.6 %collective-permute-start.9 = (bf16[16,2048]{1,0:T(8,128)(2,1)S(1)}, bf16[16,2048]{1,0:T(8,128)(2,1)S(1)}, u32[]{:S(2)}, u32[]{:S(2)}) collective-permute-start(bf16[16,2048]{1,0:T(8,128)(2,1)S(1)} %get-tuple-element.75), channel_id=1, source_target_pairs={{0,2},{1,3},{2,0},{3,1},{4,6},{5,7},{6,4},{7,5},{8,10},{9,11},{10,... | collective-permute-start | bytes 196616 | tf_op jit(solution)/shard_map/ppermute | solution.py:398
  65.8 0.2 collective-permute-start.10
  66.0 2.3 %collective-permute-done.4.got_a = bf16[64,2048]{1,0:T(8,128)(2,1)S(1)} collective-permute-done((bf16[64,2048]{1,0:T(8,128)(2,1)S(1)}, bf16[64,2048]{1,0:T(8,128)(2,1)S(1)}, u32[]{:S(2)}, u32[]{:S(2)}) %collective-permute-start.4) | collective-permute-done | bytes 262176 | tf_op jit(solution)/shard_map/ppermute | solution.py:398
  68.4 2.6 %collective-permute-start.11 = (bf16[16,2048]{1,0:T(8,128)(2,1)S(1)}, bf16[16,2048]{1,0:T(8,128)(2,1)S(1)}, u32[]{:S(2)}, u32[]{:S(2)}) collective-permute-start(bf16[16,2048]{1,0:T(8,128)(2,1)S(1)} %get-tuple-element.77), channel_id=1, source_target_pairs={{0,4},{1,5},{2,6},{3,7},{4,0},{5,1},{6,2},{7,3},{8,12},{9,13},{10,... | collective-permute-start | bytes 196616 | tf_op jit(solution)/shard_map/ppermute | solution.py:398
  71.1 1.6 %collective-permute-start.13 = (bf16[16,2048]{1,0:T(8,128)(2,1)S(1)}, bf16[16,2048]{1,0:T(8,128)(2,1)S(1)}, u32[]{:S(2)}, u32[]{:S(2)}) collective-permute-start(bf16[16,2048]{1,0:T(8,128)(2,1)S(1)} %get-tuple-element.79), channel_id=1, source_target_pairs={{0,6},{1,7},{2,4},{3,5},{4,2},{5,3},{6,0},{7,1},{8,14},{9,15},{10,... | collective-permute-start | bytes 196616 | tf_op jit(solution)/shard_map/ppermute | solution.py:398
  72.7 2.2 %collective-permute-start.14 = (bf16[16,2048]{1,0:T(8,128)(2,1)S(1)}, bf16[16,2048]{1,0:T(8,128)(2,1)S(1)}, u32[]{:S(2)}, u32[]{:S(2)}) collective-permute-start(bf16[16,2048]{1,0:T(8,128)(2,1)S(1)} %get-tuple-element.80), channel_id=1, source_target_pairs={{0,7},{1,6},{2,5},{3,4},{4,3},{5,2},{6,1},{7,0},{8,15},{9,14},{10,... | collective-permute-start | bytes 196616 | tf_op jit(solution)/shard_map/ppermute | solution.py:398
  74.9 0.2 collective-permute-start.15
  75.1 4.7 %collective-permute-start.16 = (bf16[16,2048]{1,0:T(8,128)(2,1)S(1)}, bf16[16,2048]{1,0:T(8,128)(2,1)S(1)}, u32[]{:S(2)}, u32[]{:S(2)}) collective-permute-start(bf16[16,2048]{1,0:T(8,128)(2,1)S(1)} %get-tuple-element.87), channel_id=1, source_target_pairs={{0,2},{1,3},{2,0},{3,1},{4,6},{5,7},{6,4},{7,5},{8,10},{9,11},{10,... | collective-permute-start | bytes 196616 | tf_op jit(solution)/shard_map/ppermute | solution.py:398
  79.9 4.6 %collective-permute-start.18 = (bf16[16,2048]{1,0:T(8,128)(2,1)S(1)}, bf16[16,2048]{1,0:T(8,128)(2,1)S(1)}, u32[]{:S(2)}, u32[]{:S(2)}) collective-permute-start(bf16[16,2048]{1,0:T(8,128)(2,1)S(1)} %get-tuple-element.89), channel_id=1, source_target_pairs={{0,4},{1,5},{2,6},{3,7},{4,0},{5,1},{6,2},{7,3},{8,12},{9,13},{10,... | collective-permute-start | bytes 196616 | tf_op jit(solution)/shard_map/ppermute | solution.py:398
  84.5 0.4 collective-permute-start.19
  84.9 2.2 %collective-permute-start.20 = (bf16[16,2048]{1,0:T(8,128)(2,1)S(1)}, bf16[16,2048]{1,0:T(8,128)(2,1)S(1)}, u32[]{:S(2)}, u32[]{:S(2)}) collective-permute-start(bf16[16,2048]{1,0:T(8,128)(2,1)S(1)} %get-tuple-element.91), channel_id=1, source_target_pairs={{0,6},{1,7},{2,4},{3,5},{4,2},{5,3},{6,0},{7,1},{8,14},{9,15},{10,... | collective-permute-start | bytes 196616 | tf_op jit(solution)/shard_map/ppermute | solution.py:398
  87.2 0.6 collective-permute-start.21
  87.9 6.0 %latitude_sum.2 = (f32[1024,128]{1,0:T(8,128)S(1)}, f32[768,128]{1,0:T(8,128)S(1)}) custom-call(s32[2]{0:T(128)S(1)} %pad_add_fusion.1.here_ref, bf16[16,2048]{1,0:T(8,128)(2,1)S(1)} %get-tuple-element.73.refs_0_, bf16[16,2048]{1,0:T(8,128)(2,1)S(1)} %collective-permute-done.8.refs_1_, bf16[16,2048]{1,0:T(8,128)(2,1)S(1)} %collective-permute-done.9.refs_2_, ...), custom_call_target="tpu_custom_call" | custom-call | flops 1000000 | bytes 100000 | tf_op jit(solution)/shard_map/latitude_sum/pallas_call | solution.py:343
  94.0 6.5 %latitude_sum.3 = (bf16[256,256]{1,0:T(8,128)(2,1)S(1)}, bf16[256,256]{1,0:T(8,128)(2,1)S(1)}, bf16[256,256]{1,0:T(8,128)(2,1)S(1)}, bf16[256,256]{1,0:T(8,128)(2,1)S(1)}) custom-call(s32[2]{0:T(128)S(1)} %pad_add_fusion.1.here_ref, bf16[16,2048]{1,0:T(8,128)(2,1)S(1)} %get-tuple-element.85.refs_0_, bf16[16,2048]{1,0:T(8,128)(2,1)S(1)} %collective-permute-done.15.refs_1_, ...), custom_call_target="tpu_custom_call" | custom-call | flops 1000000 | bytes 100000 | tf_op jit(solution)/shard_map/latitude_sum/pallas_call | solution.py:343
  100.5 0.6 copy-done.7
  101.1 1.5 %collective-permute-start.22 = (bf16[256,256]{1,0:T(8,128)(2,1)S(1)}, bf16[256,256]{1,0:T(8,128)(2,1)S(1)}, u32[]{:S(2)}, u32[]{:S(2)}) collective-permute-start(bf16[256,256]{1,0:T(8,128)(2,1)S(1)} %get-tuple-element.94), channel_id=1, source_target_pairs={{0,8},{8,0},{16,24},{24,16},{1,9},{9,1},{17,25},{25,17},{2,10},{10... | collective-permute-start | bytes 393224 | tf_op jit(solution)/shard_map/ppermute | solution.py:398
  102.6 0.7 collective-permute-start.23
  103.2 1.4 %collective-permute-start.24 = (bf16[256,256]{1,0:T(8,128)(2,1)S(1)}, bf16[256,256]{1,0:T(8,128)(2,1)S(1)}, u32[]{:S(2)}, u32[]{:S(2)}) collective-permute-start(bf16[256,256]{1,0:T(8,128)(2,1)S(1)} %get-tuple-element.96), channel_id=1, source_target_pairs={{0,24},{8,16},{16,8},{24,0},{1,25},{9,17},{17,9},{25,1},{2,26},{10... | collective-permute-start | bytes 393224 | tf_op jit(solution)/shard_map/ppermute | solution.py:398
  104.6 2.8 %collective-permute-done.22.refs_1_ = bf16[256,256]{1,0:T(8,128)(2,1)S(1)} collective-permute-done((bf16[256,256]{1,0:T(8,128)(2,1)S(1)}, bf16[256,256]{1,0:T(8,128)(2,1)S(1)}, u32[]{:S(2)}, u32[]{:S(2)}) %collective-permute-start.22) | collective-permute-done | bytes 131104 | tf_op jit(solution)/shard_map/ppermute | solution.py:398
  107.4 4.2 %collective-permute-done.23.refs_2_ = bf16[256,256]{1,0:T(8,128)(2,1)S(1)} collective-permute-done((bf16[256,256]{1,0:T(8,128)(2,1)S(1)}, bf16[256,256]{1,0:T(8,128)(2,1)S(1)}, u32[]{:S(2)}, u32[]{:S(2)}) %collective-permute-start.23) | collective-permute-done | bytes 131104 | tf_op jit(solution)/shard_map/ppermute | solution.py:398
  111.6 0.6 copy-done.13
  112.3 2.8 %slot_order.1 = f32[2,64,8,256]{3,2,1,0:T(8,128)} custom-call(s32[2]{0:T(128)} %copy-done.11, s32[512]{0:T(512)} %orders_ref.1, bf16[256,256]{1,0:T(8,128)(2,1)} %copy-done.7, bf16[256,256]{1,0:T(8,128)(2,1)} %copy-done.12, bf16[256,256]{1,0:T(8,128)(2,1)} %copy-done.13, bf16[256,256]{1,0:T(8,128)(2,1)} %copy-done.14), custom_call_target="tpu_custom_call" | custom-call | tf_op jit(solution)/shard_map/slot_order/pallas_call | solution.py:383
  (75 shorter events, 1.0 us)
Async XLA Ops:
  2.8 1.6 %copy-start = (bf16[2048,512]{1,0:T(8,128)(2,1)S(1)}, bf16[2048,512]{1,0:T(8,128)(2,1)}, u32[]{:S(2)}) copy-start(bf16[2048,512]{1,0:T(8,128)(2,1)} %constant.89.clone.odd_ref) | copy-start | bytes 6291460
  4.4 1.0 copy-start.1
  5.4 1.0 copy-start.2
  22.4 21.1 %collective-permute-start.2 = (bf16[128,2048]{1,0:T(8,128)(2,1)}, bf16[128,2048]{1,0:T(8,128)(2,1)S(1)}, u32[]{:S(2)}, u32[]{:S(2)}) collective-permute-start(bf16[128,2048]{1,0:T(8,128)(2,1)} %get-tuple-element.57), channel_id=1, source_target_pairs={{0,8},{8,0},{16,24},{24,16},{1,9},{9,1},{17,25},{25,17},{2,10},{10... | collective-permute-start | bytes 1572872 | tf_op jit(solution)/shard_map/ppermute | solution.py:398
  25.3 18.1 %collective-permute-start.3 = (bf16[128,2048]{1,0:T(8,128)(2,1)}, bf16[128,2048]{1,0:T(8,128)(2,1)S(1)}, u32[]{:S(2)}, u32[]{:S(2)}) collective-permute-start(bf16[128,2048]{1,0:T(8,128)(2,1)} %get-tuple-element.59), channel_id=1, source_target_pairs={{0,16},{8,24},{16,0},{24,8},{1,17},{9,25},{17,1},{25,9},{2,18},{10... | collective-permute-start | bytes 1572872 | tf_op jit(solution)/shard_map/ppermute | solution.py:398
  26.8 16.6 %copy-start.5 = (bf16[128,2048]{1,0:T(8,128)(2,1)S(1)}, bf16[128,2048]{1,0:T(8,128)(2,1)}, u32[]{:S(2)}) copy-start(bf16[128,2048]{1,0:T(8,128)(2,1)} %get-tuple-element.51.keep_a) | copy-start | bytes 1572868
  26.8 16.6 %copy-start.6 = (bf16[128,2048]{1,0:T(8,128)(2,1)S(1)}, bf16[128,2048]{1,0:T(8,128)(2,1)}, u32[]{:S(2)}) copy-start(bf16[128,2048]{1,0:T(8,128)(2,1)} %get-tuple-element.58.keep_b) | copy-start | bytes 1572868
  26.8 20.5 %copy-start.9 = (f32[3,512]{1,0:T(4,128)S(1)}, f32[3,512]{1,0:T(4,128)}, u32[]{:S(2)}) copy-start(f32[3,512]{1,0:T(4,128)} %constant.93.clone.rows_ref) | copy-start | bytes 18436
  26.8 20.5 %copy-start.10 = (f32[1,512]{1,0:T(1,128)S(1)}, f32[1,512]{1,0:T(1,128)}, u32[]{:S(2)}) copy-start(f32[1,512]{1,0:T(1,128)} %constant.91.clone.growth_ref) | copy-start | bytes 6148
  26.9 24.2 %copy-start.8 = (f32[3,1024]{1,0:T(4,128)S(1)}, f32[3,1024]{1,0:T(4,128)}, u32[]{:S(2)}) copy-start(f32[3,1024]{1,0:T(4,128)} %constant.92.clone.rows_ref) | copy-start | bytes 36868
  42.7 15.2 %collective-permute-start = (bf16[128,2048]{1,0:T(8,128)(2,1)}, bf16[128,2048]{1,0:T(8,128)(2,1)}, u32[]{:S(2)}, u32[]{:S(2)}) collective-permute-start(bf16[128,2048]{1,0:T(8,128)(2,1)} %get-tuple-element.54), channel_id=1, source_target_pairs={{0,8},{8,0},{16,24},{24,16},{1,9},{9,1},{17,25},{25,17},{2,10},{10... | collective-permute-start | bytes 1572872 | tf_op jit(solution)/shard_map/ppermute | solution.py:398
  43.2 15.2 %collective-permute-start.1 = (bf16[128,2048]{1,0:T(8,128)(2,1)}, bf16[128,2048]{1,0:T(8,128)(2,1)}, u32[]{:S(2)}, u32[]{:S(2)}) collective-permute-start(bf16[128,2048]{1,0:T(8,128)(2,1)} %get-tuple-element.56), channel_id=1, source_target_pairs={{0,16},{8,24},{16,0},{24,8},{1,17},{9,25},{17,1},{25,9},{2,18},{10... | collective-permute-start | bytes 1572872 | tf_op jit(solution)/shard_map/ppermute | solution.py:398
  43.7 20.3 %collective-permute-start.7 = (bf16[64,2048]{1,0:T(8,128)(2,1)S(1)}, bf16[64,2048]{1,0:T(8,128)(2,1)S(1)}, u32[]{:S(2)}, u32[]{:S(2)}) collective-permute-start(bf16[64,2048]{1,0:T(8,128)(2,1)S(1)} %get-tuple-element.72), channel_id=1, source_target_pairs={{0,8},{8,0},{16,24},{24,16},{1,9},{9,1},{17,25},{25,17},{2,10},{10... | collective-permute-start | bytes 786440 | tf_op jit(solution)/shard_map/ppermute | solution.py:398
  45.7 18.3 %collective-permute-start.6 = (bf16[64,2048]{1,0:T(8,128)(2,1)S(1)}, bf16[64,2048]{1,0:T(8,128)(2,1)S(1)}, u32[]{:S(2)}, u32[]{:S(2)}) collective-permute-start(bf16[64,2048]{1,0:T(8,128)(2,1)S(1)} %get-tuple-element.60), channel_id=1, source_target_pairs={{0,16},{8,24},{16,0},{24,8},{1,17},{9,25},{17,1},{25,9},{2,18},{10... | collective-permute-start | bytes 786440 | tf_op jit(solution)/shard_map/ppermute | solution.py:398
  58.4 1.0 copy-start.3
  59.5 1.0 copy-start.4
  61.9 6.4 %collective-permute-start.4 = (bf16[64,2048]{1,0:T(8,128)(2,1)S(1)}, bf16[64,2048]{1,0:T(8,128)(2,1)S(1)}, u32[]{:S(2)}, u32[]{:S(2)}) collective-permute-start(bf16[64,2048]{1,0:T(8,128)(2,1)S(1)} %get-tuple-element.66), channel_id=1, source_target_pairs={{0,16},{8,24},{16,0},{24,8},{1,17},{9,25},{17,1},{25,9},{2,18},{10... | collective-permute-start | bytes 786440 | tf_op jit(solution)/shard_map/ppermute | solution.py:398
  62.1 8.9 %collective-permute-start.5 = (bf16[64,2048]{1,0:T(8,128)(2,1)S(1)}, bf16[64,2048]{1,0:T(8,128)(2,1)S(1)}, u32[]{:S(2)}, u32[]{:S(2)}) collective-permute-start(bf16[64,2048]{1,0:T(8,128)(2,1)S(1)} %get-tuple-element.68), channel_id=1, source_target_pairs={{0,8},{8,0},{16,24},{24,16},{1,9},{9,1},{17,25},{25,17},{2,10},{10... | collective-permute-start | bytes 786440 | tf_op jit(solution)/shard_map/ppermute | solution.py:398
  64.1 7.0 %collective-permute-start.8 = (bf16[16,2048]{1,0:T(8,128)(2,1)S(1)}, bf16[16,2048]{1,0:T(8,128)(2,1)S(1)}, u32[]{:S(2)}, u32[]{:S(2)}) collective-permute-start(bf16[16,2048]{1,0:T(8,128)(2,1)S(1)} %get-tuple-element.74), channel_id=1, source_target_pairs={{0,1},{1,0},{2,3},{3,2},{4,5},{5,4},{6,7},{7,6},{8,9},{9,8},{10,11... | collective-permute-start | bytes 196616 | tf_op jit(solution)/shard_map/ppermute | solution.py:398
  64.2 8.5 %collective-permute-start.9 = (bf16[16,2048]{1,0:T(8,128)(2,1)S(1)}, bf16[16,2048]{1,0:T(8,128)(2,1)S(1)}, u32[]{:S(2)}, u32[]{:S(2)}) collective-permute-start(bf16[16,2048]{1,0:T(8,128)(2,1)S(1)} %get-tuple-element.75), channel_id=1, source_target_pairs={{0,2},{1,3},{2,0},{3,1},{4,6},{5,7},{6,4},{7,5},{8,10},{9,11},{10,... | collective-permute-start | bytes 196616 | tf_op jit(solution)/shard_map/ppermute | solution.py:398
  65.8 9.1 %collective-permute-start.10 = (bf16[16,2048]{1,0:T(8,128)(2,1)S(1)}, bf16[16,2048]{1,0:T(8,128)(2,1)S(1)}, u32[]{:S(2)}, u32[]{:S(2)}) collective-permute-start(bf16[16,2048]{1,0:T(8,128)(2,1)S(1)} %get-tuple-element.76), channel_id=1, source_target_pairs={{0,3},{1,2},{2,1},{3,0},{4,7},{5,6},{6,5},{7,4},{8,11},{9,10},{10,... | collective-permute-start | bytes 196616 | tf_op jit(solution)/shard_map/ppermute | solution.py:398
  68.4 6.7 %collective-permute-start.11 = (bf16[16,2048]{1,0:T(8,128)(2,1)S(1)}, bf16[16,2048]{1,0:T(8,128)(2,1)S(1)}, u32[]{:S(2)}, u32[]{:S(2)}) collective-permute-start(bf16[16,2048]{1,0:T(8,128)(2,1)S(1)} %get-tuple-element.77), channel_id=1, source_target_pairs={{0,4},{1,5},{2,6},{3,7},{4,0},{5,1},{6,2},{7,3},{8,12},{9,13},{10,... | collective-permute-start | bytes 196616 | tf_op jit(solution)/shard_map/ppermute | solution.py:398
  71.0 8.8 %collective-permute-start.12 = (bf16[16,2048]{1,0:T(8,128)(2,1)S(1)}, bf16[16,2048]{1,0:T(8,128)(2,1)S(1)}, u32[]{:S(2)}, u32[]{:S(2)}) collective-permute-start(bf16[16,2048]{1,0:T(8,128)(2,1)S(1)} %get-tuple-element.78), channel_id=1, source_target_pairs={{0,5},{1,4},{2,7},{3,6},{4,1},{5,0},{6,3},{7,2},{8,13},{9,12},{10,... | collective-permute-start | bytes 196616 | tf_op jit(solution)/shard_map/ppermute | solution.py:398
  71.1 8.8 %collective-permute-start.13 = (bf16[16,2048]{1,0:T(8,128)(2,1)S(1)}, bf16[16,2048]{1,0:T(8,128)(2,1)S(1)}, u32[]{:S(2)}, u32[]{:S(2)}) collective-permute-start(bf16[16,2048]{1,0:T(8,128)(2,1)S(1)} %get-tuple-element.79), channel_id=1, source_target_pairs={{0,6},{1,7},{2,4},{3,5},{4,2},{5,3},{6,0},{7,1},{8,14},{9,15},{10,... | collective-permute-start | bytes 196616 | tf_op jit(solution)/shard_map/ppermute | solution.py:398
  72.7 11.8 %collective-permute-start.14 = (bf16[16,2048]{1,0:T(8,128)(2,1)S(1)}, bf16[16,2048]{1,0:T(8,128)(2,1)S(1)}, u32[]{:S(2)}, u32[]{:S(2)}) collective-permute-start(bf16[16,2048]{1,0:T(8,128)(2,1)S(1)} %get-tuple-element.80), channel_id=1, source_target_pairs={{0,7},{1,6},{2,5},{3,4},{4,3},{5,2},{6,1},{7,0},{8,15},{9,14},{10,... | collective-permute-start | bytes 196616 | tf_op jit(solution)/shard_map/ppermute | solution.py:398
  74.9 10.0 %collective-permute-start.15 = (bf16[16,2048]{1,0:T(8,128)(2,1)S(1)}, bf16[16,2048]{1,0:T(8,128)(2,1)S(1)}, u32[]{:S(2)}, u32[]{:S(2)}) collective-permute-start(bf16[16,2048]{1,0:T(8,128)(2,1)S(1)} %get-tuple-element.86), channel_id=1, source_target_pairs={{0,1},{1,0},{2,3},{3,2},{4,5},{5,4},{6,7},{7,6},{8,9},{9,8},{10,11... | collective-permute-start | bytes 196616 | tf_op jit(solution)/shard_map/ppermute | solution.py:398
  75.1 12.1 %collective-permute-start.16 = (bf16[16,2048]{1,0:T(8,128)(2,1)S(1)}, bf16[16,2048]{1,0:T(8,128)(2,1)S(1)}, u32[]{:S(2)}, u32[]{:S(2)}) collective-permute-start(bf16[16,2048]{1,0:T(8,128)(2,1)S(1)} %get-tuple-element.87), channel_id=1, source_target_pairs={{0,2},{1,3},{2,0},{3,1},{4,6},{5,7},{6,4},{7,5},{8,10},{9,11},{10,... | collective-permute-start | bytes 196616 | tf_op jit(solution)/shard_map/ppermute | solution.py:398
  79.8 14.1 %collective-permute-start.17 = (bf16[16,2048]{1,0:T(8,128)(2,1)S(1)}, bf16[16,2048]{1,0:T(8,128)(2,1)S(1)}, u32[]{:S(2)}, u32[]{:S(2)}) collective-permute-start(bf16[16,2048]{1,0:T(8,128)(2,1)S(1)} %get-tuple-element.88), channel_id=1, source_target_pairs={{0,3},{1,2},{2,1},{3,0},{4,7},{5,6},{6,5},{7,4},{8,11},{9,10},{10,... | collective-permute-start | bytes 196616 | tf_op jit(solution)/shard_map/ppermute | solution.py:398
  79.9 14.1 %collective-permute-start.18 = (bf16[16,2048]{1,0:T(8,128)(2,1)S(1)}, bf16[16,2048]{1,0:T(8,128)(2,1)S(1)}, u32[]{:S(2)}, u32[]{:S(2)}) collective-permute-start(bf16[16,2048]{1,0:T(8,128)(2,1)S(1)} %get-tuple-element.89), channel_id=1, source_target_pairs={{0,4},{1,5},{2,6},{3,7},{4,0},{5,1},{6,2},{7,3},{8,12},{9,13},{10,... | collective-permute-start | bytes 196616 | tf_op jit(solution)/shard_map/ppermute | solution.py:398
  84.5 9.5 %collective-permute-start.19 = (bf16[16,2048]{1,0:T(8,128)(2,1)S(1)}, bf16[16,2048]{1,0:T(8,128)(2,1)S(1)}, u32[]{:S(2)}, u32[]{:S(2)}) collective-permute-start(bf16[16,2048]{1,0:T(8,128)(2,1)S(1)} %get-tuple-element.90), channel_id=1, source_target_pairs={{0,5},{1,4},{2,7},{3,6},{4,1},{5,0},{6,3},{7,2},{8,13},{9,12},{10,... | collective-permute-start | bytes 196616 | tf_op jit(solution)/shard_map/ppermute | solution.py:398
  84.9 9.0 %collective-permute-start.20 = (bf16[16,2048]{1,0:T(8,128)(2,1)S(1)}, bf16[16,2048]{1,0:T(8,128)(2,1)S(1)}, u32[]{:S(2)}, u32[]{:S(2)}) collective-permute-start(bf16[16,2048]{1,0:T(8,128)(2,1)S(1)} %get-tuple-element.91), channel_id=1, source_target_pairs={{0,6},{1,7},{2,4},{3,5},{4,2},{5,3},{6,0},{7,1},{8,14},{9,15},{10,... | collective-permute-start | bytes 196616 | tf_op jit(solution)/shard_map/ppermute | solution.py:398
  87.2 6.8 %collective-permute-start.21 = (bf16[16,2048]{1,0:T(8,128)(2,1)S(1)}, bf16[16,2048]{1,0:T(8,128)(2,1)S(1)}, u32[]{:S(2)}, u32[]{:S(2)}) collective-permute-start(bf16[16,2048]{1,0:T(8,128)(2,1)S(1)} %get-tuple-element.92), channel_id=1, source_target_pairs={{0,7},{1,6},{2,5},{3,4},{4,3},{5,2},{6,1},{7,0},{8,15},{9,14},{10,... | collective-permute-start | bytes 196616 | tf_op jit(solution)/shard_map/ppermute | solution.py:398
  87.9 6.1 %copy-start.11 = (s32[2]{0:T(128)}, s32[2]{0:T(128)S(1)}, u32[]{:S(2)}) copy-start(s32[2]{0:T(128)S(1)} %pad_add_fusion.1.here_ref) | copy-start | bytes 28
  100.5 0.6 copy-start.7
  101.1 6.3 %collective-permute-start.22 = (bf16[256,256]{1,0:T(8,128)(2,1)S(1)}, bf16[256,256]{1,0:T(8,128)(2,1)S(1)}, u32[]{:S(2)}, u32[]{:S(2)}) collective-permute-start(bf16[256,256]{1,0:T(8,128)(2,1)S(1)} %get-tuple-element.94), channel_id=1, source_target_pairs={{0,8},{8,0},{16,24},{24,16},{1,9},{9,1},{17,25},{25,17},{2,10},{10... | collective-permute-start | bytes 393224 | tf_op jit(solution)/shard_map/ppermute | solution.py:398
  102.6 9.0 %collective-permute-start.23 = (bf16[256,256]{1,0:T(8,128)(2,1)S(1)}, bf16[256,256]{1,0:T(8,128)(2,1)S(1)}, u32[]{:S(2)}, u32[]{:S(2)}) collective-permute-start(bf16[256,256]{1,0:T(8,128)(2,1)S(1)} %get-tuple-element.95), channel_id=1, source_target_pairs={{0,16},{8,24},{16,0},{24,8},{1,17},{9,25},{17,1},{25,9},{2,18},{10... | collective-permute-start | bytes 393224 | tf_op jit(solution)/shard_map/ppermute | solution.py:398
  103.2 8.4 %collective-permute-start.24 = (bf16[256,256]{1,0:T(8,128)(2,1)S(1)}, bf16[256,256]{1,0:T(8,128)(2,1)S(1)}, u32[]{:S(2)}, u32[]{:S(2)}) collective-permute-start(bf16[256,256]{1,0:T(8,128)(2,1)S(1)} %get-tuple-element.96), channel_id=1, source_target_pairs={{0,24},{8,16},{16,8},{24,0},{1,25},{9,17},{17,9},{25,1},{2,26},{10... | collective-permute-start | bytes 393224 | tf_op jit(solution)/shard_map/ppermute | solution.py:398
  107.4 4.2 %copy-start.12 = (bf16[256,256]{1,0:T(8,128)(2,1)}, bf16[256,256]{1,0:T(8,128)(2,1)S(1)}, u32[]{:S(2)}) copy-start(bf16[256,256]{1,0:T(8,128)(2,1)S(1)} %collective-permute-done.22.refs_1_) | copy-start | bytes 393220
  111.6 0.7 copy-start.13
  111.6 0.7 copy-start.14

commit v4 on v3

--- a/solution.py
+++ b/solution.py
@@ -84,15 +84,14 @@
         for folded, table_ref in ((sum_s, fours_ref), (diff_s, twos_ref), (odd_s, odd_ref))
     ]
     for i in range(count):
-        bands = []
-        for coef in coefs:
-            coef = coef[i * tall : (i + 1) * tall]
-            middle = coef.shape[1] // 2
-            bands.append(
-                product(time_ref[0, 0, 0], coef[:, :middle])
-                + product(time_ref[0, 0, 1], coef[:, middle:])
-            )
-        band = jnp.concatenate(bands, axis=1).astype(jnp.bfloat16)
+        at = slice(i * tall, (i + 1) * tall)
+        cosines = [coef[at, : coef.shape[1] // 2] for coef in coefs]
+        sines = [coef[at, coef.shape[1] // 2 :] for coef in coefs]
+        stacked = jnp.concatenate(
+            [jnp.concatenate(cosines, axis=1), jnp.concatenate(sines, axis=1)], axis=0
+        )
+        both = jnp.concatenate([time_ref[0, 0, 0], time_ref[0, 0, 1]], axis=1)
+        band = product(both, stacked).astype(jnp.bfloat16)
         placed = lax.dot_general(
             place_ref[...], band, (((1,), (1,)), ((), ())), preferred_element_type=jnp.float32
         ).astype(jnp.bfloat16)

time: 116 us -> 113 us (0.974)
  Pallas kernels: 59.4 us -> 57.2 us
    pallas_call x2, Pallas kernels: 31.7 us -> 29.5 us  [transform_chunk(): pl.pallas_call(transform_kernel, grid_spec=pltpu.PrefetchScalarGridSpec(n...]
  transfers between devices with their start and end apart: 25 -> 25, of which waited for: 4 -> 4; matrix products, arithmetic and copies ran while one was open for 0% -> 0% of each run, Pallas kernels for 30% -> 29%
where the time goes in v4:
time: 113 us
  Pallas kernels  57.2 us (51%)
  starting transfers between devices  35.3 us (31%)
  waiting for transfers between devices  9.82 us (9%)
  local copies, waits for them, and re-layouts  8.45 us (7%)
  other arithmetic  1.78 us (2%)
    ppermute x25, starting transfers between devices, swap_with(): return lax.ppermute(x, axis, [(i, i ^ offset) for i in range(count)])  35.3 us
    pallas_call x2, Pallas kernels, transform_chunk(): pl.pallas_call(transform_kernel, grid_spec=pltpu.PrefetchScalarGridSpec(n...  29.5 us
    pallas_call x2, Pallas kernels, contract_chunk(): pl.pallas_call(partial(contract_kernel, halves, last, bool(acc), len(z),...  12.5 us
    pallas_call x2, Pallas kernels, polynomials(): pl.pallas_call(partial(polynomial_kernel, half, begin), grid=((L - begin)...  10.5 us
    ppermute x25, waiting for transfers between devices, swap_with(): return lax.ppermute(x, axis, [(i, i ^ offset) for i in range(count)])  9.82 us
    unnamed x31, local copies, waits for them, and re-layouts  7.12 us
    pallas_call x1, Pallas kernels, arrange(): pl.pallas_call(partial(arrange_kernel, owned), grid_spec=pltpu.PrefetchSc...  2.84 us
  transfers between devices with their start and end apart: 25, of which 4 were waited for; matrix products, arithmetic and copies ran while one was open for 0% of the time, Pallas kernels for 29%

profile of v4, /device:TPU:0, one launch (start us, length us, event | category | flops | bytes accessed | tf_op | source)
XLA Modules:
  0.0 112.9 jit_solution(1251540276475712960)
XLA Ops:
  0.0 0.8 reshape.207
  0.8 1.2 %fusion.9 = (s32[8,4,8]{2,1,0:T(4,128)S(1)}, s32[8,4,8]{2,1,0:T(4,128)S(1)}) fusion(s32[8,4,8,2]{3,2,1,0:T(8,128)S(1)} %reshape.207), kind=kLoop, calls=%fused_computation.42 | loop fusion | flops 512 | bytes 4096 | tf_op jit(solution)/shard_map/reduce_max | solution.py:515
  2.2 0.1 concatenate.39
  2.4 0.1 concatenate.38
  2.6 0.2 fusion.place_ref
  2.8 1.6 %copy-done = bf16[2048,512]{1,0:T(8,128)(2,1)S(1)} copy-done((bf16[2048,512]{1,0:T(8,128)(2,1)S(1)}, bf16[2048,512]{1,0:T(8,128)(2,1)}, u32[]{:S(2)}) %copy-start) | copy-done | bytes 2097176
  4.4 1.0 copy-done.1
  5.4 1.0 copy-done.2
  6.5 14.8 %longitude_time.2 = (bf16[128,2048]{1,0:T(8,128)(2,1)}, bf16[128,2048]{1,0:T(8,128)(2,1)}, bf16[128,2048]{1,0:T(8,128)(2,1)}, bf16[128,2048]{1,0:T(8,128)(2,1)}) custom-call(s32[2]{0:T(128)S(1)} %pad_add_fusion.2.where_ref, bf16[16,256,4096]{2,1,0:T(8,128)(2,1)} %frames_ref.3, bf16[1024,256]{1,0:T(8,128)(2,1)S(1)} %copy-done.2, ...), custom_call_target="tpu_custom_call" | custom-call | flops 1000000 | bytes 100000 | tf_op jit(solution)/shard_map/longitude_time/pallas_call | solution.py:122
  21.3 2.9 %collective-permute-start.2 = (bf16[128,2048]{1,0:T(8,128)(2,1)}, bf16[128,2048]{1,0:T(8,128)(2,1)S(1)}, u32[]{:S(2)}, u32[]{:S(2)}) collective-permute-start(bf16[128,2048]{1,0:T(8,128)(2,1)} %get-tuple-element.57), channel_id=1, source_target_pairs={{0,8},{8,0},{16,24},{24,16},{1,9},{9,1},{17,25},{25,17},{2,10},{10... | collective-permute-start | bytes 1572872 | tf_op jit(solution)/shard_map/ppermute | solution.py:397
  24.2 1.5 %collective-permute-start.3 = (bf16[128,2048]{1,0:T(8,128)(2,1)}, bf16[128,2048]{1,0:T(8,128)(2,1)S(1)}, u32[]{:S(2)}, u32[]{:S(2)}) collective-permute-start(bf16[128,2048]{1,0:T(8,128)(2,1)} %get-tuple-element.59), channel_id=1, source_target_pairs={{0,16},{8,24},{16,0},{24,8},{1,17},{9,25},{17,1},{25,9},{2,18},{10... | collective-permute-start | bytes 1572872 | tf_op jit(solution)/shard_map/ppermute | solution.py:397
  25.7 14.7 %longitude_time.3 = (bf16[128,2048]{1,0:T(8,128)(2,1)}, bf16[128,2048]{1,0:T(8,128)(2,1)}, bf16[128,2048]{1,0:T(8,128)(2,1)}, bf16[128,2048]{1,0:T(8,128)(2,1)}) custom-call(s32[2]{0:T(128)S(1)} %pad_add_fusion.2.where_ref, bf16[16,256,4096]{2,1,0:T(8,128)(2,1)} %frames_ref.3, bf16[1024,256]{1,0:T(8,128)(2,1)S(1)} %copy-done.2, ...), custom_call_target="tpu_custom_call" | custom-call | flops 1000000 | bytes 100000 | tf_op jit(solution)/shard_map/longitude_time/pallas_call | solution.py:122
  40.5 0.5 collective-permute-start
  41.1 0.1 dynamic-slice_reduce_fusion
  41.2 0.2 sum_step.2
  41.5 2.0 %collective-permute-start.7 = (bf16[64,2048]{1,0:T(8,128)(2,1)S(1)}, bf16[64,2048]{1,0:T(8,128)(2,1)S(1)}, u32[]{:S(2)}, u32[]{:S(2)}) collective-permute-start(bf16[64,2048]{1,0:T(8,128)(2,1)S(1)} %get-tuple-element.72), channel_id=1, source_target_pairs={{0,8},{8,0},{16,24},{24,16},{1,9},{9,1},{17,25},{25,17},{2,10},{10... | collective-permute-start | bytes 786440 | tf_op jit(solution)/shard_map/ppermute | solution.py:397
  43.5 1.5 %collective-permute-start.6 = (bf16[64,2048]{1,0:T(8,128)(2,1)S(1)}, bf16[64,2048]{1,0:T(8,128)(2,1)S(1)}, u32[]{:S(2)}, u32[]{:S(2)}) collective-permute-start(bf16[64,2048]{1,0:T(8,128)(2,1)S(1)} %get-tuple-element.60), channel_id=1, source_target_pairs={{0,16},{8,24},{16,0},{24,8},{1,17},{9,25},{17,1},{25,9},{2,18},{10... | collective-permute-start | bytes 786440 | tf_op jit(solution)/shard_map/ppermute | solution.py:397
  45.1 3.6 %legendre.3 = (bf16[6144,512]{1,0:T(8,128)(2,1)S(1)}, f32[8,128]{1,0:T(8,128)S(1)}) custom-call(f32[8,128]{1,0:T(8,128)S(1)} %broadcast_in_dim.7.orders_ref, f32[1,512]{1,0:T(1,128)S(1)} %copy-done.10, f32[3,512]{1,0:T(4,128)S(1)} %copy-done.9), custom_call_target="tpu_custom_call" | custom-call | flops 1000000 | bytes 100000 | tf_op jit(solution)/shard_map/legendre/pallas_call | solution.py:229
  48.8 6.9 %legendre.2 = (bf16[8192,1024]{1,0:T(8,128)(2,1)S(1)}, f32[8,128]{1,0:T(8,128)S(1)}) custom-call(f32[8,128]{1,0:T(8,128)S(1)} %broadcast_in_dim.6.orders_ref, f32[1,512]{1,0:T(1,128)S(1)} %copy-done.10, f32[3,1024]{1,0:T(4,128)S(1)} %copy-done.8), custom_call_target="tpu_custom_call" | custom-call | flops 1000000 | bytes 100000 | tf_op jit(solution)/shard_map/legendre/pallas_call | solution.py:229
  55.7 0.5 collective-permute-done.1.got_b
  56.2 1.0 copy-done.3
  57.2 1.0 copy-done.4
  58.3 1.4 %sum_step.3 = (f32[64,2048]{1,0:T(8,128)S(1)}, bf16[64,2048]{1,0:T(8,128)(2,1)S(1)}, f32[64,2048]{1,0:T(8,128)S(1)}, bf16[64,2048]{1,0:T(8,128)(2,1)S(1)}) custom-call(bf16[128,2048]{1,0:T(8,128)(2,1)S(1)} %copy-done.3, bf16[128,2048]{1,0:T(8,128)(2,1)} %collective-permute-done.got_a, bf16[128,2048]{1,0:T(8,128)(2,1)S(1)} %copy-done.4, ...), custom_call_target="tpu_custom_call" | custom-call | flops 1000000 | bytes 100000 | tf_op jit(solution)/shard_map/sum_step/pallas_call | solution.py:430
  59.7 0.1 collective-permute-start.4
  59.8 1.9 %collective-permute-start.5 = (bf16[64,2048]{1,0:T(8,128)(2,1)S(1)}, bf16[64,2048]{1,0:T(8,128)(2,1)S(1)}, u32[]{:S(2)}, u32[]{:S(2)}) collective-permute-start(bf16[64,2048]{1,0:T(8,128)(2,1)S(1)} %get-tuple-element.68), channel_id=1, source_target_pairs={{0,8},{8,0},{16,24},{24,16},{1,9},{9,1},{17,25},{25,17},{2,10},{10... | collective-permute-start | bytes 786440 | tf_op jit(solution)/shard_map/ppermute | solution.py:397
  61.8 0.1 sum_end.3
  62.0 1.6 %collective-permute-start.9 = (bf16[16,2048]{1,0:T(8,128)(2,1)S(1)}, bf16[16,2048]{1,0:T(8,128)(2,1)S(1)}, u32[]{:S(2)}, u32[]{:S(2)}) collective-permute-start(bf16[16,2048]{1,0:T(8,128)(2,1)S(1)} %get-tuple-element.75), channel_id=1, source_target_pairs={{0,2},{1,3},{2,0},{3,1},{4,6},{5,7},{6,4},{7,5},{8,10},{9,11},{10,... | collective-permute-start | bytes 196616 | tf_op jit(solution)/shard_map/ppermute | solution.py:397
  63.6 0.2 collective-permute-start.10
  63.8 2.3 %collective-permute-done.4.got_a = bf16[64,2048]{1,0:T(8,128)(2,1)S(1)} collective-permute-done((bf16[64,2048]{1,0:T(8,128)(2,1)S(1)}, bf16[64,2048]{1,0:T(8,128)(2,1)S(1)}, u32[]{:S(2)}, u32[]{:S(2)}) %collective-permute-start.4) | collective-permute-done | bytes 262176 | tf_op jit(solution)/shard_map/ppermute | solution.py:397
  66.2 2.6 %collective-permute-start.11 = (bf16[16,2048]{1,0:T(8,128)(2,1)S(1)}, bf16[16,2048]{1,0:T(8,128)(2,1)S(1)}, u32[]{:S(2)}, u32[]{:S(2)}) collective-permute-start(bf16[16,2048]{1,0:T(8,128)(2,1)S(1)} %get-tuple-element.77), channel_id=1, source_target_pairs={{0,4},{1,5},{2,6},{3,7},{4,0},{5,1},{6,2},{7,3},{8,12},{9,13},{10,... | collective-permute-start | bytes 196616 | tf_op jit(solution)/shard_map/ppermute | solution.py:397
  68.9 1.6 %collective-permute-start.13 = (bf16[16,2048]{1,0:T(8,128)(2,1)S(1)}, bf16[16,2048]{1,0:T(8,128)(2,1)S(1)}, u32[]{:S(2)}, u32[]{:S(2)}) collective-permute-start(bf16[16,2048]{1,0:T(8,128)(2,1)S(1)} %get-tuple-element.79), channel_id=1, source_target_pairs={{0,6},{1,7},{2,4},{3,5},{4,2},{5,3},{6,0},{7,1},{8,14},{9,15},{10,... | collective-permute-start | bytes 196616 | tf_op jit(solution)/shard_map/ppermute | solution.py:397
  70.4 2.3 %collective-permute-start.14 = (bf16[16,2048]{1,0:T(8,128)(2,1)S(1)}, bf16[16,2048]{1,0:T(8,128)(2,1)S(1)}, u32[]{:S(2)}, u32[]{:S(2)}) collective-permute-start(bf16[16,2048]{1,0:T(8,128)(2,1)S(1)} %get-tuple-element.80), channel_id=1, source_target_pairs={{0,7},{1,6},{2,5},{3,4},{4,3},{5,2},{6,1},{7,0},{8,15},{9,14},{10,... | collective-permute-start | bytes 196616 | tf_op jit(solution)/shard_map/ppermute | solution.py:397
  72.7 0.2 collective-permute-start.15
  72.9 4.7 %collective-permute-start.16 = (bf16[16,2048]{1,0:T(8,128)(2,1)S(1)}, bf16[16,2048]{1,0:T(8,128)(2,1)S(1)}, u32[]{:S(2)}, u32[]{:S(2)}) collective-permute-start(bf16[16,2048]{1,0:T(8,128)(2,1)S(1)} %get-tuple-element.87), channel_id=1, source_target_pairs={{0,2},{1,3},{2,0},{3,1},{4,6},{5,7},{6,4},{7,5},{8,10},{9,11},{10,... | collective-permute-start | bytes 196616 | tf_op jit(solution)/shard_map/ppermute | solution.py:397
  77.7 4.6 %collective-permute-start.18 = (bf16[16,2048]{1,0:T(8,128)(2,1)S(1)}, bf16[16,2048]{1,0:T(8,128)(2,1)S(1)}, u32[]{:S(2)}, u32[]{:S(2)}) collective-permute-start(bf16[16,2048]{1,0:T(8,128)(2,1)S(1)} %get-tuple-element.89), channel_id=1, source_target_pairs={{0,4},{1,5},{2,6},{3,7},{4,0},{5,1},{6,2},{7,3},{8,12},{9,13},{10,... | collective-permute-start | bytes 196616 | tf_op jit(solution)/shard_map/ppermute | solution.py:397
  82.3 0.4 collective-permute-start.19
  82.7 2.2 %collective-permute-start.20 = (bf16[16,2048]{1,0:T(8,128)(2,1)S(1)}, bf16[16,2048]{1,0:T(8,128)(2,1)S(1)}, u32[]{:S(2)}, u32[]{:S(2)}) collective-permute-start(bf16[16,2048]{1,0:T(8,128)(2,1)S(1)} %get-tuple-element.91), channel_id=1, source_target_pairs={{0,6},{1,7},{2,4},{3,5},{4,2},{5,3},{6,0},{7,1},{8,14},{9,15},{10,... | collective-permute-start | bytes 196616 | tf_op jit(solution)/shard_map/ppermute | solution.py:397
  85.0 0.6 collective-permute-start.21
  85.7 6.0 %latitude_sum.2 = (f32[1024,128]{1,0:T(8,128)S(1)}, f32[768,128]{1,0:T(8,128)S(1)}) custom-call(s32[2]{0:T(128)S(1)} %pad_add_fusion.1.here_ref, bf16[16,2048]{1,0:T(8,128)(2,1)S(1)} %get-tuple-element.73.refs_0_, bf16[16,2048]{1,0:T(8,128)(2,1)S(1)} %collective-permute-done.8.refs_1_, bf16[16,2048]{1,0:T(8,128)(2,1)S(1)} %collective-permute-done.9.refs_2_, ...), custom_call_target="tpu_custom_call" | custom-call | flops 1000000 | bytes 100000 | tf_op jit(solution)/shard_map/latitude_sum/pallas_call | solution.py:342
  91.8 6.5 %latitude_sum.3 = (bf16[256,256]{1,0:T(8,128)(2,1)S(1)}, bf16[256,256]{1,0:T(8,128)(2,1)S(1)}, bf16[256,256]{1,0:T(8,128)(2,1)S(1)}, bf16[256,256]{1,0:T(8,128)(2,1)S(1)}) custom-call(s32[2]{0:T(128)S(1)} %pad_add_fusion.1.here_ref, bf16[16,2048]{1,0:T(8,128)(2,1)S(1)} %get-tuple-element.85.refs_0_, bf16[16,2048]{1,0:T(8,128)(2,1)S(1)} %collective-permute-done.15.refs_1_, ...), custom_call_target="tpu_custom_call" | custom-call | flops 1000000 | bytes 100000 | tf_op jit(solution)/shard_map/latitude_sum/pallas_call | solution.py:342
  98.3 0.6 copy-done.7
  98.9 1.4 %collective-permute-start.22 = (bf16[256,256]{1,0:T(8,128)(2,1)S(1)}, bf16[256,256]{1,0:T(8,128)(2,1)S(1)}, u32[]{:S(2)}, u32[]{:S(2)}) collective-permute-start(bf16[256,256]{1,0:T(8,128)(2,1)S(1)} %get-tuple-element.94), channel_id=1, source_target_pairs={{0,8},{8,0},{16,24},{24,16},{1,9},{9,1},{17,25},{25,17},{2,10},{10... | collective-permute-start | bytes 393224 | tf_op jit(solution)/shard_map/ppermute | solution.py:397
  100.4 0.7 collective-permute-start.23
  101.0 1.4 %collective-permute-start.24 = (bf16[256,256]{1,0:T(8,128)(2,1)S(1)}, bf16[256,256]{1,0:T(8,128)(2,1)S(1)}, u32[]{:S(2)}, u32[]{:S(2)}) collective-permute-start(bf16[256,256]{1,0:T(8,128)(2,1)S(1)} %get-tuple-element.96), channel_id=1, source_target_pairs={{0,24},{8,16},{16,8},{24,0},{1,25},{9,17},{17,9},{25,1},{2,26},{10... | collective-permute-start | bytes 393224 | tf_op jit(solution)/shard_map/ppermute | solution.py:397
  102.4 2.8 %collective-permute-done.22.refs_1_ = bf16[256,256]{1,0:T(8,128)(2,1)S(1)} collective-permute-done((bf16[256,256]{1,0:T(8,128)(2,1)S(1)}, bf16[256,256]{1,0:T(8,128)(2,1)S(1)}, u32[]{:S(2)}, u32[]{:S(2)}) %collective-permute-start.22) | collective-permute-done | bytes 131104 | tf_op jit(solution)/shard_map/ppermute | solution.py:397
  105.2 4.2 %collective-permute-done.23.refs_2_ = bf16[256,256]{1,0:T(8,128)(2,1)S(1)} collective-permute-done((bf16[256,256]{1,0:T(8,128)(2,1)S(1)}, bf16[256,256]{1,0:T(8,128)(2,1)S(1)}, u32[]{:S(2)}, u32[]{:S(2)}) %collective-permute-start.23) | collective-permute-done | bytes 131104 | tf_op jit(solution)/shard_map/ppermute | solution.py:397
  109.4 0.6 copy-done.13
  110.1 2.8 %slot_order.1 = f32[2,64,8,256]{3,2,1,0:T(8,128)} custom-call(s32[2]{0:T(128)} %copy-done.11, s32[512]{0:T(512)} %orders_ref.1, bf16[256,256]{1,0:T(8,128)(2,1)} %copy-done.7, bf16[256,256]{1,0:T(8,128)(2,1)} %copy-done.12, bf16[256,256]{1,0:T(8,128)(2,1)} %copy-done.13, bf16[256,256]{1,0:T(8,128)(2,1)} %copy-done.14), custom_call_target="tpu_custom_call" | custom-call | tf_op jit(solution)/shard_map/slot_order/pallas_call | solution.py:382
  (75 shorter events, 1.0 us)
Async XLA Ops:
  2.8 1.6 %copy-start = (bf16[2048,512]{1,0:T(8,128)(2,1)S(1)}, bf16[2048,512]{1,0:T(8,128)(2,1)}, u32[]{:S(2)}) copy-start(bf16[2048,512]{1,0:T(8,128)(2,1)} %constant.89.clone.odd_ref) | copy-start | bytes 6291460
  4.4 1.0 copy-start.1
  5.4 1.0 copy-start.2
  21.3 19.9 %collective-permute-start.2 = (bf16[128,2048]{1,0:T(8,128)(2,1)}, bf16[128,2048]{1,0:T(8,128)(2,1)S(1)}, u32[]{:S(2)}, u32[]{:S(2)}) collective-permute-start(bf16[128,2048]{1,0:T(8,128)(2,1)} %get-tuple-element.57), channel_id=1, source_target_pairs={{0,8},{8,0},{16,24},{24,16},{1,9},{9,1},{17,25},{25,17},{2,10},{10... | collective-permute-start | bytes 1572872 | tf_op jit(solution)/shard_map/ppermute | solution.py:397
  24.2 17.0 %collective-permute-start.3 = (bf16[128,2048]{1,0:T(8,128)(2,1)}, bf16[128,2048]{1,0:T(8,128)(2,1)S(1)}, u32[]{:S(2)}, u32[]{:S(2)}) collective-permute-start(bf16[128,2048]{1,0:T(8,128)(2,1)} %get-tuple-element.59), channel_id=1, source_target_pairs={{0,16},{8,24},{16,0},{24,8},{1,17},{9,25},{17,1},{25,9},{2,18},{10... | collective-permute-start | bytes 1572872 | tf_op jit(solution)/shard_map/ppermute | solution.py:397
  25.7 15.5 %copy-start.5 = (bf16[128,2048]{1,0:T(8,128)(2,1)S(1)}, bf16[128,2048]{1,0:T(8,128)(2,1)}, u32[]{:S(2)}) copy-start(bf16[128,2048]{1,0:T(8,128)(2,1)} %get-tuple-element.51.keep_a) | copy-start | bytes 1572868
  25.7 15.5 %copy-start.6 = (bf16[128,2048]{1,0:T(8,128)(2,1)S(1)}, bf16[128,2048]{1,0:T(8,128)(2,1)}, u32[]{:S(2)}) copy-start(bf16[128,2048]{1,0:T(8,128)(2,1)} %get-tuple-element.58.keep_b) | copy-start | bytes 1572868
  25.7 19.4 %copy-start.9 = (f32[3,512]{1,0:T(4,128)S(1)}, f32[3,512]{1,0:T(4,128)}, u32[]{:S(2)}) copy-start(f32[3,512]{1,0:T(4,128)} %constant.93.clone.rows_ref) | copy-start | bytes 18436
  25.7 19.4 %copy-start.10 = (f32[1,512]{1,0:T(1,128)S(1)}, f32[1,512]{1,0:T(1,128)}, u32[]{:S(2)}) copy-start(f32[1,512]{1,0:T(1,128)} %constant.91.clone.growth_ref) | copy-start | bytes 6148
  25.7 23.1 %copy-start.8 = (f32[3,1024]{1,0:T(4,128)S(1)}, f32[3,1024]{1,0:T(4,128)}, u32[]{:S(2)}) copy-start(f32[3,1024]{1,0:T(4,128)} %constant.92.clone.rows_ref) | copy-start | bytes 36868
  40.5 15.2 %collective-permute-start = (bf16[128,2048]{1,0:T(8,128)(2,1)}, bf16[128,2048]{1,0:T(8,128)(2,1)}, u32[]{:S(2)}, u32[]{:S(2)}) collective-permute-start(bf16[128,2048]{1,0:T(8,128)(2,1)} %get-tuple-element.54), channel_id=1, source_target_pairs={{0,8},{8,0},{16,24},{24,16},{1,9},{9,1},{17,25},{25,17},{2,10},{10... | collective-permute-start | bytes 1572872 | tf_op jit(solution)/shard_map/ppermute | solution.py:397
  41.0 15.2 %collective-permute-start.1 = (bf16[128,2048]{1,0:T(8,128)(2,1)}, bf16[128,2048]{1,0:T(8,128)(2,1)}, u32[]{:S(2)}, u32[]{:S(2)}) collective-permute-start(bf16[128,2048]{1,0:T(8,128)(2,1)} %get-tuple-element.56), channel_id=1, source_target_pairs={{0,16},{8,24},{16,0},{24,8},{1,17},{9,25},{17,1},{25,9},{2,18},{10... | collective-permute-start | bytes 1572872 | tf_op jit(solution)/shard_map/ppermute | solution.py:397
  41.5 20.3 %collective-permute-start.7 = (bf16[64,2048]{1,0:T(8,128)(2,1)S(1)}, bf16[64,2048]{1,0:T(8,128)(2,1)S(1)}, u32[]{:S(2)}, u32[]{:S(2)}) collective-permute-start(bf16[64,2048]{1,0:T(8,128)(2,1)S(1)} %get-tuple-element.72), channel_id=1, source_target_pairs={{0,8},{8,0},{16,24},{24,16},{1,9},{9,1},{17,25},{25,17},{2,10},{10... | collective-permute-start | bytes 786440 | tf_op jit(solution)/shard_map/ppermute | solution.py:397
  43.5 18.3 %collective-permute-start.6 = (bf16[64,2048]{1,0:T(8,128)(2,1)S(1)}, bf16[64,2048]{1,0:T(8,128)(2,1)S(1)}, u32[]{:S(2)}, u32[]{:S(2)}) collective-permute-start(bf16[64,2048]{1,0:T(8,128)(2,1)S(1)} %get-tuple-element.60), channel_id=1, source_target_pairs={{0,16},{8,24},{16,0},{24,8},{1,17},{9,25},{17,1},{25,9},{2,18},{10... | collective-permute-start | bytes 786440 | tf_op jit(solution)/shard_map/ppermute | solution.py:397
  56.2 1.0 copy-start.3
  57.2 1.0 copy-start.4
  59.7 6.4 %collective-permute-start.4 = (bf16[64,2048]{1,0:T(8,128)(2,1)S(1)}, bf16[64,2048]{1,0:T(8,128)(2,1)S(1)}, u32[]{:S(2)}, u32[]{:S(2)}) collective-permute-start(bf16[64,2048]{1,0:T(8,128)(2,1)S(1)} %get-tuple-element.66), channel_id=1, source_target_pairs={{0,16},{8,24},{16,0},{24,8},{1,17},{9,25},{17,1},{25,9},{2,18},{10... | collective-permute-start | bytes 786440 | tf_op jit(solution)/shard_map/ppermute | solution.py:397
  59.8 8.9 %collective-permute-start.5 = (bf16[64,2048]{1,0:T(8,128)(2,1)S(1)}, bf16[64,2048]{1,0:T(8,128)(2,1)S(1)}, u32[]{:S(2)}, u32[]{:S(2)}) collective-permute-start(bf16[64,2048]{1,0:T(8,128)(2,1)S(1)} %get-tuple-element.68), channel_id=1, source_target_pairs={{0,8},{8,0},{16,24},{24,16},{1,9},{9,1},{17,25},{25,17},{2,10},{10... | collective-permute-start | bytes 786440 | tf_op jit(solution)/shard_map/ppermute | solution.py:397
  61.9 7.0 %collective-permute-start.8 = (bf16[16,2048]{1,0:T(8,128)(2,1)S(1)}, bf16[16,2048]{1,0:T(8,128)(2,1)S(1)}, u32[]{:S(2)}, u32[]{:S(2)}) collective-permute-start(bf16[16,2048]{1,0:T(8,128)(2,1)S(1)} %get-tuple-element.74), channel_id=1, source_target_pairs={{0,1},{1,0},{2,3},{3,2},{4,5},{5,4},{6,7},{7,6},{8,9},{9,8},{10,11... | collective-permute-start | bytes 196616 | tf_op jit(solution)/shard_map/ppermute | solution.py:397
  62.0 8.5 %collective-permute-start.9 = (bf16[16,2048]{1,0:T(8,128)(2,1)S(1)}, bf16[16,2048]{1,0:T(8,128)(2,1)S(1)}, u32[]{:S(2)}, u32[]{:S(2)}) collective-permute-start(bf16[16,2048]{1,0:T(8,128)(2,1)S(1)} %get-tuple-element.75), channel_id=1, source_target_pairs={{0,2},{1,3},{2,0},{3,1},{4,6},{5,7},{6,4},{7,5},{8,10},{9,11},{10,... | collective-permute-start | bytes 196616 | tf_op jit(solution)/shard_map/ppermute | solution.py:397
  63.6 9.1 %collective-permute-start.10 = (bf16[16,2048]{1,0:T(8,128)(2,1)S(1)}, bf16[16,2048]{1,0:T(8,128)(2,1)S(1)}, u32[]{:S(2)}, u32[]{:S(2)}) collective-permute-start(bf16[16,2048]{1,0:T(8,128)(2,1)S(1)} %get-tuple-element.76), channel_id=1, source_target_pairs={{0,3},{1,2},{2,1},{3,0},{4,7},{5,6},{6,5},{7,4},{8,11},{9,10},{10,... | collective-permute-start | bytes 196616 | tf_op jit(solution)/shard_map/ppermute | solution.py:397
  66.2 6.7 %collective-permute-start.11 = (bf16[16,2048]{1,0:T(8,128)(2,1)S(1)}, bf16[16,2048]{1,0:T(8,128)(2,1)S(1)}, u32[]{:S(2)}, u32[]{:S(2)}) collective-permute-start(bf16[16,2048]{1,0:T(8,128)(2,1)S(1)} %get-tuple-element.77), channel_id=1, source_target_pairs={{0,4},{1,5},{2,6},{3,7},{4,0},{5,1},{6,2},{7,3},{8,12},{9,13},{10,... | collective-permute-start | bytes 196616 | tf_op jit(solution)/shard_map/ppermute | solution.py:397
  68.7 8.8 %collective-permute-start.12 = (bf16[16,2048]{1,0:T(8,128)(2,1)S(1)}, bf16[16,2048]{1,0:T(8,128)(2,1)S(1)}, u32[]{:S(2)}, u32[]{:S(2)}) collective-permute-start(bf16[16,2048]{1,0:T(8,128)(2,1)S(1)} %get-tuple-element.78), channel_id=1, source_target_pairs={{0,5},{1,4},{2,7},{3,6},{4,1},{5,0},{6,3},{7,2},{8,13},{9,12},{10,... | collective-permute-start | bytes 196616 | tf_op jit(solution)/shard_map/ppermute | solution.py:397
  68.9 8.8 %collective-permute-start.13 = (bf16[16,2048]{1,0:T(8,128)(2,1)S(1)}, bf16[16,2048]{1,0:T(8,128)(2,1)S(1)}, u32[]{:S(2)}, u32[]{:S(2)}) collective-permute-start(bf16[16,2048]{1,0:T(8,128)(2,1)S(1)} %get-tuple-element.79), channel_id=1, source_target_pairs={{0,6},{1,7},{2,4},{3,5},{4,2},{5,3},{6,0},{7,1},{8,14},{9,15},{10,... | collective-permute-start | bytes 196616 | tf_op jit(solution)/shard_map/ppermute | solution.py:397
  70.4 11.8 %collective-permute-start.14 = (bf16[16,2048]{1,0:T(8,128)(2,1)S(1)}, bf16[16,2048]{1,0:T(8,128)(2,1)S(1)}, u32[]{:S(2)}, u32[]{:S(2)}) collective-permute-start(bf16[16,2048]{1,0:T(8,128)(2,1)S(1)} %get-tuple-element.80), channel_id=1, source_target_pairs={{0,7},{1,6},{2,5},{3,4},{4,3},{5,2},{6,1},{7,0},{8,15},{9,14},{10,... | collective-permute-start | bytes 196616 | tf_op jit(solution)/shard_map/ppermute | solution.py:397
  72.7 10.0 %collective-permute-start.15 = (bf16[16,2048]{1,0:T(8,128)(2,1)S(1)}, bf16[16,2048]{1,0:T(8,128)(2,1)S(1)}, u32[]{:S(2)}, u32[]{:S(2)}) collective-permute-start(bf16[16,2048]{1,0:T(8,128)(2,1)S(1)} %get-tuple-element.86), channel_id=1, source_target_pairs={{0,1},{1,0},{2,3},{3,2},{4,5},{5,4},{6,7},{7,6},{8,9},{9,8},{10,11... | collective-permute-start | bytes 196616 | tf_op jit(solution)/shard_map/ppermute | solution.py:397
  72.9 12.1 %collective-permute-start.16 = (bf16[16,2048]{1,0:T(8,128)(2,1)S(1)}, bf16[16,2048]{1,0:T(8,128)(2,1)S(1)}, u32[]{:S(2)}, u32[]{:S(2)}) collective-permute-start(bf16[16,2048]{1,0:T(8,128)(2,1)S(1)} %get-tuple-element.87), channel_id=1, source_target_pairs={{0,2},{1,3},{2,0},{3,1},{4,6},{5,7},{6,4},{7,5},{8,10},{9,11},{10,... | collective-permute-start | bytes 196616 | tf_op jit(solution)/shard_map/ppermute | solution.py:397
  77.6 14.2 %collective-permute-start.17 = (bf16[16,2048]{1,0:T(8,128)(2,1)S(1)}, bf16[16,2048]{1,0:T(8,128)(2,1)S(1)}, u32[]{:S(2)}, u32[]{:S(2)}) collective-permute-start(bf16[16,2048]{1,0:T(8,128)(2,1)S(1)} %get-tuple-element.88), channel_id=1, source_target_pairs={{0,3},{1,2},{2,1},{3,0},{4,7},{5,6},{6,5},{7,4},{8,11},{9,10},{10,... | collective-permute-start | bytes 196616 | tf_op jit(solution)/shard_map/ppermute | solution.py:397
  77.7 14.1 %collective-permute-start.18 = (bf16[16,2048]{1,0:T(8,128)(2,1)S(1)}, bf16[16,2048]{1,0:T(8,128)(2,1)S(1)}, u32[]{:S(2)}, u32[]{:S(2)}) collective-permute-start(bf16[16,2048]{1,0:T(8,128)(2,1)S(1)} %get-tuple-element.89), channel_id=1, source_target_pairs={{0,4},{1,5},{2,6},{3,7},{4,0},{5,1},{6,2},{7,3},{8,12},{9,13},{10,... | collective-permute-start | bytes 196616 | tf_op jit(solution)/shard_map/ppermute | solution.py:397
  82.3 9.5 %collective-permute-start.19 = (bf16[16,2048]{1,0:T(8,128)(2,1)S(1)}, bf16[16,2048]{1,0:T(8,128)(2,1)S(1)}, u32[]{:S(2)}, u32[]{:S(2)}) collective-permute-start(bf16[16,2048]{1,0:T(8,128)(2,1)S(1)} %get-tuple-element.90), channel_id=1, source_target_pairs={{0,5},{1,4},{2,7},{3,6},{4,1},{5,0},{6,3},{7,2},{8,13},{9,12},{10,... | collective-permute-start | bytes 196616 | tf_op jit(solution)/shard_map/ppermute | solution.py:397
  82.7 9.0 %collective-permute-start.20 = (bf16[16,2048]{1,0:T(8,128)(2,1)S(1)}, bf16[16,2048]{1,0:T(8,128)(2,1)S(1)}, u32[]{:S(2)}, u32[]{:S(2)}) collective-permute-start(bf16[16,2048]{1,0:T(8,128)(2,1)S(1)} %get-tuple-element.91), channel_id=1, source_target_pairs={{0,6},{1,7},{2,4},{3,5},{4,2},{5,3},{6,0},{7,1},{8,14},{9,15},{10,... | collective-permute-start | bytes 196616 | tf_op jit(solution)/shard_map/ppermute | solution.py:397
  85.0 6.8 %collective-permute-start.21 = (bf16[16,2048]{1,0:T(8,128)(2,1)S(1)}, bf16[16,2048]{1,0:T(8,128)(2,1)S(1)}, u32[]{:S(2)}, u32[]{:S(2)}) collective-permute-start(bf16[16,2048]{1,0:T(8,128)(2,1)S(1)} %get-tuple-element.92), channel_id=1, source_target_pairs={{0,7},{1,6},{2,5},{3,4},{4,3},{5,2},{6,1},{7,0},{8,15},{9,14},{10,... | collective-permute-start | bytes 196616 | tf_op jit(solution)/shard_map/ppermute | solution.py:397
  85.7 6.1 %copy-start.11 = (s32[2]{0:T(128)}, s32[2]{0:T(128)S(1)}, u32[]{:S(2)}) copy-start(s32[2]{0:T(128)S(1)} %pad_add_fusion.1.here_ref) | copy-start | bytes 28
  98.3 0.6 copy-start.7
  98.9 6.3 %collective-permute-start.22 = (bf16[256,256]{1,0:T(8,128)(2,1)S(1)}, bf16[256,256]{1,0:T(8,128)(2,1)S(1)}, u32[]{:S(2)}, u32[]{:S(2)}) collective-permute-start(bf16[256,256]{1,0:T(8,128)(2,1)S(1)} %get-tuple-element.94), channel_id=1, source_target_pairs={{0,8},{8,0},{16,24},{24,16},{1,9},{9,1},{17,25},{25,17},{2,10},{10... | collective-permute-start | bytes 393224 | tf_op jit(solution)/shard_map/ppermute | solution.py:397
  100.4 9.0 %collective-permute-start.23 = (bf16[256,256]{1,0:T(8,128)(2,1)S(1)}, bf16[256,256]{1,0:T(8,128)(2,1)S(1)}, u32[]{:S(2)}, u32[]{:S(2)}) collective-permute-start(bf16[256,256]{1,0:T(8,128)(2,1)S(1)} %get-tuple-element.95), channel_id=1, source_target_pairs={{0,16},{8,24},{16,0},{24,8},{1,17},{9,25},{17,1},{25,9},{2,18},{10... | collective-permute-start | bytes 393224 | tf_op jit(solution)/shard_map/ppermute | solution.py:397
  101.0 8.4 %collective-permute-start.24 = (bf16[256,256]{1,0:T(8,128)(2,1)S(1)}, bf16[256,256]{1,0:T(8,128)(2,1)S(1)}, u32[]{:S(2)}, u32[]{:S(2)}) collective-permute-start(bf16[256,256]{1,0:T(8,128)(2,1)S(1)} %get-tuple-element.96), channel_id=1, source_target_pairs={{0,24},{8,16},{16,8},{24,0},{1,25},{9,17},{17,9},{25,1},{2,26},{10... | collective-permute-start | bytes 393224 | tf_op jit(solution)/shard_map/ppermute | solution.py:397
  105.2 4.2 %copy-start.12 = (bf16[256,256]{1,0:T(8,128)(2,1)}, bf16[256,256]{1,0:T(8,128)(2,1)S(1)}, u32[]{:S(2)}) copy-start(bf16[256,256]{1,0:T(8,128)(2,1)S(1)} %collective-permute-done.22.refs_1_) | copy-start | bytes 393220
  109.4 0.7 copy-start.13
  109.4 0.7 copy-start.14
